TPU v7x, 32 devices: a whole 2x2x4 slice. The times are simulated.
32 devices in a mesh: blk: 16 (over z, y, core), frq: 2 (over x).
Axes of the slice: x: 2, y: 2, z: 4, core: 2. Of those that a mesh axis runs over, the one named last changes fastest.
Arguments:
- spectra: bfloat16 [2, 4096, 4, 2048], P(None, 'blk', None, 'frq'), may hold values from -6 to 6
- channel_valid: int32 [4096], P('blk'), may hold values 0 or 1
Outputs:
- stacked: float32 [16, 4, 201, 256], P('blk', None, None, 'frq')
Inputs may be any that keep to these rules, and one draw needn't show every extreme that they name: `channel_valid`: 1 marks a usable channel.
All inputs are finite; a program needn't handle non-finite values. No bound on the sum of `channel_valid` on one device may be relied on, other than what follows from the above.
Results may differ from a plain program's by a relative error of at most 0.006.
Values may be sent and summed in bfloat16 or wider, within the bound.
No kernel may reach another device: no remote copies, remote signals or barrier semaphores. Data moves between devices by JAX's collectives and lax.ppermute only.
A program may use at most 384 MiB of HBM per device.

v0:
```python
import math

import jax
import jax.numpy as jnp
from jax import lax
from jax.sharding import PartitionSpec as P

LAGS = 201
ROUNDS = 4


def from_behind(value, axis, steps):
    count = lax.axis_size(axis)
    first, last = (max(0, -steps), min(count, count - steps))
    return lax.ppermute(value, axis, [(source, source + steps) for source in range(first, last)])


def matmul_high(left, right):
    return jnp.dot(left, right, precision=lax.Precision.HIGHEST, preferred_element_type=jnp.float32)


def angle_table(first_index, second_index, period):
    product = jnp.mod(first_index[:, None] * second_index[None, :], period)
    return 2.0 * math.pi / period * product.astype(jnp.float32)


def split_table(table):
    upper = table.astype(jnp.bfloat16)
    lower = (table - upper.astype(jnp.float32)).astype(jnp.bfloat16)
    return (upper, lower)


def twiddle_product(pair, data):
    return jnp.dot(pair[0], data, preferred_element_type=jnp.float32) + jnp.dot(
        pair[1], data, preferred_element_type=jnp.float32
    )


def to_wavenumber(spectrum_in, cos_pair, sin_pair):
    channels = spectrum_in.shape[1]
    flattened = spectrum_in.reshape(2, channels, -1)
    real_part = twiddle_product(cos_pair, flattened[0]) + twiddle_product(sin_pair, flattened[1])
    imag_part = twiddle_product(cos_pair, flattened[1]) - twiddle_product(sin_pair, flattened[0])
    return jnp.stack([real_part, imag_part])


def lag_terms(own_hat, far_hat, windows, inv_cos, inv_sin, lag_cos, lag_sin, normalizer):
    length = own_hat.shape[1]
    own_hat = own_hat.reshape(2, length, windows, -1)
    far_hat = far_hat.reshape(2, length, windows, -1)
    cross_real = jnp.sum(own_hat[0] * far_hat[0] + own_hat[1] * far_hat[1], axis=1)
    cross_imag = jnp.sum(own_hat[1] * far_hat[0] - own_hat[0] * far_hat[1], axis=1)
    stack_real = matmul_high(inv_cos, cross_real) - matmul_high(inv_sin, cross_imag)
    stack_imag = matmul_high(inv_sin, cross_real) + matmul_high(inv_cos, cross_imag)
    return normalizer * (matmul_high(lag_cos, stack_real.T) - matmul_high(lag_sin, stack_imag.T))


def on_device(spectra, channel_valid):
    channels = spectra.shape[1]
    windows = spectra.shape[2]
    freq_local = spectra.shape[3]
    spectra_f = spectra.astype(jnp.float32)
    mean_power = jnp.mean(
        spectra_f[0] * spectra_f[0] + spectra_f[1] * spectra_f[1], axis=1, keepdims=True
    )
    whiten_scale = channel_valid.astype(jnp.float32)[:, None, None] / jnp.maximum(
        jnp.sqrt(mean_power), 0.5
    )
    whitened = (spectra_f * whiten_scale[None]).astype(jnp.bfloat16)
    length = 2 * channels
    chan_index = jnp.arange(channels, dtype=jnp.int32)
    wave_index = jnp.arange(length, dtype=jnp.int32)
    fwd_angle = angle_table(wave_index, chan_index, length)
    cos_pair = split_table(jnp.cos(fwd_angle))
    sin_pair = split_table(jnp.sin(fwd_angle))
    inv_angle = angle_table(chan_index - channels // 2, wave_index, length)
    inv_cos, inv_sin = (jnp.cos(inv_angle) / length, jnp.sin(inv_angle) / length)
    freq_total = freq_local * lax.axis_size("frq")
    freq_start = lax.axis_index("frq") * freq_local
    lag_index = jnp.arange(LAGS, dtype=jnp.int32) - (LAGS - 1) // 2
    freq_index = freq_start + jnp.arange(freq_local, dtype=jnp.int32)
    lag_angle = angle_table(lag_index, freq_index, 2 * freq_total)
    lag_cos, lag_sin = (jnp.cos(lag_angle), jnp.sin(lag_angle))
    normalizer = 1.0 / math.sqrt(windows * channels * freq_total)
    own_hat = to_wavenumber(whitened, cos_pair, sin_pair)
    partials = []
    for distance in range(1, ROUNDS + 1):
        far_raw = from_behind(whitened, "blk", distance)
        far_hat = to_wavenumber(far_raw, cos_pair, sin_pair)
        partial_term = lag_terms(
            own_hat, far_hat, windows, inv_cos, inv_sin, lag_cos, lag_sin, normalizer
        )
        partials.append(lax.psum_scatter(partial_term, "frq", scatter_dimension=1, tiled=True))
    stacked = jnp.stack(partials)
    return stacked[None]


def solution(mesh):
    return jax.shard_map(
        on_device,
        mesh=mesh,
        in_specs=(P(None, "blk", None, "frq"), P("blk")),
        out_specs=P("blk", None, None, "frq"),
        check_vma=False,
    )
```

profile of v0, /device:TPU:0, one launch (start us, length us, event | category | flops | bytes accessed | tf_op | source)
XLA Modules:
  0.0 905.1 jit_solution(15758095580509529953)
XLA Ops:
  86.1 29.7 %collective-permute-done.3 = bf16[2,256,4,1024]{3,2,1,0:T(4,128)(2,1)} collective-permute-done((bf16[2,256,4,1024]{3,2,1,0:T(4,128)(2,1)}, bf16[2,256,4,1024]{3,2,1,0:T(4,128)(2,1)}, u32[]{:S(2)}, u32[]{:S(2)}) %collective-permute-start.3) | collective-permute-done | bytes 4194336 | tf_op jit(solution)/shard_map/ppermute | solution.py:15
  123.6 84.9 %collective-permute-done.1 = bf16[2,256,4,1024]{3,2,1,0:T(4,128)(2,1)} collective-permute-done((bf16[2,256,4,1024]{3,2,1,0:T(4,128)(2,1)}, bf16[2,256,4,1024]{3,2,1,0:T(4,128)(2,1)}, u32[]{:S(2)}, u32[]{:S(2)}) %collective-permute-start.1) | collective-permute-done | bytes 4194336 | tf_op jit(solution)/shard_map/ppermute | solution.py:15
  346.8 13.6 %add_add_fusion = f32[512,4096]{1,0:T(8,128)} fusion(f32[512,4096]{1,0:T(8,128)} %fusion.82, f32[512,4096]{1,0:T(8,128)} %fusion.40, f32[512,4096]{1,0:T(8,128)} %fusion.59, bf16[256,4096]{1,0:T(8,128)(2,1)S(1)} %bitcast.120), kind=kOutput, calls=%fused_computation.3 | convolution fusion | flops 1081999360 | bytes 35651584 | tf_op jit(solution)/shard_map/dot_general | solution.py:34
  360.5 13.7 %add_add_fusion.1 = f32[512,4096]{1,0:T(8,128)} fusion(f32[512,4096]{1,0:T(8,128)} %fusion.84, f32[512,4096]{1,0:T(8,128)} %fusion.44, f32[512,4096]{1,0:T(8,128)} %fusion.61, bf16[256,4096]{1,0:T(8,128)(2,1)S(1)} %bitcast.124), kind=kOutput, calls=%fused_computation.7 | convolution fusion | flops 1081999360 | bytes 35651584 | tf_op jit(solution)/shard_map/dot_general | solution.py:34
  374.1 14.0 %add_add_fusion.2 = f32[512,4096]{1,0:T(8,128)} fusion(f32[512,4096]{1,0:T(8,128)} %fusion.86, f32[512,4096]{1,0:T(8,128)} %fusion.48, f32[512,4096]{1,0:T(8,128)} %fusion.63, bf16[256,4096]{1,0:T(8,128)(2,1)S(1)} %bitcast.128), kind=kOutput, calls=%fused_computation.11 | convolution fusion | flops 1081999360 | bytes 35651584 | tf_op jit(solution)/shard_map/dot_general | solution.py:34
  388.2 13.8 %add_add_fusion.3 = f32[512,4096]{1,0:T(8,128)} fusion(f32[512,4096]{1,0:T(8,128)} %fusion.88, f32[512,4096]{1,0:T(8,128)} %fusion.54, f32[512,4096]{1,0:T(8,128)} %fusion.66, bf16[256,4096]{1,0:T(8,128)(2,1)S(1)} %bitcast.132), kind=kOutput, calls=%fused_computation.16 | convolution fusion | flops 1081999360 | bytes 35651584 | tf_op jit(solution)/shard_map/dot_general | solution.py:34
  402.0 13.8 %add_subtract_fusion = f32[512,4096]{1,0:T(8,128)} fusion(f32[512,4096]{1,0:T(8,128)} %fusion.81, f32[512,4096]{1,0:T(8,128)} %fusion.38, f32[512,4096]{1,0:T(8,128)} %fusion.58, bf16[256,4096]{1,0:T(8,128)(2,1)S(1)} %bitcast.104), kind=kOutput, calls=%fused_computation.2 | convolution fusion | flops 1081999360 | bytes 35651584 | tf_op jit(solution)/shard_map/dot_general | solution.py:34
  415.7 9.9 %add_subtract_fusion.1 = f32[512,4096]{1,0:T(8,128)} fusion(f32[512,4096]{1,0:T(8,128)} %fusion.83, f32[512,4096]{1,0:T(8,128)S(1)} %bitcast.142, f32[512,4096]{1,0:T(8,128)} %fusion.60, bf16[256,4096]{1,0:T(8,128)(2,1)S(1)} %bitcast.108), kind=kOutput, calls=%fused_computation.6 | convolution fusion | flops 1081999360 | bytes 35651584 | tf_op jit(solution)/shard_map/dot_general | solution.py:34
  425.6 13.7 %add_subtract_fusion.2 = f32[512,4096]{1,0:T(8,128)} fusion(f32[512,4096]{1,0:T(8,128)} %fusion.85, f32[512,4096]{1,0:T(8,128)} %fusion.46, f32[512,4096]{1,0:T(8,128)} %fusion.62, bf16[256,4096]{1,0:T(8,128)(2,1)S(1)} %bitcast.112), kind=kOutput, calls=%fused_computation.10 | convolution fusion | flops 1081999360 | bytes 35651584 | tf_op jit(solution)/shard_map/dot_general | solution.py:34
  439.3 13.8 %add_subtract_fusion.3 = f32[512,4096]{1,0:T(8,128)} fusion(f32[512,4096]{1,0:T(8,128)} %fusion.87, f32[512,4096]{1,0:T(8,128)} %fusion.50, f32[512,4096]{1,0:T(8,128)} %fusion.64, bf16[256,4096]{1,0:T(8,128)(2,1)S(1)} %bitcast.116), kind=kOutput, calls=%fused_computation.14 | convolution fusion | flops 1081999360 | bytes 35651584 | tf_op jit(solution)/shard_map/dot_general | solution.py:34
  453.1 53.3 %multiply_subtract_fusion.3 = (f32[512,4096]{1,0:T(8,128)}, f32[512,4096]{1,0:T(8,128)}, f32[512,4096]{1,0:T(8,128)}, f32[512,4096]{1,0:T(8,128)}, f32[512,4096]...) fusion(f32[512,4096]{1,0:T(8,128)} %add_subtract_fusion.3, ...), kind=kOutput, calls=%fused_computation.12 | convolution fusion | flops 1132724224 | bytes 169869312 | tf_op jit(solution)/shard_map/dot_general | solution.py:34
  506.4 11.0 %add.286 = f32[512,4,1024]{2,1,0:T(4,128)} reshape(f32[512,4096]{1,0:T(8,128)} %get-tuple-element.6) | data formatting | bytes 16777216 | tf_op jit(solution)/shard_map/add | solution.py:51
  517.4 8.5 reduce_sum.82
  536.0 10.8 %add.294 = f32[512,4,1024]{2,1,0:T(4,128)} reshape(f32[512,4096]{1,0:T(8,128)} %get-tuple-element.17) | data formatting | bytes 16777216 | tf_op jit(solution)/shard_map/add | solution.py:51
  565.2 10.8 %add.302 = f32[512,4,1024]{2,1,0:T(4,128)} reshape(f32[512,4096]{1,0:T(8,128)} %get-tuple-element.15) | data formatting | bytes 16777216 | tf_op jit(solution)/shard_map/add | solution.py:51
  594.7 10.8 %add.310 = f32[512,4,1024]{2,1,0:T(4,128)} reshape(f32[512,4096]{1,0:T(8,128)} %get-tuple-element.13) | data formatting | bytes 16777216 | tf_op jit(solution)/shard_map/add | solution.py:51
  622.9 10.8 %sub.150 = f32[512,4,1024]{2,1,0:T(4,128)} reshape(f32[512,4096]{1,0:T(8,128)} %get-tuple-element.5) | data formatting | bytes 16777216 | tf_op jit(solution)/shard_map/sub | solution.py:52
  660.8 11.2 %sub.155 = f32[512,4,1024]{2,1,0:T(4,128)} reshape(f32[512,4096]{1,0:T(8,128)} %get-tuple-element.18) | data formatting | bytes 16777216 | tf_op jit(solution)/shard_map/sub | solution.py:52
  695.3 11.2 %sub.160 = f32[512,4,1024]{2,1,0:T(4,128)} reshape(f32[512,4096]{1,0:T(8,128)} %get-tuple-element.16) | data formatting | bytes 16777216 | tf_op jit(solution)/shard_map/sub | solution.py:52
  706.5 8.5 reduce_sum.87
  731.5 10.8 %sub.165 = f32[512,4,1024]{2,1,0:T(4,128)} reshape(f32[512,4096]{1,0:T(8,128)} %get-tuple-element.14) | data formatting | bytes 16777216 | tf_op jit(solution)/shard_map/sub | solution.py:52
  786.2 80.2 %reduce-scatter.7.cloned.1.call-done = f32[201,128]{1,0:T(8,128)} async-done(((f32[201,256]{1,0:T(8,128)}), f32[201,128]{1,0:T(8,128)}) %reduce-scatter.7.cloned.1.call-update) | async-done | bytes 102928 | tf_op jit(solution)/shard_map/reduce_scatter | solution.py:93
  866.3 16.6 %reduce-scatter.9.cloned.1.call-done = f32[201,128]{1,0:T(8,128)} async-done(((f32[201,256]{1,0:T(8,128)}), f32[201,128]{1,0:T(8,128)}) %reduce-scatter.9.cloned.1.call-update) | async-done | bytes 102928 | tf_op jit(solution)/shard_map/reduce_scatter | solution.py:93
  882.9 13.2 %reduce-scatter.11.cloned.1.call-done = f32[201,128]{1,0:T(8,128)} async-done(((f32[201,256]{1,0:T(8,128)}), f32[201,128]{1,0:T(8,128)}) %reduce-scatter.11.cloned.1.call-update) | async-done | bytes 102928 | tf_op jit(solution)/shard_map/reduce_scatter | solution.py:93
  (140 shorter events, 402.3 us)
Async XLA Ops:
  6.5 779.6 %reduce-scatter.5.cloned.1.call-start = ((), (), s32[]{:S(2)}) async-start(), calls=%async_computation.4 | async-start | bytes 319488 | tf_op jit(solution)/shard_map/reduce_scatter | solution.py:93
  19.6 96.2 %collective-permute-start.3 = (bf16[2,256,4,1024]{3,2,1,0:T(4,128)(2,1)}, bf16[2,256,4,1024]{3,2,1,0:T(4,128)(2,1)}, u32[]{:S(2)}, u32[]{:S(2)}) collective-permute-start(bf16[2,256,4,1024]{3,2,1,0:T(4,128)(2,1)} %multiply_convert_fusion), channel_id=1, source_target_pairs={{0,8},{2,10},{4,12},{6,14},{8,16},{10,18},{12,20},{14,22},{16,24},... | collective-permute-start | bytes 12582920 | tf_op jit(solution)/shard_map/ppermute | solution.py:15
  26.4 93.2 %collective-permute-start.2 = (bf16[2,256,4,1024]{3,2,1,0:T(4,128)(2,1)}, bf16[2,256,4,1024]{3,2,1,0:T(4,128)(2,1)}, u32[]{:S(2)}, u32[]{:S(2)}) collective-permute-start(bf16[2,256,4,1024]{3,2,1,0:T(4,128)(2,1)} %multiply_convert_fusion), channel_id=1, source_target_pairs={{0,6},{2,8},{4,10},{6,12},{8,14},{10,16},{12,18},{14,20},{16,22},{... | collective-permute-start | bytes 12582920 | tf_op jit(solution)/shard_map/ppermute | solution.py:15
  31.0 177.5 %collective-permute-start.1 = (bf16[2,256,4,1024]{3,2,1,0:T(4,128)(2,1)}, bf16[2,256,4,1024]{3,2,1,0:T(4,128)(2,1)}, u32[]{:S(2)}, u32[]{:S(2)}) collective-permute-start(bf16[2,256,4,1024]{3,2,1,0:T(4,128)(2,1)} %multiply_convert_fusion), channel_id=1, source_target_pairs={{0,4},{2,6},{4,8},{6,10},{8,12},{10,14},{12,16},{14,18},{16,20},{1... | collective-permute-start | bytes 12582920 | tf_op jit(solution)/shard_map/ppermute | solution.py:15
  35.1 208.9 %collective-permute-start = (bf16[2,256,4,1024]{3,2,1,0:T(4,128)(2,1)}, bf16[2,256,4,1024]{3,2,1,0:T(4,128)(2,1)}, u32[]{:S(2)}, u32[]{:S(2)}) collective-permute-start(bf16[2,256,4,1024]{3,2,1,0:T(4,128)(2,1)} %multiply_convert_fusion), channel_id=1, source_target_pairs={{0,2},{2,4},{4,6},{6,8},{8,10},{10,12},{12,14},{14,16},{16,18},{18... | collective-permute-start | bytes 12582920 | tf_op jit(solution)/shard_map/ppermute | solution.py:15
  42.6 5.2 copy-start
  60.3 16.8 %slice-start.2 = ((s8[8388608]{0:T(1024)(128)(4,1)}), s8[4194304]{0:T(1024)(128)(4,1)S(1)}, s32[]{:S(2)}) async-start(s8[8388608]{0:T(1024)(128)(4,1)} %bitcast.143), calls=%async_computation.10 | async-start | bytes 8388608
  60.3 16.8 %slice-start.4 = ((s8[8388608]{0:T(1024)(128)(4,1)}), s8[4194304]{0:T(1024)(128)(4,1)S(1)}, s32[]{:S(2)}) async-start(s8[8388608]{0:T(1024)(128)(4,1)} %bitcast.145), calls=%async_computation.12 | async-start | bytes 8388608
  65.6 5.8 copy-start.1
  65.6 11.5 %slice-start.3 = ((s8[8388608]{0:T(1024)(128)(4,1)}), s8[4194304]{0:T(1024)(128)(4,1)S(1)}, s32[]{:S(2)}) async-start(s8[8388608]{0:T(1024)(128)(4,1)} %bitcast.143), calls=%async_computation.11 | async-start | bytes 8388608
  65.6 11.5 %slice-start.5 = ((s8[8388608]{0:T(1024)(128)(4,1)}), s8[4194304]{0:T(1024)(128)(4,1)S(1)}, s32[]{:S(2)}) async-start(s8[8388608]{0:T(1024)(128)(4,1)} %bitcast.145), calls=%async_computation.13 | async-start | bytes 8388608
  388.2 27.6 %slice-start = ((s8[8388608]{0:T(1024)(128)(4,1)}), s8[4194304]{0:T(1024)(128)(4,1)S(1)}, s32[]{:S(2)}) async-start(s8[8388608]{0:T(1024)(128)(4,1)} %bitcast.141), calls=%async_computation.8 | async-start | bytes 8388608
  402.0 13.8 %slice-start.1 = ((s8[8388608]{0:T(1024)(128)(4,1)}), s8[4194304]{0:T(1024)(128)(4,1)S(1)}, s32[]{:S(2)}) async-start(s8[8388608]{0:T(1024)(128)(4,1)} %bitcast.141), calls=%async_computation.9 | async-start | bytes 8388608
  439.3 13.8 %copy-start.2 = (bf16[32,8,4,1024]{3,1,2,0:T(8,128)(2,1)S(1)}, bf16[32,8,4,1024]{3,1,2,0:T(8,128)(2,1)}, u32[]{:S(2)}) copy-start(bf16[32,8,4,1024]{3,1,2,0:T(8,128)(2,1)} %copy-done) | copy-start | bytes 6291460
  517.4 8.5 copy-start.8
  642.2 5.2 copy-start.6
  642.2 9.3 %copy-start.9 = (s32[1024]{0:T(1024)S(1)}, s32[1024]{0:T(1024)}, u32[]{:S(2)}) copy-start(s32[1024]{0:T(1024)} %iota_add_fusion) | copy-start | bytes 12292
  642.2 9.3 %copy-start.11 = (s32[201]{0:T(256)S(1)}, s32[201]{0:T(256)}, u32[]{:S(2)}) copy-start(s32[201]{0:T(256)} %iota_add_fusion.2) | copy-start | bytes 2416
  660.7 205.6 %reduce-scatter.7.cloned.1.call-start = ((), (), s32[]{:S(2)}) async-start(), calls=%async_computation.5 | async-start | bytes 319488 | tf_op jit(solution)/shard_map/reduce_scatter | solution.py:93
  680.5 6.6 copy-start.5
  715.0 16.5 %copy-start.3 = (f32[512,1024]{1,0:T(8,128)}, f32[512,1024]{1,0:T(8,128)S(1)}, u32[]{:S(2)}) copy-start(f32[512,1024]{1,0:T(8,128)S(1)} %reduce_sum.87) | copy-start | bytes 6291460
  757.6 125.3 %reduce-scatter.9.cloned.1.call-start = ((), (), s32[]{:S(2)}) async-start(), calls=%async_computation.6 | async-start | bytes 319488 | tf_op jit(solution)/shard_map/reduce_scatter | solution.py:93
  757.6 6.7 copy-start.7
  774.2 121.9 %reduce-scatter.11.cloned.1.call-start = ((), (), s32[]{:S(2)}) async-start(), calls=%async_computation.7 | async-start | bytes 319488 | tf_op jit(solution)/shard_map/reduce_scatter | solution.py:93
  (2 other events, 8.8 us)
Sparse Core Ops, SparseCore 0:
  660.9 108.5 reduce-scatter.4
  771.6 94.6 reduce-scatter.6
  868.5 14.2 reduce-scatter.8
  885.0 11.0 reduce-scatter.10
where the time goes:
time: 913 us; the launch traced here: 905 us
  matrix products  451 us (49%)
  waiting for transfers between devices  225 us (25%)
  local copies, waits for them, and re-layouts  112 us (12%)
  other arithmetic  83.8 us (9%)
  starting transfers between devices  19.5 us (2%)
  between operations  14.1 us (2%)
    dot_general x20, matrix products, twiddle_product(): jnp.dot(pair[0], data, preferred_element_type=jnp.float32)  170 us
    dot_general x20, matrix products, twiddle_product(): jnp.dot(pair[1], data, preferred_element_type=jnp.float32)  158 us
    dot_general x24, matrix products, matmul_high(): jnp.dot(left, right, precision=lax.Precision.HIGHEST, preferred_element_t...  123 us
    ppermute x4, waiting for transfers between devices, from_behind(): lax.ppermute(value, axis, [(source, source + steps) for source in range(f...  115 us
    reduce_scatter x4, waiting for transfers between devices, on_device(): lax.psum_scatter(partial_term, 'frq', scatter_dimension=1, tiled=True)  110 us
    sub x4, local copies, waits for them, and re-layouts, lag_terms(): own_hat[1] * far_hat[0] - own_hat[0] * far_hat[1]  44.1 us
    add x4, local copies, waits for them, and re-layouts, lag_terms(): own_hat[0] * far_hat[0] + own_hat[1] * far_hat[1]  43.5 us
    reduce_sum x4, other arithmetic, lag_terms(): jnp.sum(own_hat[0] * far_hat[0] + own_hat[1] * far_hat[1], axis=1)  34 us
  transfers between devices with their start and end apart: 8, of which 5 were waited for; matrix products, arithmetic and copies ran while one was open for 24% of the time, Pallas kernels for 0%

commit v1 on v0

v1 whole, which is shorter than its diff:
```python
import functools
import math

import jax
import jax.numpy as jnp
import ml_dtypes
import numpy as np
from jax import lax
from jax.experimental import pallas as pl
from jax.experimental.pallas import tpu as pltpu
from jax.sharding import PartitionSpec as P

LAGS = 201
ROUNDS = 4
GROUP = 4
PARTS = 2
LANES = 128
F32, BF16 = jnp.float32, jnp.bfloat16


def after(value, *others):
    return lax.optimization_barrier((value, others))[0]


def pair_list(part):
    pairs = []
    for own in range(GROUP):
        for distance in range(1, ROUNDS + 1):
            far = own - distance
            if far >= 0:
                pairs.append((own, far))
            elif part == 0:
                pairs.append((GROUP + own, far + GROUP))
            else:
                pairs.append((own, GROUP + far + GROUP))
    return pairs


def whiten_kernel(pieces, items, pos_ref, valid_ref, *refs):
    ins, outs, held = refs[: len(pieces)], refs[len(pieces) : -1], refs[-1]
    tile, windows = ins[0].shape[1:3]
    place = (tile, valid_ref.shape[1])
    row = lax.broadcasted_iota(jnp.int32, place, 0) + pl.program_id(0) * tile
    here = row == lax.broadcasted_iota(jnp.int32, place, 1)
    valid = jnp.sum(jnp.where(here, valid_ref[...].astype(F32), 0.0), axis=1, keepdims=True)
    for at, piece in enumerate(pieces):
        for half in range(2):
            held[at, half] = ins[at][half].reshape(tile * windows, LANES).astype(F32)
        values = [
            [held[at, half, pl.ds(w, tile, stride=windows), :] for half in range(2)] for w in range(windows)
        ]
        power = values[0][0] * values[0][0] + values[0][1] * values[0][1]
        for real, imag in values[1:]:
            power = power + (real * real + imag * imag)
        scale = valid / jnp.maximum(jnp.sqrt(power * (1.0 / windows)), 0.5)
        for w in range(windows):
            both = jnp.concatenate([values[w][half] * scale for half in range(2)], axis=1).astype(BF16)
            for item, out in zip(items, outs):
                for index, wanted in enumerate(item):
                    if wanted == piece:
                        out[index, w] = both


def whiten(spectra, valid, pos, items):
    _, channels, windows, freqs = spectra.shape
    parts = freqs // (GROUP * LANES)
    tile = min(64, channels)
    pieces = sorted({piece for item in items for piece in item})
    in_specs = [pl.BlockSpec((1, channels), lambda i, pos: (0, 0))] + [
        pl.BlockSpec(
            (2, tile, windows, LANES),
            lambda i, pos, flip=flip, part=part: (0, i, 0, (pos[0] ^ flip) * parts + part),
        )
        for flip, part in pieces
    ]
    out_specs = [pl.BlockSpec((len(item), windows, tile, 2 * LANES), lambda i, pos: (0, 0, i, 0)) for item in items]
    return pl.pallas_call(
        functools.partial(whiten_kernel, pieces, items),
        grid_spec=pltpu.PrefetchScalarGridSpec(
            num_scalar_prefetch=1,
            grid=(channels // tile,),
            in_specs=in_specs,
            out_specs=out_specs,
            scratch_shapes=[pltpu.VMEM((len(pieces), 2, tile * windows, LANES), F32)],
        ),
        out_shape=[jax.ShapeDtypeStruct((len(item), windows, channels, 2 * LANES), BF16) for item in items],
        compiler_params=pltpu.CompilerParams(vmem_limit_bytes=56 << 20),
        cost_estimate=pl.CostEstimate(flops=0, bytes_accessed=1000, transcendentals=0),
        name="whiten",
    )(pos, valid, *([spectra] * len(pieces)))


def correlate_kernel(pairs, pos_ref, *refs):
    blocks = refs[: 2 * GROUP]
    fwd_ref, lag_ref, inv_ref, keep_ref, send_ref, hat, plus, cross = refs[2 * GROUP :]
    w = pl.program_id(0)
    windows = pl.num_programs(0)
    member = pos_ref[0]
    half = fwd_ref.shape[0] // 2
    for index in range(2 * GROUP):
        slot = (member ^ (index % GROUP)) + (index // GROUP) * GROUP
        terms = jnp.dot(fwd_ref[...], blocks[index][0, 0], preferred_element_type=F32)
        cos_r, cos_i = terms[:half, :LANES], terms[:half, LANES:]
        sin_r, sin_i = terms[half:, :LANES], terms[half:, LANES:]
        hat[slot, w, 0] = cos_r + sin_i
        hat[slot, w, 1] = cos_i - sin_r
        hat[slot, w, 2] = cos_r - sin_i
        hat[slot, w, 3] = cos_i + sin_r

    @pl.when(w == windows - 1)
    def _():
        def products(step, carry):
            rows = pl.ds(pl.multiple_of(step * 8, 8), 8)
            odd_rows = pl.ds(pl.multiple_of(half + step * 8, 8), 8)
            sums = []
            for sign in range(2):
                sums = [None] * (2 * len(pairs))
                for win in range(hat.shape[1]):
                    real = [hat[slot, win, 2 * sign, rows, :] for slot in range(2 * GROUP)]
                    imag = [hat[slot, win, 2 * sign + 1, rows, :] for slot in range(2 * GROUP)]
                    for n, (own, far) in enumerate(pairs):
                        part_r = real[own] * real[far] + imag[own] * imag[far]
                        part_i = imag[own] * real[far] - real[own] * imag[far]
                        sums[2 * n] = part_r if win == 0 else sums[2 * n] + part_r
                        sums[2 * n + 1] = part_i if win == 0 else sums[2 * n + 1] + part_i
                for n in range(len(pairs)):
                    if sign == 0:
                        plus[2 * n], plus[2 * n + 1] = sums[2 * n], sums[2 * n + 1]
                    else:
                        plus_r, plus_i = plus[2 * n], plus[2 * n + 1]
                        minus_r, minus_i = sums[2 * n], sums[2 * n + 1]
                        cross[n, rows, :LANES] = plus_r + minus_r
                        cross[n, rows, LANES:] = plus_i + minus_i
                        cross[n, odd_rows, :LANES] = plus_i - minus_i
                        cross[n, odd_rows, LANES:] = minus_r - plus_r
            return carry

        lax.fori_loop(0, half // 8, products, 0)

        def lags(n, carry):
            folded = cross[n].astype(BF16)
            by_offset = jnp.dot(inv_ref[...], folded, preferred_element_type=F32).astype(BF16)
            result = jnp.dot(by_offset, lag_ref[0], preferred_element_type=F32).astype(BF16)
            flip = (n // ROUNDS) ^ member
            place, distance = flip // 2, n % ROUNDS

            @pl.when(flip % 2 == 0)
            def _():
                keep_ref[place, distance] = result

            @pl.when(flip % 2 == 1)
            def _():
                send_ref[place, distance] = result

            return carry

        lax.fori_loop(0, len(pairs), lags, 0, unroll=4)


def correlate(pos, part, blocks, tables):
    fwd, lag, inv = tables
    _, windows, channels, lanes = blocks[0][0].shape
    width = lag.shape[2]
    pairs = pair_list(part)
    half = fwd.shape[0] // 2
    in_specs = [
        pl.BlockSpec((1, 1, channels, lanes), lambda w, pos, place=place: (place, w, 0, 0)) for _, place in blocks
    ] + [
        pl.BlockSpec(fwd.shape, lambda w, pos: (0, 0)),
        pl.BlockSpec((1, lanes, width), lambda w, pos: ((pos[1] * GROUP + pos[0]) * PARTS + part, 0, 0)),
        pl.BlockSpec(inv.shape, lambda w, pos: (0, 0)),
    ]
    out_spec = pl.BlockSpec((2, ROUNDS, channels, width), lambda w, pos: (0, 0, 0, 0))
    return pl.pallas_call(
        functools.partial(correlate_kernel, pairs),
        grid_spec=pltpu.PrefetchScalarGridSpec(
            num_scalar_prefetch=1,
            grid=(windows,),
            in_specs=in_specs,
            out_specs=[out_spec, out_spec],
            scratch_shapes=[
                pltpu.VMEM((2 * GROUP, windows, 4, half, LANES), F32),
                pltpu.VMEM((2 * len(pairs), 8, LANES), F32),
                pltpu.VMEM((len(pairs), 2 * half, 2 * LANES), F32),
            ],
        ),
        out_shape=[jax.ShapeDtypeStruct((2, ROUNDS, channels, width), BF16)] * 2,
        compiler_params=pltpu.CompilerParams(vmem_limit_bytes=48 << 20),
        cost_estimate=pl.CostEstimate(flops=0, bytes_accessed=1000, transcendentals=0),
        name="correlate",
    )(pos, *[array for array, _ in blocks], fwd, lag, inv)


def halves_kernel(pos_ref, *refs):
    for index in range(4):
        keep, came, out = refs[index], refs[4 + index], refs[8 + index]
        out[...] = (keep[0].astype(F32) + came[0].astype(F32)).astype(out.dtype)


def halves(pos, keep, came):
    _, rounds, channels, width = keep.shape
    rows = channels // 2
    specs = [
        pl.BlockSpec((1, rounds, rows, width), lambda i, pos, f=f, g=g: (f, 0, pos[1] ^ g, 0))
        for f in range(2)
        for g in range(2)
    ]
    out_spec = pl.BlockSpec((rounds, rows, width), lambda i, pos: (0, 0, 0))
    return pl.pallas_call(
        halves_kernel,
        grid_spec=pltpu.PrefetchScalarGridSpec(
            num_scalar_prefetch=1, grid=(1,), in_specs=specs * 2, out_specs=[out_spec] * 4
        ),
        out_shape=[jax.ShapeDtypeStruct((rounds, rows, width), t) for t in (F32, BF16, BF16, BF16)],
        compiler_params=pltpu.CompilerParams(vmem_limit_bytes=32 << 20),
        name="halves",
    )(pos, *([keep] * 4), *([came] * 4))


def total_kernel(first, *refs):
    result = first[...]
    for ref in refs[:-1]:
        result = result + ref[...].astype(F32)
    refs[-1][...] = result.astype(refs[-1].dtype)


def total(first, *others):
    return pl.pallas_call(
        total_kernel,
        out_shape=jax.ShapeDtypeStruct(first.shape, BF16),
        name="total",
    )(first, *others)


def finish_kernel(normalizer, pos_ref, own_ref, behind_ref, *refs):
    member = pos_ref[0]
    out = refs[-1]
    for distance in range(ROUNDS):
        here = own_ref[distance].astype(F32)
        result = jnp.where(distance < member, here, behind_ref[distance].astype(F32))
        for ref in refs[:-1]:
            result = result + ref[distance].astype(F32)
        out[:, distance, :] = jnp.transpose(result * normalizer)[:LAGS]


def finish(pos, own, behind, terms, normalizer):
    width = own.shape[1]
    return pl.pallas_call(
        functools.partial(finish_kernel, normalizer),
        in_specs=[pl.BlockSpec(memory_space=pltpu.SMEM)]
        + [pl.BlockSpec(memory_space=pltpu.VMEM)] * (2 + len(terms)),
        out_shape=jax.ShapeDtypeStruct((LAGS, ROUNDS, width), F32),
        name="finish",
    )(pos, own, behind, *terms)


def make_tables(channels, freq_total, freq_local):
    half = 3 * channels // 4
    wave = 2 * np.arange(half) + 1
    period = 4 * half
    fwd_angle = 2.0 * np.pi / period * ((wave[:, None] * np.arange(channels)[None, :]) % period)
    fwd = np.concatenate([np.cos(fwd_angle), np.sin(fwd_angle)], axis=0)
    inv_angle = 2.0 * np.pi / period * ((wave[:, None] * (np.arange(channels) - channels // 2)[None, :]) % period)
    inv = np.concatenate([np.cos(inv_angle), -np.sin(inv_angle)], axis=0).T
    width = -(-LAGS // LANES) * LANES
    bins = freq_local // (GROUP * PARTS)
    tau = np.arange(LAGS) - (LAGS - 1) // 2
    lag_angle = np.pi / freq_total * ((np.arange(freq_total)[:, None] * tau[None, :]) % (2 * freq_total))
    lag_angle = lag_angle.reshape(freq_total // bins, bins, LAGS)
    lag = np.zeros((freq_total // bins, 2 * LANES, width), np.float64)
    lag[:, :bins, :LAGS] = np.cos(lag_angle)
    lag[:, LANES : LANES + bins, :LAGS] = -np.sin(lag_angle)
    return tuple(table.astype(ml_dtypes.bfloat16) for table in (fwd, lag, inv))


def on_device(n_frq, spectra, channel_valid):
    _, channels, windows, freq_local = spectra.shape
    n_blk = lax.axis_size("blk")
    freq_total = freq_local * n_frq
    fwd, lag, inv = make_tables(channels, freq_total, freq_local)
    tables = (jnp.asarray(fwd), jnp.asarray(lag), jnp.asarray(inv))
    normalizer = 1.0 / math.sqrt(windows * channels * freq_total) / (3 * channels // 2)
    member = lax.rem(lax.axis_index("blk"), GROUP)
    side = lax.axis_index("frq")
    pos = jnp.stack([member, side]).astype(jnp.int32)
    valid = channel_valid[None, :]
    bins = freq_local // (GROUP * PARTS)
    if bins != LANES:
        split = spectra.reshape(2, channels, windows, GROUP * PARTS, bins)
        split = jnp.pad(split, ((0, 0),) * 4 + ((0, LANES - bins),))
        spectra = split.reshape(2, channels, windows, GROUP * PARTS * LANES)

    def move(value, target):
        pairs = [(i, target(i)) for i in range(n_blk) if 0 <= target(i) < n_blk]
        return lax.ppermute(value, "blk", pairs)

    def swap(value, flip):
        return move(value, lambda i: i ^ flip)

    y02, y03 = whiten(spectra, valid, pos, [[(2, 0)], [(3, 0)]])
    y02_came = swap(y02, 2)
    y03_came = swap(y03, 3)
    own0, own1, core0, core1, core, y12, y13 = whiten(
        spectra,
        valid,
        after(pos, y02),
        [[(0, 0)], [(0, 1)], [(1, 0)], [(1, 1)], [(1, 0), (1, 1)], [(2, 1)], [(3, 1)]],
    )
    core_came = swap(core, 1)
    n00 = move(own0, lambda i: i - GROUP)
    n10 = move(own1, lambda i: i + GROUP)
    n01 = move(after(core0, core_came), lambda i: (i ^ 1) - GROUP)
    n11 = move(after(core1, n10), lambda i: (i ^ 1) + GROUP)
    y12_came = swap(after(y12, y02_came), 2)
    y13_came = swap(after(y13, y03_came), 3)
    far02 = move(after(y02_came, n00), lambda i: i - GROUP)
    far03 = move(after(y03_came, n01), lambda i: i - GROUP)
    far12 = move(after(y12_came, n11), lambda i: i + GROUP)
    far13 = move(y13_came, lambda i: i + GROUP)

    blocks0 = [(own0, 0), (core_came, 0), (y02_came, 0), (y03_came, 0), (n00, 0), (n01, 0), (far02, 0), (far03, 0)]
    blocks1 = [(own1, 0), (core_came, 1), (y12_came, 0), (y13_came, 0), (n10, 0), (n11, 0), (far12, 0), (far13, 0)]
    keep0, send0 = correlate(after(pos, y12_came, n11), 0, blocks0, tables)
    came0 = swap(send0, 1)

    if n_frq == 2:

        def both(value, flip, cross):
            flat = [(i, x) for i in range(n_blk) for x in range(2)]
            pairs = [(2 * i + x, 2 * (i ^ flip) + (x ^ cross)) for i, x in flat]
            return lax.ppermute(value, ("blk", "frq"), pairs)

        def spread(other, far_mine, far_other):
            return both(other, 0, 1), both(far_mine, 2, 0), both(far_other, 2, 1)

        mine0, *rest = halves(after(pos, far13), keep0, came0)
        rest = spread(*rest)
        keep1, send1 = correlate(pos, 1, blocks1, tables)
        sum0 = total(mine0, *rest)
        behind = move(sum0, lambda i: i + GROUP)
        mine1, *rest = halves(pos, keep1, swap(send1, 1))
        terms = (mine1, *spread(*rest))
    else:

        def spread(keep, came):
            both = keep.astype(F32) + came.astype(F32)
            mine = both[0] + swap(both[1].astype(BF16), 2).astype(F32)
            return lax.psum_scatter(mine, "frq", scatter_dimension=1, tiled=True)

        sum0 = spread(keep0, came0).astype(BF16)
        behind = move(sum0, lambda i: i + GROUP)
        keep1, send1 = correlate(pos, 1, blocks1, tables)
        terms = (spread(keep1, swap(send1, 1)),)
    stacked = finish(pos, sum0, behind, terms, normalizer)
    return jnp.transpose(stacked, (1, 0, 2))[None]


def solution(mesh):
    return jax.shard_map(
        functools.partial(on_device, mesh.shape["frq"]),
        mesh=mesh,
        in_specs=(P(None, "blk", None, "frq"), P("blk")),
        out_specs=P("blk", None, None, "frq"),
        check_vma=False,
    )
```

time: 913 us -> 134 us (0.15)
  matrix products: 451 us -> 0 us
  waiting for transfers between devices: 225 us -> 42.1 us
  local copies, waits for them, and re-layouts: 112 us -> 3.37 us
  other arithmetic: 83.8 us -> 0.59 us
  Pallas kernels: 0 us -> 47.8 us
  starting transfers between devices: 19.5 us -> 39.2 us
  between operations: 14.1 us -> 0.31 us
    dot_general x64 -> x0, matrix products: 451 us -> none  [the longest x20 170 us: twiddle_product(): jnp.dot(pair[0], data, preferred_element_type=jnp.float32)]
    reduce_scatter x4 -> x0, waiting for transfers between devices: 110 us -> none  [on_device(): lax.psum_scatter(partial_term, 'frq', scatter_dimension=1, tiled=True)]
    ppermute x4 -> x22, waiting for transfers between devices: 115 us -> 42.1 us  [the longest x16 32.7 us: move(): return lax.ppermute(value, 'blk', pairs)]
    reduce_sum x9 -> x0, other arithmetic: 72.1 us -> none  [the longest x4 34 us: lag_terms(): jnp.sum(own_hat[0] * far_hat[0] + own_hat[1] * far_hat[1], axis=1)]
    pallas_call x0 -> x8, Pallas kernels: none -> 47.8 us  [the longest x2 30.4 us: correlate(): pl.pallas_call(functools.partial(correlate_kernel, pairs), grid_spec=pltp...]
    sub x4 -> x0, local copies, waits for them, and re-layouts: 44.1 us -> none  [lag_terms(): own_hat[1] * far_hat[0] - own_hat[0] * far_hat[1]]
    add x4 -> x0, local copies, waits for them, and re-layouts: 43.5 us -> none  [lag_terms(): own_hat[0] * far_hat[0] + own_hat[1] * far_hat[1]]
    ppermute x4 -> x22, starting transfers between devices: 19.1 us -> 39.2 us  [the longest x16 30.1 us: move(): return lax.ppermute(value, 'blk', pairs)]
  transfers between devices with their start and end apart: 8 -> 22, of which waited for: 5 -> 10; matrix products, arithmetic and copies ran while one was open for 24% -> 0% of each run, Pallas kernels for 0% -> 26%
where the time goes in v1:
time: 134 us; the launch traced here: 133 us
  Pallas kernels  47.8 us (36%)
  waiting for transfers between devices  42.1 us (31%)
  starting transfers between devices  39.2 us (29%)
  local copies, waits for them, and re-layouts  3.37 us (3%)
    ppermute x16, waiting for transfers between devices, move(): return lax.ppermute(value, 'blk', pairs)  32.7 us
    pallas_call x2, Pallas kernels, correlate(): pl.pallas_call(functools.partial(correlate_kernel, pairs), grid_spec=pltp...  30.4 us
    ppermute x16, starting transfers between devices, move(): return lax.ppermute(value, 'blk', pairs)  30.1 us
    pallas_call x2, Pallas kernels, whiten(): pl.pallas_call(functools.partial(whiten_kernel, pieces, items), grid_spec...  11.2 us
    ppermute x6, waiting for transfers between devices, both(): return lax.ppermute(value, ('blk', 'frq'), pairs)  9.42 us
    ppermute x6, starting transfers between devices, both(): return lax.ppermute(value, ('blk', 'frq'), pairs)  9.02 us
    unnamed x34, local copies, waits for them, and re-layouts  3.37 us
  transfers between devices with their start and end apart: 22, of which 10 were waited for; matrix products, arithmetic and copies ran while one was open for 0% of the time, Pallas kernels for 26%

profile of v1, /device:TPU:0, one launch (start us, length us, event | category | flops | bytes accessed | tf_op | source)
XLA Modules:
  0.0 133.3 jit_solution(11082421021863618742)
XLA Ops:
  0.6 4.5 %whiten.2 = (bf16[1,4,256,256]{3,2,1,0:T(8,128)(2,1)}, bf16[1,4,256,256]{3,2,1,0:T(8,128)(2,1)}) custom-call(s32[2]{0:T(128)} %pad_add_fusion.pos_ref, s32[1,256]{1,0:T(1,128)} %bitcast.6, bf16[2,256,4,1024]{3,2,1,0:T(4,128)(2,1)} %refs_5_.1, bf16[2,256,4,1024]{3,2,1,0:T(4,128)(2,1)} %refs_5_.1), custom_call_target="tpu_custom_call" | custom-call | bytes 1000 | tf_op jit(solution)/shard_map/whiten/pallas_call | solution.py:77
  5.2 6.6 %whiten.3 = (bf16[1,4,256,256]{3,2,1,0:T(8,128)(2,1)}, bf16[1,4,256,256]{3,2,1,0:T(8,128)(2,1)}, bf16[1,4,256,256]{3,2,1,0:T(8,128)(2,1)}, bf16[1,4,256,256]{3,2...) custom-call(s32[2]{0:T(128)} %pad_add_fusion.pos_ref, ...), custom_call_target="tpu_custom_call" | custom-call | bytes 1000 | tf_op jit(solution)/shard_map/whiten/pallas_call | solution.py:77
  12.3 4.7 %collective-permute-start.5 = (bf16[1,4,256,256]{3,2,1,0:T(8,128)(2,1)}, bf16[1,4,256,256]{3,2,1,0:T(8,128)(2,1)S(1)}, u32[]{:S(2)}, u32[]{:S(2)}) collective-permute-start(bf16[1,4,256,256]{3,2,1,0:T(8,128)(2,1)} %get-tuple-element.45.refs_0_), channel_id=1, source_target_pairs={{0,8},{2,10},{4,12},{6,14},{8,16},{10,18},{12,20},{14,22},{16,24},... | collective-permute-start | bytes 1572872 | tf_op jit(solution)/shard_map/ppermute | solution.py:295
  17.0 1.6 %collective-permute-start.3 = (bf16[1,4,256,256]{3,2,1,0:T(8,128)(2,1)S(1)}, bf16[1,4,256,256]{3,2,1,0:T(8,128)(2,1)S(1)}, u32[]{:S(2)}, u32[]{:S(2)}) collective-permute-start(bf16[1,4,256,256]{3,2,1,0:T(8,128)(2,1)S(1)} %copy-done.16), channel_id=1, source_target_pairs={{0,4},{2,6},{4,0},{6,2},{8,12},{10,14},{12,8},{14,10},{16,20},{18,... | collective-permute-start | bytes 1572872 | tf_op jit(solution)/shard_map/ppermute | solution.py:295
  21.2 7.8 %collective-permute-done.5.refs_4_ = bf16[1,4,256,256]{3,2,1,0:T(8,128)(2,1)S(1)} collective-permute-done((bf16[1,4,256,256]{3,2,1,0:T(8,128)(2,1)}, bf16[1,4,256,256]{3,2,1,0:T(8,128)(2,1)S(1)}, u32[]{:S(2)}, u32[]{:S(2)}) %collective-permute-start.5) | collective-permute-done | bytes 524320 | tf_op jit(solution)/shard_map/ppermute | solution.py:295
  28.9 3.5 %collective-permute-start.6 = (bf16[1,4,256,256]{3,2,1,0:T(8,128)(2,1)}, bf16[1,4,256,256]{3,2,1,0:T(8,128)(2,1)S(1)}, u32[]{:S(2)}, u32[]{:S(2)}) collective-permute-start(bf16[1,4,256,256]{3,2,1,0:T(8,128)(2,1)} %get-tuple-element.46), channel_id=1, source_target_pairs={{0,10},{2,8},{4,14},{6,12},{8,18},{10,16},{12,22},{14,20},{16,26},... | collective-permute-start | bytes 1572872 | tf_op jit(solution)/shard_map/ppermute | solution.py:295
  32.4 1.6 %collective-permute-start.4 = (bf16[1,4,256,256]{3,2,1,0:T(8,128)(2,1)}, bf16[1,4,256,256]{3,2,1,0:T(8,128)(2,1)S(1)}, u32[]{:S(2)}, u32[]{:S(2)}) collective-permute-start(bf16[1,4,256,256]{3,2,1,0:T(8,128)(2,1)} %get-tuple-element.43), channel_id=1, source_target_pairs={{0,4},{2,6},{4,0},{6,2},{8,12},{10,14},{12,8},{14,10},{16,20},{18,... | collective-permute-start | bytes 1572872 | tf_op jit(solution)/shard_map/ppermute | solution.py:295
  34.0 8.1 %collective-permute-done.refs_3_ = bf16[1,4,256,256]{3,2,1,0:T(8,128)(2,1)S(1)} collective-permute-done((bf16[1,4,256,256]{3,2,1,0:T(8,128)(2,1)S(1)}, bf16[1,4,256,256]{3,2,1,0:T(8,128)(2,1)S(1)}, u32[]{:S(2)}, u32[]{:S(2)}) %collective-permute-start) | collective-permute-done | bytes 524320 | tf_op jit(solution)/shard_map/ppermute | solution.py:295
  42.1 2.2 %collective-permute-start.1 = (bf16[1,4,256,256]{3,2,1,0:T(8,128)(2,1)}, bf16[1,4,256,256]{3,2,1,0:T(8,128)(2,1)S(1)}, u32[]{:S(2)}, u32[]{:S(2)}) collective-permute-start(bf16[1,4,256,256]{3,2,1,0:T(8,128)(2,1)} %get-tuple-element.40), channel_id=1, source_target_pairs={{0,6},{2,4},{4,2},{6,0},{8,14},{10,12},{12,10},{14,8},{16,22},{18,... | collective-permute-start | bytes 1572872 | tf_op jit(solution)/shard_map/ppermute | solution.py:295
  47.4 6.9 %collective-permute-done.4.refs_2_ = bf16[1,4,256,256]{3,2,1,0:T(8,128)(2,1)S(1)} collective-permute-done((bf16[1,4,256,256]{3,2,1,0:T(8,128)(2,1)}, bf16[1,4,256,256]{3,2,1,0:T(8,128)(2,1)S(1)}, u32[]{:S(2)}, u32[]{:S(2)}) %collective-permute-start.4) | collective-permute-done | bytes 524320 | tf_op jit(solution)/shard_map/ppermute | solution.py:295
  54.3 3.5 %collective-permute-start.17 = (bf16[1,4,256,256]{3,2,1,0:T(8,128)(2,1)S(1)}, bf16[1,4,256,256]{3,2,1,0:T(8,128)(2,1)S(1)}, u32[]{:S(2)}, u32[]{:S(2)}) collective-permute-start(bf16[1,4,256,256]{3,2,1,0:T(8,128)(2,1)S(1)} %collective-permute-done.4.refs_2_), channel_id=1, source_target_pairs={{0,8},{2,10},{4,12},{6,14},{8,16},{10,18},{12,20},{14,22},{16,24},... | collective-permute-start | bytes 1572872 | tf_op jit(solution)/shard_map/ppermute | solution.py:295
  57.8 6.0 %collective-permute-done.1.refs_3_ = bf16[1,4,256,256]{3,2,1,0:T(8,128)(2,1)S(1)} collective-permute-done((bf16[1,4,256,256]{3,2,1,0:T(8,128)(2,1)}, bf16[1,4,256,256]{3,2,1,0:T(8,128)(2,1)S(1)}, u32[]{:S(2)}, u32[]{:S(2)}) %collective-permute-start.1) | collective-permute-done | bytes 524320 | tf_op jit(solution)/shard_map/ppermute | solution.py:295
  63.8 3.5 %collective-permute-start.2 = (bf16[1,4,256,256]{3,2,1,0:T(8,128)(2,1)S(1)}, bf16[1,4,256,256]{3,2,1,0:T(8,128)(2,1)S(1)}, u32[]{:S(2)}, u32[]{:S(2)}) collective-permute-start(bf16[1,4,256,256]{3,2,1,0:T(8,128)(2,1)S(1)} %collective-permute-done.1.refs_3_), channel_id=1, source_target_pairs={{0,8},{2,10},{4,12},{6,14},{8,16},{10,18},{12,20},{14,22},{16,24},... | collective-permute-start | bytes 1572872 | tf_op jit(solution)/shard_map/ppermute | solution.py:295
  67.3 2.8 %collective-permute-done.11.refs_7_ = bf16[1,4,256,256]{3,2,1,0:T(8,128)(2,1)S(1)} collective-permute-done((bf16[1,4,256,256]{3,2,1,0:T(8,128)(2,1)S(1)}, bf16[1,4,256,256]{3,2,1,0:T(8,128)(2,1)S(1)}, u32[]{:S(2)}, u32[]{:S(2)}) %collective-permute-start.11) | collective-permute-done | bytes 524320 | tf_op jit(solution)/shard_map/ppermute | solution.py:295
  71.2 15.4 %correlate.2 = (bf16[2,4,256,256]{3,2,1,0:T(8,128)(2,1)S(1)}, bf16[2,4,256,256]{3,2,1,0:T(8,128)(2,1)S(1)}) custom-call(s32[2]{0:T(128)S(1)} %copy-done.6, bf16[1,4,256,256]{3,2,1,0:T(8,128)(2,1)S(1)} %copy-done.3, bf16[2,4,256,256]{3,2,1,0:T(8,128)(2,1)} %copy-done.7, bf16[1,4,256,256]{3,2,1,0:T(8,128)(2,1)S(1)} %collective-permute-done.3.refs_2_, ...), custom_call_target="tpu_custom_call" | custom-call | bytes 1000 | tf_op jit(solution)/shard_map/correlate/pallas_call | solution.py:174
  86.7 15.1 %correlate.3 = (bf16[2,4,256,256]{3,2,1,0:T(8,128)(2,1)S(1)}, bf16[2,4,256,256]{3,2,1,0:T(8,128)(2,1)S(1)}) custom-call(s32[2]{0:T(128)S(1)} %copy-done.6, bf16[1,4,256,256]{3,2,1,0:T(8,128)(2,1)S(1)} %copy-done.2, bf16[2,4,256,256]{3,2,1,0:T(8,128)(2,1)} %copy-done.7, bf16[1,4,256,256]{3,2,1,0:T(8,128)(2,1)S(1)} %collective-permute-done.4.refs_2_, ...), custom_call_target="tpu_custom_call" | custom-call | bytes 1000 | tf_op jit(solution)/shard_map/correlate/pallas_call | solution.py:174
  103.1 1.6 %collective-permute-start.13 = (bf16[4,128,256]{2,1,0:T(8,128)(2,1)S(1)}, bf16[4,128,256]{2,1,0:T(8,128)(2,1)S(1)}, u32[]{:S(2)}, u32[]{:S(2)}) collective-permute-start(bf16[4,128,256]{2,1,0:T(8,128)(2,1)S(1)} %get-tuple-element.57), channel_id=1, source_target_pairs={{0,1},{1,0},{2,3},{3,2},{4,5},{5,4},{6,7},{7,6},{8,9},{9,8},{10,11... | collective-permute-start | bytes 786440 | tf_op jit(solution)/shard_map/ppermute | solution.py:331
  104.7 1.5 %collective-permute-start.14 = (bf16[4,128,256]{2,1,0:T(8,128)(2,1)S(1)}, bf16[4,128,256]{2,1,0:T(8,128)(2,1)S(1)}, u32[]{:S(2)}, u32[]{:S(2)}) collective-permute-start(bf16[4,128,256]{2,1,0:T(8,128)(2,1)S(1)} %get-tuple-element.58), channel_id=1, source_target_pairs={{0,4},{1,5},{2,6},{3,7},{4,0},{5,1},{6,2},{7,3},{8,12},{9,13},{10,... | collective-permute-start | bytes 786440 | tf_op jit(solution)/shard_map/ppermute | solution.py:331
  112.3 2.5 %collective-permute-start.21 = (bf16[4,128,256]{2,1,0:T(8,128)(2,1)S(1)}, bf16[4,128,256]{2,1,0:T(8,128)(2,1)S(1)}, u32[]{:S(2)}, u32[]{:S(2)}) collective-permute-start(bf16[4,128,256]{2,1,0:T(8,128)(2,1)S(1)} %get-tuple-element.66), channel_id=1, source_target_pairs={{0,5},{1,4},{2,7},{3,6},{4,1},{5,0},{6,3},{7,2},{8,13},{9,12},{10,... | collective-permute-start | bytes 786440 | tf_op jit(solution)/shard_map/ppermute | solution.py:331
  114.8 4.7 %collective-permute-done.14.refs_1_ = bf16[4,128,256]{2,1,0:T(8,128)(2,1)S(1)} collective-permute-done((bf16[4,128,256]{2,1,0:T(8,128)(2,1)S(1)}, bf16[4,128,256]{2,1,0:T(8,128)(2,1)S(1)}, u32[]{:S(2)}, u32[]{:S(2)}) %collective-permute-start.14) | collective-permute-done | bytes 262176 | tf_op jit(solution)/shard_map/ppermute | solution.py:331
  120.3 2.1 %total.1.own_ref = bf16[4,128,256]{2,1,0:T(8,128)(2,1)} custom-call(f32[4,128,256]{2,1,0:T(8,128)} %copy-done.4, bf16[4,128,256]{2,1,0:T(8,128)(2,1)} %copy-done.8, bf16[4,128,256]{2,1,0:T(8,128)(2,1)} %copy-done.9, bf16[4,128,256]{2,1,0:T(8,128)(2,1)} %copy-done.10), custom_call_target="tpu_custom_call" | custom-call | tf_op jit(solution)/shard_map/total/pallas_call | solution.py:228
  122.4 3.4 %collective-permute-start.16 = (bf16[4,128,256]{2,1,0:T(8,128)(2,1)}, bf16[4,128,256]{2,1,0:T(8,128)(2,1)S(1)}, u32[]{:S(2)}, u32[]{:S(2)}) collective-permute-start(bf16[4,128,256]{2,1,0:T(8,128)(2,1)} %total.1.own_ref), channel_id=1, source_target_pairs={{0,8},{2,10},{4,12},{6,14},{8,16},{10,18},{12,20},{14,22},{16,24},... | collective-permute-start | bytes 786440 | tf_op jit(solution)/shard_map/ppermute | solution.py:295
  125.8 3.6 %collective-permute-done.20.refs_2_ = bf16[4,128,256]{2,1,0:T(8,128)(2,1)S(1)} collective-permute-done((bf16[4,128,256]{2,1,0:T(8,128)(2,1)S(1)}, bf16[4,128,256]{2,1,0:T(8,128)(2,1)S(1)}, u32[]{:S(2)}, u32[]{:S(2)}) %collective-permute-start.20) | collective-permute-done | bytes 262176 | tf_op jit(solution)/shard_map/ppermute | solution.py:331
  130.7 2.6 %finish.1 = f32[201,4,128]{2,1,0:T(4,128)} custom-call(s32[2]{0:T(128)} %pad_add_fusion.pos_ref, bf16[4,128,256]{2,1,0:T(8,128)(2,1)} %total.1.own_ref, bf16[4,128,256]{2,1,0:T(8,128)(2,1)} %copy-done.14, f32[4,128,256]{2,1,0:T(8,128)} %copy-done.5, bf16[4,128,256]{2,1,0:T(8,128)(2,1)} %copy-done.11, bf16[4,128,256]{2,1,0:T(8,128)(2,1)} %copy-done.12, ...), custom_call_target="tpu_custom_call" | custom-call | tf_op jit(solution)/shard_map/finish/pallas_call | solution.py:248
  (63 shorter events, 17.4 us)
Async XLA Ops:
  5.1 65.0 %copy-start = (bf16[384,256]{1,0:T(8,128)(2,1)S(1)}, bf16[384,256]{1,0:T(8,128)(2,1)}, u32[]{:S(2)}) copy-start(bf16[384,256]{1,0:T(8,128)(2,1)} %constant.19.clone.refs_8_) | copy-start | bytes 589828
  11.8 74.9 %copy-start.2 = (bf16[1,4,256,256]{3,2,1,0:T(8,128)(2,1)S(1)}, bf16[1,4,256,256]{3,2,1,0:T(8,128)(2,1)}, u32[]{:S(2)}) copy-start(bf16[1,4,256,256]{3,2,1,0:T(8,128)(2,1)} %get-tuple-element.45.refs_0_) | copy-start | bytes 1572868
  11.8 8.1 %collective-permute-start.7 = (bf16[2,4,256,256]{3,2,1,0:T(8,128)(2,1)}, bf16[2,4,256,256]{3,2,1,0:T(8,128)(2,1)S(1)}, u32[]{:S(2)}, u32[]{:S(2)}) collective-permute-start(bf16[2,4,256,256]{3,2,1,0:T(8,128)(2,1)} %get-tuple-element.49), channel_id=1, source_target_pairs={{0,2},{2,0},{4,6},{6,4},{8,10},{10,8},{12,14},{14,12},{16,18},{18,... | collective-permute-start | bytes 3145736 | tf_op jit(solution)/shard_map/ppermute | solution.py:295
  12.3 16.6 %collective-permute-start.5 = (bf16[1,4,256,256]{3,2,1,0:T(8,128)(2,1)}, bf16[1,4,256,256]{3,2,1,0:T(8,128)(2,1)S(1)}, u32[]{:S(2)}, u32[]{:S(2)}) collective-permute-start(bf16[1,4,256,256]{3,2,1,0:T(8,128)(2,1)} %get-tuple-element.45.refs_0_), channel_id=1, source_target_pairs={{0,8},{2,10},{4,12},{6,14},{8,16},{10,18},{12,20},{14,22},{16,24},... | collective-permute-start | bytes 1572872 | tf_op jit(solution)/shard_map/ppermute | solution.py:295
  17.0 15.4 %collective-permute-start.3 = (bf16[1,4,256,256]{3,2,1,0:T(8,128)(2,1)S(1)}, bf16[1,4,256,256]{3,2,1,0:T(8,128)(2,1)S(1)}, u32[]{:S(2)}, u32[]{:S(2)}) collective-permute-start(bf16[1,4,256,256]{3,2,1,0:T(8,128)(2,1)S(1)} %copy-done.16), channel_id=1, source_target_pairs={{0,4},{2,6},{4,0},{6,2},{8,12},{10,14},{12,8},{14,10},{16,20},{18,... | collective-permute-start | bytes 1572872 | tf_op jit(solution)/shard_map/ppermute | solution.py:295
  18.6 23.5 %collective-permute-start = (bf16[1,4,256,256]{3,2,1,0:T(8,128)(2,1)S(1)}, bf16[1,4,256,256]{3,2,1,0:T(8,128)(2,1)S(1)}, u32[]{:S(2)}, u32[]{:S(2)}) collective-permute-start(bf16[1,4,256,256]{3,2,1,0:T(8,128)(2,1)S(1)} %copy-done.15), channel_id=1, source_target_pairs={{0,6},{2,4},{4,2},{6,0},{8,14},{10,12},{12,10},{14,8},{16,22},{18,... | collective-permute-start | bytes 1572872 | tf_op jit(solution)/shard_map/ppermute | solution.py:295
  18.6 25.7 %collective-permute-start.8 = (bf16[1,4,256,256]{3,2,1,0:T(8,128)(2,1)}, bf16[1,4,256,256]{3,2,1,0:T(8,128)(2,1)S(1)}, u32[]{:S(2)}, u32[]{:S(2)}) collective-permute-start(bf16[1,4,256,256]{3,2,1,0:T(8,128)(2,1)} %get-tuple-element.48.refs_0_), channel_id=1, source_target_pairs={{8,0},{10,2},{12,4},{14,6},{16,8},{18,10},{20,12},{22,14},{24,16},... | collective-permute-start | bytes 1572872 | tf_op jit(solution)/shard_map/ppermute | solution.py:295
  19.9 26.2 %collective-permute-start.9 = (bf16[1,4,256,256]{3,2,1,0:T(8,128)(2,1)}, bf16[1,4,256,256]{3,2,1,0:T(8,128)(2,1)S(1)}, u32[]{:S(2)}, u32[]{:S(2)}) collective-permute-start(bf16[1,4,256,256]{3,2,1,0:T(8,128)(2,1)} %get-tuple-element.51), channel_id=1, source_target_pairs={{8,2},{10,0},{12,6},{14,4},{16,10},{18,8},{20,14},{22,12},{24,18},... | collective-permute-start | bytes 1572872 | tf_op jit(solution)/shard_map/ppermute | solution.py:295
  28.9 18.4 %collective-permute-start.6 = (bf16[1,4,256,256]{3,2,1,0:T(8,128)(2,1)}, bf16[1,4,256,256]{3,2,1,0:T(8,128)(2,1)S(1)}, u32[]{:S(2)}, u32[]{:S(2)}) collective-permute-start(bf16[1,4,256,256]{3,2,1,0:T(8,128)(2,1)} %get-tuple-element.46), channel_id=1, source_target_pairs={{0,10},{2,8},{4,14},{6,12},{8,18},{10,16},{12,22},{14,20},{16,26},... | collective-permute-start | bytes 1572872 | tf_op jit(solution)/shard_map/ppermute | solution.py:295
  32.4 21.9 %collective-permute-start.4 = (bf16[1,4,256,256]{3,2,1,0:T(8,128)(2,1)}, bf16[1,4,256,256]{3,2,1,0:T(8,128)(2,1)S(1)}, u32[]{:S(2)}, u32[]{:S(2)}) collective-permute-start(bf16[1,4,256,256]{3,2,1,0:T(8,128)(2,1)} %get-tuple-element.43), channel_id=1, source_target_pairs={{0,4},{2,6},{4,0},{6,2},{8,12},{10,14},{12,8},{14,10},{16,20},{18,... | collective-permute-start | bytes 1572872 | tf_op jit(solution)/shard_map/ppermute | solution.py:295
  42.1 21.7 %collective-permute-start.1 = (bf16[1,4,256,256]{3,2,1,0:T(8,128)(2,1)}, bf16[1,4,256,256]{3,2,1,0:T(8,128)(2,1)S(1)}, u32[]{:S(2)}, u32[]{:S(2)}) collective-permute-start(bf16[1,4,256,256]{3,2,1,0:T(8,128)(2,1)} %get-tuple-element.40), channel_id=1, source_target_pairs={{0,6},{2,4},{4,2},{6,0},{8,14},{10,12},{12,10},{14,8},{16,22},{18,... | collective-permute-start | bytes 1572872 | tf_op jit(solution)/shard_map/ppermute | solution.py:295
  44.3 23.0 %collective-permute-start.10 = (bf16[1,4,256,256]{3,2,1,0:T(8,128)(2,1)S(1)}, bf16[1,4,256,256]{3,2,1,0:T(8,128)(2,1)S(1)}, u32[]{:S(2)}, u32[]{:S(2)}) collective-permute-start(bf16[1,4,256,256]{3,2,1,0:T(8,128)(2,1)S(1)} %collective-permute-done.3.refs_2_), channel_id=1, source_target_pairs={{8,0},{10,2},{12,4},{14,6},{16,8},{18,10},{20,12},{22,14},{24,16},... | collective-permute-start | bytes 1572872 | tf_op jit(solution)/shard_map/ppermute | solution.py:295
  46.1 24.0 %collective-permute-start.11 = (bf16[1,4,256,256]{3,2,1,0:T(8,128)(2,1)S(1)}, bf16[1,4,256,256]{3,2,1,0:T(8,128)(2,1)S(1)}, u32[]{:S(2)}, u32[]{:S(2)}) collective-permute-start(bf16[1,4,256,256]{3,2,1,0:T(8,128)(2,1)S(1)} %collective-permute-done.refs_3_), channel_id=1, source_target_pairs={{8,0},{10,2},{12,4},{14,6},{16,8},{18,10},{20,12},{22,14},{24,16},... | collective-permute-start | bytes 1572872 | tf_op jit(solution)/shard_map/ppermute | solution.py:295
  54.3 32.3 %collective-permute-start.17 = (bf16[1,4,256,256]{3,2,1,0:T(8,128)(2,1)S(1)}, bf16[1,4,256,256]{3,2,1,0:T(8,128)(2,1)S(1)}, u32[]{:S(2)}, u32[]{:S(2)}) collective-permute-start(bf16[1,4,256,256]{3,2,1,0:T(8,128)(2,1)S(1)} %collective-permute-done.4.refs_2_), channel_id=1, source_target_pairs={{0,8},{2,10},{4,12},{6,14},{8,16},{10,18},{12,20},{14,22},{16,24},... | collective-permute-start | bytes 1572872 | tf_op jit(solution)/shard_map/ppermute | solution.py:295
  63.8 22.9 %collective-permute-start.2 = (bf16[1,4,256,256]{3,2,1,0:T(8,128)(2,1)S(1)}, bf16[1,4,256,256]{3,2,1,0:T(8,128)(2,1)S(1)}, u32[]{:S(2)}, u32[]{:S(2)}) collective-permute-start(bf16[1,4,256,256]{3,2,1,0:T(8,128)(2,1)S(1)} %collective-permute-done.1.refs_3_), channel_id=1, source_target_pairs={{0,8},{2,10},{4,12},{6,14},{8,16},{10,18},{12,20},{14,22},{16,24},... | collective-permute-start | bytes 1572872 | tf_op jit(solution)/shard_map/ppermute | solution.py:295
  86.6 15.7 %collective-permute-start.12 = (bf16[2,4,256,256]{3,2,1,0:T(8,128)(2,1)S(1)}, bf16[2,4,256,256]{3,2,1,0:T(8,128)(2,1)S(1)}, u32[]{:S(2)}, u32[]{:S(2)}) collective-permute-start(bf16[2,4,256,256]{3,2,1,0:T(8,128)(2,1)S(1)} %get-tuple-element.55), channel_id=1, source_target_pairs={{0,2},{2,0},{4,6},{6,4},{8,10},{10,8},{12,14},{14,12},{16,18},{18,... | collective-permute-start | bytes 3145736 | tf_op jit(solution)/shard_map/ppermute | solution.py:295
  101.8 4.9 %collective-permute-start.18 = (bf16[2,4,256,256]{3,2,1,0:T(8,128)(2,1)S(1)}, bf16[2,4,256,256]{3,2,1,0:T(8,128)(2,1)S(1)}, u32[]{:S(2)}, u32[]{:S(2)}) collective-permute-start(bf16[2,4,256,256]{3,2,1,0:T(8,128)(2,1)S(1)} %get-tuple-element.62), channel_id=1, source_target_pairs={{0,2},{2,0},{4,6},{6,4},{8,10},{10,8},{12,14},{14,12},{16,18},{18,... | collective-permute-start | bytes 3145736 | tf_op jit(solution)/shard_map/ppermute | solution.py:295
  103.1 9.2 %collective-permute-start.13 = (bf16[4,128,256]{2,1,0:T(8,128)(2,1)S(1)}, bf16[4,128,256]{2,1,0:T(8,128)(2,1)S(1)}, u32[]{:S(2)}, u32[]{:S(2)}) collective-permute-start(bf16[4,128,256]{2,1,0:T(8,128)(2,1)S(1)} %get-tuple-element.57), channel_id=1, source_target_pairs={{0,1},{1,0},{2,3},{3,2},{4,5},{5,4},{6,7},{7,6},{8,9},{9,8},{10,11... | collective-permute-start | bytes 786440 | tf_op jit(solution)/shard_map/ppermute | solution.py:331
  104.7 14.8 %collective-permute-start.14 = (bf16[4,128,256]{2,1,0:T(8,128)(2,1)S(1)}, bf16[4,128,256]{2,1,0:T(8,128)(2,1)S(1)}, u32[]{:S(2)}, u32[]{:S(2)}) collective-permute-start(bf16[4,128,256]{2,1,0:T(8,128)(2,1)S(1)} %get-tuple-element.58), channel_id=1, source_target_pairs={{0,4},{1,5},{2,6},{3,7},{4,0},{5,1},{6,2},{7,3},{8,12},{9,13},{10,... | collective-permute-start | bytes 786440 | tf_op jit(solution)/shard_map/ppermute | solution.py:331
  106.2 13.3 %collective-permute-start.15 = (bf16[4,128,256]{2,1,0:T(8,128)(2,1)S(1)}, bf16[4,128,256]{2,1,0:T(8,128)(2,1)S(1)}, u32[]{:S(2)}, u32[]{:S(2)}) collective-permute-start(bf16[4,128,256]{2,1,0:T(8,128)(2,1)S(1)} %get-tuple-element.59), channel_id=1, source_target_pairs={{0,5},{1,4},{2,7},{3,6},{4,1},{5,0},{6,3},{7,2},{8,13},{9,12},{10,... | collective-permute-start | bytes 786440 | tf_op jit(solution)/shard_map/ppermute | solution.py:331
  108.3 17.6 %collective-permute-start.19 = (bf16[4,128,256]{2,1,0:T(8,128)(2,1)S(1)}, bf16[4,128,256]{2,1,0:T(8,128)(2,1)S(1)}, u32[]{:S(2)}, u32[]{:S(2)}) collective-permute-start(bf16[4,128,256]{2,1,0:T(8,128)(2,1)S(1)} %get-tuple-element.64), channel_id=1, source_target_pairs={{0,1},{1,0},{2,3},{3,2},{4,5},{5,4},{6,7},{7,6},{8,9},{9,8},{10,11... | collective-permute-start | bytes 786440 | tf_op jit(solution)/shard_map/ppermute | solution.py:331
  109.8 19.7 %collective-permute-start.20 = (bf16[4,128,256]{2,1,0:T(8,128)(2,1)S(1)}, bf16[4,128,256]{2,1,0:T(8,128)(2,1)S(1)}, u32[]{:S(2)}, u32[]{:S(2)}) collective-permute-start(bf16[4,128,256]{2,1,0:T(8,128)(2,1)S(1)} %get-tuple-element.65), channel_id=1, source_target_pairs={{0,4},{1,5},{2,6},{3,7},{4,0},{5,1},{6,2},{7,3},{8,12},{9,13},{10,... | collective-permute-start | bytes 786440 | tf_op jit(solution)/shard_map/ppermute | solution.py:331
  112.3 17.1 %collective-permute-start.21 = (bf16[4,128,256]{2,1,0:T(8,128)(2,1)S(1)}, bf16[4,128,256]{2,1,0:T(8,128)(2,1)S(1)}, u32[]{:S(2)}, u32[]{:S(2)}) collective-permute-start(bf16[4,128,256]{2,1,0:T(8,128)(2,1)S(1)} %get-tuple-element.66), channel_id=1, source_target_pairs={{0,5},{1,4},{2,7},{3,6},{4,1},{5,0},{6,3},{7,2},{8,13},{9,12},{10,... | collective-permute-start | bytes 786440 | tf_op jit(solution)/shard_map/ppermute | solution.py:331
  122.4 7.6 %collective-permute-start.16 = (bf16[4,128,256]{2,1,0:T(8,128)(2,1)}, bf16[4,128,256]{2,1,0:T(8,128)(2,1)S(1)}, u32[]{:S(2)}, u32[]{:S(2)}) collective-permute-start(bf16[4,128,256]{2,1,0:T(8,128)(2,1)} %total.1.own_ref), channel_id=1, source_target_pairs={{0,8},{2,10},{4,12},{6,14},{8,16},{10,18},{12,20},{14,22},{16,24},... | collective-permute-start | bytes 786440 | tf_op jit(solution)/shard_map/ppermute | solution.py:295
  (15 other events, 226.8 us)

commit v2 on v1

v2 whole, which is shorter than its diff:
```python
import functools
import math

import jax
import jax.numpy as jnp
import ml_dtypes
import numpy as np
from jax import lax
from jax.experimental import pallas as pl
from jax.experimental.pallas import tpu as pltpu
from jax.sharding import PartitionSpec as P

LAGS = 201
ROUNDS = 4
GROUP = 4
PARTS = 2
LANES = 128
F32, BF16 = jnp.float32, jnp.bfloat16


def after(value, *others):
    return lax.optimization_barrier((value, others))[0]


def pair_list():
    pairs = []
    for own in range(GROUP):
        for distance in range(1, ROUNDS + 1):
            far = own - distance
            if far >= 0:
                pairs.append((own, far))
            elif far + GROUP >= 2:
                pairs.append((own, far + GROUP + 2))
            else:
                pairs.append((own + 6, far + GROUP))
    return pairs


def pieces_of(items):
    return sorted({piece for item in items for piece in item})


def whiten_kernel(items, pos_ref, valid_ref, spectra_ref, *refs):
    outs, held = refs[:-1], refs[-1]
    _, tile, windows, freqs = spectra_ref.shape
    parts = freqs // (GROUP * LANES)
    place = (tile, valid_ref.shape[1])
    row = lax.broadcasted_iota(jnp.int32, place, 0) + pl.program_id(0) * tile
    here = row == lax.broadcasted_iota(jnp.int32, place, 1)
    valid = jnp.sum(jnp.where(here, valid_ref[...].astype(F32), 0.0), axis=1, keepdims=True)
    for at, piece in enumerate(pieces_of(items)):
        lanes = pl.ds(pl.multiple_of(((pos_ref[0] ^ piece[0]) * parts + piece[1]) * LANES, LANES), LANES)
        for half in range(2):
            held[at, half] = spectra_ref[half, :, :, lanes].reshape(tile * windows, LANES).astype(F32)
        values = [[held[at, half, pl.ds(w, tile, stride=windows), :] for half in range(2)] for w in range(windows)]
        power = values[0][0] * values[0][0] + values[0][1] * values[0][1]
        for real, imag in values[1:]:
            power = power + (real * real + imag * imag)
        scale = valid / jnp.maximum(jnp.sqrt(power * (1.0 / windows)), 0.5)
        for w in range(windows):
            both = jnp.concatenate([values[w][half] * scale for half in range(2)], axis=1).astype(BF16)
            for item, out in zip(items, outs):
                for index, wanted in enumerate(item):
                    if wanted == piece:
                        out[index, w] = both


def whiten(spectra, valid, pos, items):
    _, channels, windows, freqs = spectra.shape
    tile = min(64, channels)
    count = len(pieces_of(items))
    in_specs = [
        pl.BlockSpec((1, channels), lambda i, pos: (0, 0)),
        pl.BlockSpec((2, tile, windows, freqs), lambda i, pos: (0, i, 0, 0)),
    ]
    out_specs = [pl.BlockSpec((len(item), windows, tile, 2 * LANES), lambda i, pos: (0, 0, i, 0)) for item in items]
    return pl.pallas_call(
        functools.partial(whiten_kernel, items),
        grid_spec=pltpu.PrefetchScalarGridSpec(
            num_scalar_prefetch=1,
            grid=(channels // tile,),
            in_specs=in_specs,
            out_specs=out_specs,
            scratch_shapes=[pltpu.VMEM((count, 2, tile * windows, LANES), F32)],
        ),
        out_shape=[jax.ShapeDtypeStruct((len(item), windows, channels, 2 * LANES), BF16) for item in items],
        compiler_params=pltpu.CompilerParams(vmem_limit_bytes=56 << 20),
        cost_estimate=pl.CostEstimate(flops=0, bytes_accessed=1000, transcendentals=0),
        name="whiten",
    )(pos, valid, spectra)


def correlate_kernel(pairs, places, part, pos_ref, *refs):
    count = 2 * GROUP
    blocks, before = refs[:count], refs[count:-16]
    fwd_in, lag_in, inv_in, keep_out, send_out = refs[-16:-11]
    held, held_before, fwd_ref, lag_ref, inv_ref, hat, plus, cross, turned, result, sem = refs[-11:]
    member = pos_ref[0]
    half = fwd_ref.shape[0] // 2
    windows = held.shape[1]

    def load(index, source, target):
        copy = pltpu.make_async_copy(source, target, sem.at[index])
        copy.start()
        return copy

    loads = [load(count, fwd_in, fwd_ref)]
    loads += [load(index, blocks[index].at[places[index]], held.at[index]) for index in range(count)]
    later = [
        load(count + 1, inv_in, inv_ref),
        load(count + 2, lag_in.at[(pos_ref[1] * GROUP + member) * PARTS + part], lag_ref),
    ]
    later += [load(count + 3 + index, source, held_before.at[index]) for index, source in enumerate(before)]
    loads[0].wait()
    for index in range(count):
        slot = member ^ (index % GROUP)
        if index >= GROUP:
            slot = jnp.where(slot < 2, slot + 6, slot + 2)
        loads[1 + index].wait()
        for w in range(windows):
            terms = jnp.dot(fwd_ref[...], held[index, w], preferred_element_type=F32)
            cos_r, cos_i = terms[:half, :LANES], terms[:half, LANES:]
            sin_r, sin_i = terms[half:, :LANES], terms[half:, LANES:]
            hat[slot, w, 0] = cos_r + sin_i
            hat[slot, w, 1] = cos_i - sin_r
            hat[slot, w, 2] = cos_r - sin_i
            hat[slot, w, 3] = cos_i + sin_r

    def products(step, carry):
        rows = pl.ds(pl.multiple_of(step * 8, 8), 8)
        odd_rows = pl.ds(pl.multiple_of(half + step * 8, 8), 8)
        for sign in range(2):
            sums = [None] * (2 * len(pairs))
            for win in range(windows):
                real = [hat[slot, win, 2 * sign, rows, :] for slot in range(count)]
                imag = [hat[slot, win, 2 * sign + 1, rows, :] for slot in range(count)]
                for n, (own, far) in enumerate(pairs):
                    part_r = real[own] * real[far] + imag[own] * imag[far]
                    part_i = imag[own] * real[far] - real[own] * imag[far]
                    sums[2 * n] = part_r if win == 0 else sums[2 * n] + part_r
                    sums[2 * n + 1] = part_i if win == 0 else sums[2 * n + 1] + part_i
            for n in range(len(pairs)):
                if sign == 0:
                    plus[2 * n], plus[2 * n + 1] = sums[2 * n], sums[2 * n + 1]
                else:
                    plus_r, plus_i = plus[2 * n], plus[2 * n + 1]
                    minus_r, minus_i = sums[2 * n], sums[2 * n + 1]
                    cross[n, rows, :LANES] = plus_r + minus_r
                    cross[n, rows, LANES:] = plus_i + minus_i
                    cross[n, odd_rows, :LANES] = plus_i - minus_i
                    cross[n, odd_rows, LANES:] = minus_r - plus_r
        return carry

    lax.fori_loop(0, half // 8, products, 0)
    for copy in later:
        copy.wait()

    def turn(n, carry):
        turned[n] = jnp.dot(inv_ref[...], cross[n].astype(BF16), preferred_element_type=F32).astype(BF16)
        return carry

    lax.fori_loop(0, len(pairs), turn, 0, unroll=8)
    stores = []
    for flip in (1, 3, 0, 2):
        for distance in range(ROUNDS):
            n = (member ^ flip) * ROUNDS + distance
            total = lax.dot_general(lag_ref[...], turned[n], (((1,), (1,)), ((), ())), preferred_element_type=F32)
            if before:
                total = total + held_before[flip % 2, flip // 2, distance].astype(F32)
            result[flip, distance] = total.astype(BF16)
        out = (keep_out, send_out)[flip % 2].at[flip // 2]
        stores.append(pltpu.make_async_copy(result.at[flip], out, sem.at[count + 5 + flip]))
        stores[-1].start()
    for copy in stores:
        copy.wait()


def correlate(pos, part, blocks, tables, before=()):
    fwd, lag, inv = tables
    _, windows, channels, lanes = blocks[0][0].shape
    rows = lag.shape[1]
    pairs = pair_list()
    half = fwd.shape[0] // 2
    places = [place for _, place in blocks]
    shape = (2, ROUNDS, rows, channels)
    anywhere = pl.BlockSpec(memory_space=pl.ANY)
    return pl.pallas_call(
        functools.partial(correlate_kernel, pairs, places, part),
        in_specs=[pl.BlockSpec(memory_space=pltpu.SMEM)] + [anywhere] * (len(blocks) + len(before) + 3),
        out_specs=[anywhere, anywhere],
        scratch_shapes=[
            pltpu.VMEM((2 * GROUP, windows, channels, lanes), BF16),
            pltpu.VMEM((2, *shape), BF16),
            pltpu.VMEM(fwd.shape, BF16),
            pltpu.VMEM(lag.shape[1:], BF16),
            pltpu.VMEM(inv.shape, BF16),
            pltpu.VMEM((2 * GROUP, windows, 4, half, LANES), F32),
            pltpu.VMEM((2 * len(pairs), 8, LANES), F32),
            pltpu.VMEM((len(pairs), 2 * half, 2 * LANES), F32),
            pltpu.VMEM((len(pairs), channels, 2 * LANES), BF16),
            pltpu.VMEM((GROUP, *shape[1:]), BF16),
            pltpu.SemaphoreType.DMA((2 * GROUP + 9,)),
        ],
        out_shape=[jax.ShapeDtypeStruct(shape, BF16)] * 2,
        compiler_params=pltpu.CompilerParams(vmem_limit_bytes=60 << 20),
        cost_estimate=pl.CostEstimate(flops=0, bytes_accessed=1000, transcendentals=0),
        name="correlate",
    )(pos, *[array for array, _ in blocks], *before, fwd, lag, inv)


def halves_kernel(pos_ref, *refs):
    for index in range(4):
        keep, came, out = refs[index], refs[4 + index], refs[8 + index]
        out[...] = (keep[0].astype(F32) + came[0].astype(F32)).astype(out.dtype)


def halves(pos, keep, came):
    _, rounds, rows, channels = keep.shape
    width = channels // 2
    specs = [
        pl.BlockSpec((1, rounds, rows, width), lambda i, pos, f=f, g=g: (f, 0, 0, pos[1] ^ g))
        for f in range(2)
        for g in range(2)
    ]
    out_spec = pl.BlockSpec((rounds, rows, width), lambda i, pos: (0, 0, 0))
    return pl.pallas_call(
        halves_kernel,
        grid_spec=pltpu.PrefetchScalarGridSpec(
            num_scalar_prefetch=1, grid=(1,), in_specs=specs * 2, out_specs=[out_spec] * 4
        ),
        out_shape=[jax.ShapeDtypeStruct((rounds, rows, width), t) for t in (F32, BF16, BF16, BF16)],
        compiler_params=pltpu.CompilerParams(vmem_limit_bytes=16 << 20),
        name="halves",
    )(pos, *([keep] * 4), *([came] * 4))


def total_kernel(*refs):
    *terms, out, back = refs
    for distance in range(ROUNDS):
        result = terms[0][distance].astype(F32)
        for term in terms[1:]:
            result = result + term[distance].astype(F32)
        out[distance] = result
        if distance >= 2:
            back[distance - 2] = result.astype(BF16)


def total(*terms):
    shape = terms[0].shape
    return pl.pallas_call(
        total_kernel,
        out_shape=[jax.ShapeDtypeStruct(shape, F32), jax.ShapeDtypeStruct((2, *shape[1:]), BF16)],
        compiler_params=pltpu.CompilerParams(vmem_limit_bytes=16 << 20),
        name="total",
    )(*terms)


def finish_kernel(normalizer, pos_ref, own_ref, behind_ref, out):
    member = pos_ref[0]
    for distance in range(ROUNDS):
        result = own_ref[distance]
        if distance >= 2:
            result = jnp.where(distance < member + 2, result, behind_ref[distance - 2].astype(F32))
        out[:, distance, :] = (result * normalizer)[:LAGS]


def finish(pos, own, behind, normalizer):
    return pl.pallas_call(
        functools.partial(finish_kernel, normalizer),
        in_specs=[pl.BlockSpec(memory_space=pltpu.SMEM)] + [pl.BlockSpec(memory_space=pltpu.VMEM)] * 2,
        out_shape=jax.ShapeDtypeStruct((LAGS, ROUNDS, own.shape[2]), F32),
        compiler_params=pltpu.CompilerParams(vmem_limit_bytes=16 << 20),
        name="finish",
    )(pos, own, behind)


def make_tables(channels, freq_total, freq_local):
    half = 3 * channels // 4
    wave = 2 * np.arange(half) + 1
    period = 4 * half
    fwd_angle = 2.0 * np.pi / period * ((wave[:, None] * np.arange(channels)[None, :]) % period)
    fwd = np.concatenate([np.cos(fwd_angle), np.sin(fwd_angle)], axis=0)
    inv_angle = 2.0 * np.pi / period * ((wave[:, None] * (np.arange(channels) - channels // 2)[None, :]) % period)
    inv = np.concatenate([np.cos(inv_angle), -np.sin(inv_angle)], axis=0).T
    rows = -(-LAGS // 16) * 16
    bins = freq_local // (GROUP * PARTS)
    tau = np.arange(LAGS) - (LAGS - 1) // 2
    lag_angle = np.pi / freq_total * ((tau[:, None] * np.arange(freq_total)[None, :]) % (2 * freq_total))
    lag_angle = lag_angle.reshape(LAGS, freq_total // bins, bins).transpose(1, 0, 2)
    lag = np.zeros((freq_total // bins, rows, 2 * LANES), np.float64)
    lag[:, :LAGS, :bins] = np.cos(lag_angle)
    lag[:, :LAGS, LANES : LANES + bins] = -np.sin(lag_angle)
    return tuple(table.astype(ml_dtypes.bfloat16) for table in (fwd, lag, inv))


def on_device(n_frq, spectra, channel_valid):
    _, channels, windows, freq_local = spectra.shape
    n_blk = lax.axis_size("blk")
    freq_total = freq_local * n_frq
    fwd, lag, inv = make_tables(channels, freq_total, freq_local)
    tables = (jnp.asarray(fwd), jnp.asarray(lag), jnp.asarray(inv))
    normalizer = 1.0 / math.sqrt(windows * channels * freq_total) / (3 * channels // 2)
    member = lax.rem(lax.axis_index("blk"), GROUP)
    side = lax.axis_index("frq")
    pos = jnp.stack([member, side]).astype(jnp.int32)
    valid = channel_valid[None, :]
    bins = freq_local // (GROUP * PARTS)
    if bins != LANES:
        split = spectra.reshape(2, channels, windows, GROUP * PARTS, bins)
        split = jnp.pad(split, ((0, 0),) * 4 + ((0, LANES - bins),))
        spectra = split.reshape(2, channels, windows, GROUP * PARTS * LANES)

    def move(value, target):
        pairs = [(i, target(i)) for i in range(n_blk) if 0 <= target(i) < n_blk]
        return lax.ppermute(value, "blk", pairs)

    def swap(value, flip):
        return move(value, lambda i: i ^ flip)

    def up(i):
        return i % GROUP >= 2

    def forward(value):
        return move(value, lambda i: i - GROUP if up(i) else i + GROUP)

    def near(value, flip):
        return move(value, lambda i: (i ^ flip) + (GROUP if up(i) else -GROUP))

    y02, y03, y12, y13, core, core0, core1, own0, own1 = whiten(
        spectra,
        valid,
        pos,
        [[(2, 0)], [(3, 0)], [(2, 1)], [(3, 1)], [(1, 0), (1, 1)], [(1, 0)], [(1, 1)], [(0, 0)], [(0, 1)]],
    )
    y02_came = swap(y02, 2)
    y03_came = swap(y03, 3)
    core_came = swap(core, 1)
    near00 = near(own0, 0)
    near01 = near(core0, 1)
    y12_came = swap(after(y12, y02_came, core_came), 2)
    far02 = forward(after(y02_came, core_came))
    near10 = near(after(own1, near00), 0)
    y13_came = swap(after(y13, y03_came, near00), 3)
    far03 = forward(after(y03_came, near00, far02))
    near11 = near(after(core1, near01), 1)
    far12 = forward(after(y12_came, far02))
    far13 = forward(after(y13_came, far03))

    blocks0 = [(own0, 0), (core_came, 0), (y02_came, 0), (y03_came, 0), (near00, 0), (near01, 0), (far02, 0), (far03, 0)]
    blocks1 = [(own1, 0), (core_came, 1), (y12_came, 0), (y13_came, 0), (near10, 0), (near11, 0), (far12, 0), (far13, 0)]
    partial = correlate(after(pos, y13_came), 0, blocks0, tables)
    keep, send = correlate(pos, 1, blocks1, tables, partial)
    came = swap(send, 1)

    if n_frq == 2:

        def both(value, flip, cross):
            flat = [(i, x) for i in range(n_blk) for x in range(2)]
            pairs = [(2 * i + x, 2 * (i ^ flip) + (x ^ cross)) for i, x in flat]
            return lax.ppermute(value, ("blk", "frq"), pairs)

        mine, other, far_mine, far_other = halves(pos, keep, came)
        terms = [mine, both(other, 0, 1), both(far_mine, 2, 0), both(far_other, 2, 1)]
    else:
        both = keep.astype(F32) + came.astype(F32)
        both = both[0] + swap(both[1].astype(BF16), 2).astype(F32)
        terms = [lax.psum_scatter(both, "frq", scatter_dimension=2, tiled=True)]
    result, back = total(*terms)
    behind = move(back, lambda i: n_blk if up(i) else i + GROUP)
    stacked = finish(pos, result, behind, normalizer)
    return jnp.transpose(stacked, (1, 0, 2))[None]


def solution(mesh):
    return jax.shard_map(
        functools.partial(on_device, mesh.shape["frq"]),
        mesh=mesh,
        in_specs=(P(None, "blk", None, "frq"), P("blk")),
        out_specs=P("blk", None, None, "frq"),
        check_vma=False,
    )
```

time: 134 us -> 116 us (0.87)
  Pallas kernels: 47.8 us -> 33.9 us
  starting transfers between devices: 39.2 us -> 35.4 us
    pallas_call x5 -> x4, Pallas kernels: 43.7 us -> 31.2 us  [the longest x2 23.9 us: correlate(): pl.pallas_call(functools.partial(correlate_kernel, pairs, places, part),...]
    ppermute x6 -> x3, starting transfers between devices: 9.02 us -> 3.55 us  [both(): return lax.ppermute(value, ('blk', 'frq'), pairs)]
    ppermute x16 -> x15, starting transfers between devices: 30.1 us -> 31.8 us  [move(): return lax.ppermute(value, 'blk', pairs)]
    ppermute x16 -> x15, waiting for transfers between devices: 32.7 us -> 32.4 us  [move(): return lax.ppermute(value, 'blk', pairs)]
    ppermute x6 -> x3, waiting for transfers between devices: 9.42 us -> 9.61 us  [both(): return lax.ppermute(value, ('blk', 'frq'), pairs)]
    unnamed x34 -> x28, local copies, waits for them, and re-layouts: 3.37 us -> 3.19 us
  transfers between devices with their start and end apart: 22 -> 18, of which waited for: 10 -> 9; matrix products, arithmetic and copies ran while one was open for 0% -> 0% of each run, Pallas kernels for 26% -> 10%
where the time goes in v2:
time: 116 us; the launch traced here: 115 us
  waiting for transfers between devices  42 us (36%)
  starting transfers between devices  35.4 us (31%)
  Pallas kernels  33.9 us (29%)
  local copies, waits for them, and re-layouts  3.19 us (3%)
    ppermute x15, waiting for transfers between devices, move(): return lax.ppermute(value, 'blk', pairs)  32.4 us
    ppermute x15, starting transfers between devices, move(): return lax.ppermute(value, 'blk', pairs)  31.8 us
    pallas_call x2, Pallas kernels, correlate(): pl.pallas_call(functools.partial(correlate_kernel, pairs, places, part),...  23.9 us
    ppermute x3, waiting for transfers between devices, both(): return lax.ppermute(value, ('blk', 'frq'), pairs)  9.61 us
    pallas_call x1, Pallas kernels, whiten(): pl.pallas_call(functools.partial(whiten_kernel, items), grid_spec=pltpu.P...  7.23 us
    ppermute x3, starting transfers between devices, both(): return lax.ppermute(value, ('blk', 'frq'), pairs)  3.55 us
    unnamed x28, local copies, waits for them, and re-layouts  3.19 us
  transfers between devices with their start and end apart: 18, of which 9 were waited for; matrix products, arithmetic and copies ran while one was open for 0% of the time, Pallas kernels for 10%

profile of v2, /device:TPU:0, one launch (start us, length us, event | category | flops | bytes accessed | tf_op | source)
XLA Modules:
  0.0 115.3 jit_solution(3451922967487713037)
XLA Ops:
  0.6 7.2 %whiten.1 = (bf16[1,4,256,256]{3,2,1,0:T(8,128)(2,1)}, bf16[1,4,256,256]{3,2,1,0:T(8,128)(2,1)}, bf16[1,4,256,256]{3,2,1,0:T(8,128)(2,1)}, bf16[1,4,256,256]{3,2...) custom-call(s32[2]{0:T(128)} %pad_add_fusion.pos_ref, ...), custom_call_target="tpu_custom_call" | custom-call | bytes 1000 | tf_op jit(solution)/shard_map/whiten/pallas_call | solution.py:77
  8.4 2.6 %collective-permute-start.1 = (bf16[1,4,256,256]{3,2,1,0:T(8,128)(2,1)}, bf16[1,4,256,256]{3,2,1,0:T(8,128)(2,1)S(1)}, u32[]{:S(2)}, u32[]{:S(2)}) collective-permute-start(bf16[1,4,256,256]{3,2,1,0:T(8,128)(2,1)} %get-tuple-element.36), channel_id=1, source_target_pairs={{0,4},{2,6},{4,0},{6,2},{8,12},{10,14},{12,8},{14,10},{16,20},{18,... | collective-permute-start | bytes 1572872 | tf_op jit(solution)/shard_map/ppermute | solution.py:315
  12.2 2.3 %collective-permute-start.3 = (bf16[1,4,256,256]{3,2,1,0:T(8,128)(2,1)}, bf16[1,4,256,256]{3,2,1,0:T(8,128)(2,1)S(1)}, u32[]{:S(2)}, u32[]{:S(2)}) collective-permute-start(bf16[1,4,256,256]{3,2,1,0:T(8,128)(2,1)} %get-tuple-element.39), channel_id=1, source_target_pairs={{0,6},{2,4},{4,2},{6,0},{8,14},{10,12},{12,10},{14,8},{16,22},{18,... | collective-permute-start | bytes 1572872 | tf_op jit(solution)/shard_map/ppermute | solution.py:315
  14.5 9.4 %collective-permute-done.1.refs_2_ = bf16[1,4,256,256]{3,2,1,0:T(8,128)(2,1)S(1)} collective-permute-done((bf16[1,4,256,256]{3,2,1,0:T(8,128)(2,1)}, bf16[1,4,256,256]{3,2,1,0:T(8,128)(2,1)S(1)}, u32[]{:S(2)}, u32[]{:S(2)}) %collective-permute-start.1) | collective-permute-done | bytes 524320 | tf_op jit(solution)/shard_map/ppermute | solution.py:315
  23.9 3.9 %collective-permute-start.9 = (bf16[1,4,256,256]{3,2,1,0:T(8,128)(2,1)S(1)}, bf16[1,4,256,256]{3,2,1,0:T(8,128)(2,1)S(1)}, u32[]{:S(2)}, u32[]{:S(2)}) collective-permute-start(bf16[1,4,256,256]{3,2,1,0:T(8,128)(2,1)S(1)} %collective-permute-done.1.refs_2_), channel_id=1, source_target_pairs={{0,8},{2,10},{8,16},{10,18},{12,4},{14,6},{16,24},{18,26},{20,12},... | collective-permute-start | bytes 1572872 | tf_op jit(solution)/shard_map/ppermute | solution.py:315
  27.9 1.3 %collective-permute-start.7 = (bf16[1,4,256,256]{3,2,1,0:T(8,128)(2,1)}, bf16[1,4,256,256]{3,2,1,0:T(8,128)(2,1)S(1)}, u32[]{:S(2)}, u32[]{:S(2)}) collective-permute-start(bf16[1,4,256,256]{3,2,1,0:T(8,128)(2,1)} %get-tuple-element.44), channel_id=1, source_target_pairs={{4,14},{6,12},{8,2},{10,0},{12,22},{14,20},{16,10},{18,8},{20,30},... | collective-permute-start | bytes 1572872 | tf_op jit(solution)/shard_map/ppermute | solution.py:315
  29.2 5.4 %collective-permute-done.3.refs_3_ = bf16[1,4,256,256]{3,2,1,0:T(8,128)(2,1)S(1)} collective-permute-done((bf16[1,4,256,256]{3,2,1,0:T(8,128)(2,1)}, bf16[1,4,256,256]{3,2,1,0:T(8,128)(2,1)S(1)}, u32[]{:S(2)}, u32[]{:S(2)}) %collective-permute-start.3) | collective-permute-done | bytes 524320 | tf_op jit(solution)/shard_map/ppermute | solution.py:315
  34.7 1.6 %collective-permute-start.2 = (bf16[1,4,256,256]{3,2,1,0:T(8,128)(2,1)}, bf16[1,4,256,256]{3,2,1,0:T(8,128)(2,1)S(1)}, u32[]{:S(2)}, u32[]{:S(2)}) collective-permute-start(bf16[1,4,256,256]{3,2,1,0:T(8,128)(2,1)} %get-tuple-element.37), channel_id=1, source_target_pairs={{0,4},{2,6},{4,0},{6,2},{8,12},{10,14},{12,8},{14,10},{16,20},{18,... | collective-permute-start | bytes 1572872 | tf_op jit(solution)/shard_map/ppermute | solution.py:315
  36.4 2.0 %collective-permute-done.9.refs_6_ = bf16[1,4,256,256]{3,2,1,0:T(8,128)(2,1)S(1)} collective-permute-done((bf16[1,4,256,256]{3,2,1,0:T(8,128)(2,1)S(1)}, bf16[1,4,256,256]{3,2,1,0:T(8,128)(2,1)S(1)}, u32[]{:S(2)}, u32[]{:S(2)}) %collective-permute-start.9) | collective-permute-done | bytes 524320 | tf_op jit(solution)/shard_map/ppermute | solution.py:315
  38.4 4.4 %collective-permute-start.11 = (bf16[1,4,256,256]{3,2,1,0:T(8,128)(2,1)S(1)}, bf16[1,4,256,256]{3,2,1,0:T(8,128)(2,1)S(1)}, u32[]{:S(2)}, u32[]{:S(2)}) collective-permute-start(bf16[1,4,256,256]{3,2,1,0:T(8,128)(2,1)S(1)} %collective-permute-done.3.refs_3_), channel_id=1, source_target_pairs={{0,8},{2,10},{8,16},{10,18},{12,4},{14,6},{16,24},{18,26},{20,12},... | collective-permute-start | bytes 1572872 | tf_op jit(solution)/shard_map/ppermute | solution.py:315
  45.4 4.2 %collective-permute-done.2.refs_2_ = bf16[1,4,256,256]{3,2,1,0:T(8,128)(2,1)S(1)} collective-permute-done((bf16[1,4,256,256]{3,2,1,0:T(8,128)(2,1)}, bf16[1,4,256,256]{3,2,1,0:T(8,128)(2,1)S(1)}, u32[]{:S(2)}, u32[]{:S(2)}) %collective-permute-start.2) | collective-permute-done | bytes 524320 | tf_op jit(solution)/shard_map/ppermute | solution.py:315
  49.6 3.5 %collective-permute-start.10 = (bf16[1,4,256,256]{3,2,1,0:T(8,128)(2,1)S(1)}, bf16[1,4,256,256]{3,2,1,0:T(8,128)(2,1)S(1)}, u32[]{:S(2)}, u32[]{:S(2)}) collective-permute-start(bf16[1,4,256,256]{3,2,1,0:T(8,128)(2,1)S(1)} %collective-permute-done.2.refs_2_), channel_id=1, source_target_pairs={{0,8},{2,10},{8,16},{10,18},{12,4},{14,6},{16,24},{18,26},{20,12},... | collective-permute-start | bytes 1572872 | tf_op jit(solution)/shard_map/ppermute | solution.py:315
  53.1 6.6 %collective-permute-done.5.refs_3_ = bf16[1,4,256,256]{3,2,1,0:T(8,128)(2,1)S(1)} collective-permute-done((bf16[1,4,256,256]{3,2,1,0:T(8,128)(2,1)}, bf16[1,4,256,256]{3,2,1,0:T(8,128)(2,1)S(1)}, u32[]{:S(2)}, u32[]{:S(2)}) %collective-permute-start.5) | collective-permute-done | bytes 524320 | tf_op jit(solution)/shard_map/ppermute | solution.py:315
  60.8 4.7 %collective-permute-start.12 = (bf16[1,4,256,256]{3,2,1,0:T(8,128)(2,1)S(1)}, bf16[1,4,256,256]{3,2,1,0:T(8,128)(2,1)}, u32[]{:S(2)}, u32[]{:S(2)}) collective-permute-start(bf16[1,4,256,256]{3,2,1,0:T(8,128)(2,1)S(1)} %collective-permute-done.5.refs_3_), channel_id=1, source_target_pairs={{0,8},{2,10},{8,16},{10,18},{12,4},{14,6},{16,24},{18,26},{20,12},... | collective-permute-start | bytes 1572872 | tf_op jit(solution)/shard_map/ppermute | solution.py:315
  65.5 11.8 %correlate.2 = (bf16[2,4,208,256]{3,2,1,0:T(8,128)(2,1)}, bf16[2,4,208,256]{3,2,1,0:T(8,128)(2,1)}) custom-call(s32[2]{0:T(128)} %pad_add_fusion.pos_ref, bf16[1,4,256,256]{3,2,1,0:T(8,128)(2,1)} %get-tuple-element.40.refs_0_, bf16[2,4,256,256]{3,2,1,0:T(8,128)(2,1)} %copy-done.2, bf16[1,4,256,256]{3,2,1,0:T(8,128)(2,1)} %copy-done.8, ...), custom_call_target="tpu_custom_call" | custom-call | bytes 1000 | tf_op jit(solution)/shard_map/correlate/pallas_call | solution.py:187
  78.5 12.0 %correlate.3 = (bf16[2,4,208,256]{3,2,1,0:T(8,128)(2,1)}, bf16[2,4,208,256]{3,2,1,0:T(8,128)(2,1)}) custom-call(s32[2]{0:T(128)} %pad_add_fusion.pos_ref, bf16[1,4,256,256]{3,2,1,0:T(8,128)(2,1)} %get-tuple-element.42.refs_0_, bf16[2,4,256,256]{3,2,1,0:T(8,128)(2,1)} %copy-done.2, bf16[1,4,256,256]{3,2,1,0:T(8,128)(2,1)} %copy-done.3, ...), custom_call_target="tpu_custom_call" | custom-call | bytes 1000 | tf_op jit(solution)/shard_map/correlate/pallas_call | solution.py:187
  90.8 2.4 %collective-permute-done.13.refs_4_.refs_5_.refs_6_.refs_7_ = bf16[2,4,208,256]{3,2,1,0:T(8,128)(2,1)S(1)} collective-permute-done((bf16[2,4,208,256]{3,2,1,0:T(8,128)(2,1)}, bf16[2,4,208,256]{3,2,1,0:T(8,128)(2,1)S(1)}, u32[]{:S(2)}, u32[]{:S(2)}) %collective-permute-start.13) | collective-permute-done | bytes 852000 | tf_op jit(solution)/shard_map/ppermute | solution.py:315
  95.5 1.6 %collective-permute-start.14 = (bf16[4,208,128]{2,1,0:T(8,128)(2,1)S(1)}, bf16[4,208,128]{2,1,0:T(8,128)(2,1)S(1)}, u32[]{:S(2)}, u32[]{:S(2)}) collective-permute-start(bf16[4,208,128]{2,1,0:T(8,128)(2,1)S(1)} %get-tuple-element.56), channel_id=1, source_target_pairs={{0,1},{1,0},{2,3},{3,2},{4,5},{5,4},{6,7},{7,6},{8,9},{9,8},{10,11... | collective-permute-start | bytes 638984 | tf_op jit(solution)/shard_map/ppermute | solution.py:360
  97.5 1.6 %collective-permute-start.16 = (bf16[4,208,128]{2,1,0:T(8,128)(2,1)S(1)}, bf16[4,208,128]{2,1,0:T(8,128)(2,1)S(1)}, u32[]{:S(2)}, u32[]{:S(2)}) collective-permute-start(bf16[4,208,128]{2,1,0:T(8,128)(2,1)S(1)} %get-tuple-element.58), channel_id=1, source_target_pairs={{0,5},{1,4},{2,7},{3,6},{4,1},{5,0},{6,3},{7,2},{8,13},{9,12},{10,... | collective-permute-start | bytes 638984 | tf_op jit(solution)/shard_map/ppermute | solution.py:360
  99.1 4.6 %collective-permute-done.14.refs_1_ = bf16[4,208,128]{2,1,0:T(8,128)(2,1)S(1)} collective-permute-done((bf16[4,208,128]{2,1,0:T(8,128)(2,1)S(1)}, bf16[4,208,128]{2,1,0:T(8,128)(2,1)S(1)}, u32[]{:S(2)}, u32[]{:S(2)}) %collective-permute-start.14) | collective-permute-done | bytes 213024 | tf_op jit(solution)/shard_map/ppermute | solution.py:360
  103.7 5.0 %collective-permute-done.15.refs_2_ = bf16[4,208,128]{2,1,0:T(8,128)(2,1)S(1)} collective-permute-done((bf16[4,208,128]{2,1,0:T(8,128)(2,1)S(1)}, bf16[4,208,128]{2,1,0:T(8,128)(2,1)S(1)}, u32[]{:S(2)}, u32[]{:S(2)}) %collective-permute-start.15) | collective-permute-done | bytes 213024 | tf_op jit(solution)/shard_map/ppermute | solution.py:360
  108.8 2.7 %collective-permute-start.17 = (bf16[2,208,128]{2,1,0:T(8,128)(2,1)S(1)}, bf16[2,208,128]{2,1,0:T(8,128)(2,1)S(1)}, u32[]{:S(2)}, u32[]{:S(2)}) collective-permute-start(bf16[2,208,128]{2,1,0:T(8,128)(2,1)S(1)} %get-tuple-element.60), channel_id=1, source_target_pairs={{0,8},{2,10},{8,16},{10,18},{16,24},{18,26},{1,9},{3,11},{9,17},{1... | collective-permute-start | bytes 319496 | tf_op jit(solution)/shard_map/ppermute | solution.py:315
  111.5 2.3 %collective-permute-done.17.behind_ref = bf16[2,208,128]{2,1,0:T(8,128)(2,1)S(1)} collective-permute-done((bf16[2,208,128]{2,1,0:T(8,128)(2,1)S(1)}, bf16[2,208,128]{2,1,0:T(8,128)(2,1)S(1)}, u32[]{:S(2)}, u32[]{:S(2)}) %collective-permute-start.17) | collective-permute-done | bytes 106528 | tf_op jit(solution)/shard_map/ppermute | solution.py:315
  113.8 1.5 %finish.1 = f32[201,4,128]{2,1,0:T(4,128)} custom-call(s32[2]{0:T(128)S(1)} %copy-done.1, f32[4,208,128]{2,1,0:T(8,128)S(1)} %get-tuple-element.59.own_ref, bf16[2,208,128]{2,1,0:T(8,128)(2,1)S(1)} %collective-permute-done.17.behind_ref), custom_call_target="tpu_custom_call" | custom-call | tf_op jit(solution)/shard_map/finish/pallas_call | solution.py:268
  (47 shorter events, 10.4 us)
Async XLA Ops:
  7.9 16.1 %collective-permute-start = (bf16[2,4,256,256]{3,2,1,0:T(8,128)(2,1)}, bf16[2,4,256,256]{3,2,1,0:T(8,128)(2,1)S(1)}, u32[]{:S(2)}, u32[]{:S(2)}) collective-permute-start(bf16[2,4,256,256]{3,2,1,0:T(8,128)(2,1)} %get-tuple-element.34), channel_id=1, source_target_pairs={{0,2},{2,0},{4,6},{6,4},{8,10},{10,8},{12,14},{14,12},{16,18},{18,... | collective-permute-start | bytes 3145736 | tf_op jit(solution)/shard_map/ppermute | solution.py:315
  8.4 15.6 %collective-permute-start.1 = (bf16[1,4,256,256]{3,2,1,0:T(8,128)(2,1)}, bf16[1,4,256,256]{3,2,1,0:T(8,128)(2,1)S(1)}, u32[]{:S(2)}, u32[]{:S(2)}) collective-permute-start(bf16[1,4,256,256]{3,2,1,0:T(8,128)(2,1)} %get-tuple-element.36), channel_id=1, source_target_pairs={{0,4},{2,6},{4,0},{6,2},{8,12},{10,14},{12,8},{14,10},{16,20},{18,... | collective-permute-start | bytes 1572872 | tf_op jit(solution)/shard_map/ppermute | solution.py:315
  11.0 18.2 %collective-permute-start.4 = (bf16[1,4,256,256]{3,2,1,0:T(8,128)(2,1)}, bf16[1,4,256,256]{3,2,1,0:T(8,128)(2,1)S(1)}, u32[]{:S(2)}, u32[]{:S(2)}) collective-permute-start(bf16[1,4,256,256]{3,2,1,0:T(8,128)(2,1)} %get-tuple-element.40.refs_0_), channel_id=1, source_target_pairs={{4,12},{6,14},{8,0},{10,2},{12,20},{14,22},{16,8},{18,10},{20,28},... | collective-permute-start | bytes 1572872 | tf_op jit(solution)/shard_map/ppermute | solution.py:315
  12.2 22.4 %collective-permute-start.3 = (bf16[1,4,256,256]{3,2,1,0:T(8,128)(2,1)}, bf16[1,4,256,256]{3,2,1,0:T(8,128)(2,1)S(1)}, u32[]{:S(2)}, u32[]{:S(2)}) collective-permute-start(bf16[1,4,256,256]{3,2,1,0:T(8,128)(2,1)} %get-tuple-element.39), channel_id=1, source_target_pairs={{0,6},{2,4},{4,2},{6,0},{8,14},{10,12},{12,10},{14,8},{16,22},{18,... | collective-permute-start | bytes 1572872 | tf_op jit(solution)/shard_map/ppermute | solution.py:315
  23.9 35.8 %copy-start.8 = (bf16[1,4,256,256]{3,2,1,0:T(8,128)(2,1)}, bf16[1,4,256,256]{3,2,1,0:T(8,128)(2,1)S(1)}, u32[]{:S(2)}) copy-start(bf16[1,4,256,256]{3,2,1,0:T(8,128)(2,1)S(1)} %collective-permute-done.1.refs_2_) | copy-start | bytes 1572868
  23.9 41.5 %copy-start.2 = (bf16[2,4,256,256]{3,2,1,0:T(8,128)(2,1)}, bf16[2,4,256,256]{3,2,1,0:T(8,128)(2,1)S(1)}, u32[]{:S(2)}) copy-start(bf16[2,4,256,256]{3,2,1,0:T(8,128)(2,1)S(1)} %collective-permute-done.refs_1_) | copy-start | bytes 3145732
  23.9 14.5 %collective-permute-start.9 = (bf16[1,4,256,256]{3,2,1,0:T(8,128)(2,1)S(1)}, bf16[1,4,256,256]{3,2,1,0:T(8,128)(2,1)S(1)}, u32[]{:S(2)}, u32[]{:S(2)}) collective-permute-start(bf16[1,4,256,256]{3,2,1,0:T(8,128)(2,1)S(1)} %collective-permute-done.1.refs_2_), channel_id=1, source_target_pairs={{0,8},{2,10},{8,16},{10,18},{12,4},{14,6},{16,24},{18,26},{20,12},... | collective-permute-start | bytes 1572872 | tf_op jit(solution)/shard_map/ppermute | solution.py:315
  27.9 16.2 %collective-permute-start.7 = (bf16[1,4,256,256]{3,2,1,0:T(8,128)(2,1)}, bf16[1,4,256,256]{3,2,1,0:T(8,128)(2,1)S(1)}, u32[]{:S(2)}, u32[]{:S(2)}) collective-permute-start(bf16[1,4,256,256]{3,2,1,0:T(8,128)(2,1)} %get-tuple-element.44), channel_id=1, source_target_pairs={{4,14},{6,12},{8,2},{10,0},{12,22},{14,20},{16,10},{18,8},{20,30},... | collective-permute-start | bytes 1572872 | tf_op jit(solution)/shard_map/ppermute | solution.py:315
  29.2 30.6 %copy-start.9 = (bf16[1,4,256,256]{3,2,1,0:T(8,128)(2,1)}, bf16[1,4,256,256]{3,2,1,0:T(8,128)(2,1)S(1)}, u32[]{:S(2)}) copy-start(bf16[1,4,256,256]{3,2,1,0:T(8,128)(2,1)S(1)} %collective-permute-done.4.refs_4_) | copy-start | bytes 1572868
  34.7 25.2 %copy-start.10 = (bf16[1,4,256,256]{3,2,1,0:T(8,128)(2,1)}, bf16[1,4,256,256]{3,2,1,0:T(8,128)(2,1)S(1)}, u32[]{:S(2)}) copy-start(bf16[1,4,256,256]{3,2,1,0:T(8,128)(2,1)S(1)} %collective-permute-done.3.refs_3_) | copy-start | bytes 1572868
  34.7 15.0 %collective-permute-start.2 = (bf16[1,4,256,256]{3,2,1,0:T(8,128)(2,1)}, bf16[1,4,256,256]{3,2,1,0:T(8,128)(2,1)S(1)}, u32[]{:S(2)}, u32[]{:S(2)}) collective-permute-start(bf16[1,4,256,256]{3,2,1,0:T(8,128)(2,1)} %get-tuple-element.37), channel_id=1, source_target_pairs={{0,4},{2,6},{4,0},{6,2},{8,12},{10,14},{12,8},{14,10},{16,20},{18,... | collective-permute-start | bytes 1572872 | tf_op jit(solution)/shard_map/ppermute | solution.py:315
  36.2 23.6 %collective-permute-start.5 = (bf16[1,4,256,256]{3,2,1,0:T(8,128)(2,1)}, bf16[1,4,256,256]{3,2,1,0:T(8,128)(2,1)S(1)}, u32[]{:S(2)}, u32[]{:S(2)}) collective-permute-start(bf16[1,4,256,256]{3,2,1,0:T(8,128)(2,1)} %get-tuple-element.41), channel_id=1, source_target_pairs={{0,6},{2,4},{4,2},{6,0},{8,14},{10,12},{12,10},{14,8},{16,22},{18,... | collective-permute-start | bytes 1572872 | tf_op jit(solution)/shard_map/ppermute | solution.py:315
  38.4 21.4 %copy-start.11 = (bf16[1,4,256,256]{3,2,1,0:T(8,128)(2,1)}, bf16[1,4,256,256]{3,2,1,0:T(8,128)(2,1)S(1)}, u32[]{:S(2)}) copy-start(bf16[1,4,256,256]{3,2,1,0:T(8,128)(2,1)S(1)} %collective-permute-done.9.refs_6_) | copy-start | bytes 1572868
  38.4 21.4 %collective-permute-start.11 = (bf16[1,4,256,256]{3,2,1,0:T(8,128)(2,1)S(1)}, bf16[1,4,256,256]{3,2,1,0:T(8,128)(2,1)S(1)}, u32[]{:S(2)}, u32[]{:S(2)}) collective-permute-start(bf16[1,4,256,256]{3,2,1,0:T(8,128)(2,1)S(1)} %collective-permute-done.3.refs_3_), channel_id=1, source_target_pairs={{0,8},{2,10},{8,16},{10,18},{12,4},{14,6},{16,24},{18,26},{20,12},... | collective-permute-start | bytes 1572872 | tf_op jit(solution)/shard_map/ppermute | solution.py:315
  42.8 34.5 %collective-permute-start.6 = (bf16[1,4,256,256]{3,2,1,0:T(8,128)(2,1)}, bf16[1,4,256,256]{3,2,1,0:T(8,128)(2,1)S(1)}, u32[]{:S(2)}, u32[]{:S(2)}) collective-permute-start(bf16[1,4,256,256]{3,2,1,0:T(8,128)(2,1)} %get-tuple-element.42.refs_0_), channel_id=1, source_target_pairs={{4,12},{6,14},{8,0},{10,2},{12,20},{14,22},{16,8},{18,10},{20,28},... | collective-permute-start | bytes 1572872 | tf_op jit(solution)/shard_map/ppermute | solution.py:315
  44.1 33.2 %collective-permute-start.8 = (bf16[1,4,256,256]{3,2,1,0:T(8,128)(2,1)}, bf16[1,4,256,256]{3,2,1,0:T(8,128)(2,1)S(1)}, u32[]{:S(2)}, u32[]{:S(2)}) collective-permute-start(bf16[1,4,256,256]{3,2,1,0:T(8,128)(2,1)} %get-tuple-element.45), channel_id=1, source_target_pairs={{4,14},{6,12},{8,2},{10,0},{12,22},{14,20},{16,10},{18,8},{20,30},... | collective-permute-start | bytes 1572872 | tf_op jit(solution)/shard_map/ppermute | solution.py:315
  49.6 27.8 %copy-start.3 = (bf16[1,4,256,256]{3,2,1,0:T(8,128)(2,1)}, bf16[1,4,256,256]{3,2,1,0:T(8,128)(2,1)S(1)}, u32[]{:S(2)}) copy-start(bf16[1,4,256,256]{3,2,1,0:T(8,128)(2,1)S(1)} %collective-permute-done.2.refs_2_) | copy-start | bytes 1572868
  49.6 27.7 %collective-permute-start.10 = (bf16[1,4,256,256]{3,2,1,0:T(8,128)(2,1)S(1)}, bf16[1,4,256,256]{3,2,1,0:T(8,128)(2,1)S(1)}, u32[]{:S(2)}, u32[]{:S(2)}) collective-permute-start(bf16[1,4,256,256]{3,2,1,0:T(8,128)(2,1)S(1)} %collective-permute-done.2.refs_2_), channel_id=1, source_target_pairs={{0,8},{2,10},{8,16},{10,18},{12,4},{14,6},{16,24},{18,26},{20,12},... | collective-permute-start | bytes 1572872 | tf_op jit(solution)/shard_map/ppermute | solution.py:315
  60.8 16.6 %collective-permute-start.12 = (bf16[1,4,256,256]{3,2,1,0:T(8,128)(2,1)S(1)}, bf16[1,4,256,256]{3,2,1,0:T(8,128)(2,1)}, u32[]{:S(2)}, u32[]{:S(2)}) collective-permute-start(bf16[1,4,256,256]{3,2,1,0:T(8,128)(2,1)S(1)} %collective-permute-done.5.refs_3_), channel_id=1, source_target_pairs={{0,8},{2,10},{8,16},{10,18},{12,4},{14,6},{16,24},{18,26},{20,12},... | collective-permute-start | bytes 1572872 | tf_op jit(solution)/shard_map/ppermute | solution.py:315
  90.5 2.7 %collective-permute-start.13 = (bf16[2,4,208,256]{3,2,1,0:T(8,128)(2,1)}, bf16[2,4,208,256]{3,2,1,0:T(8,128)(2,1)S(1)}, u32[]{:S(2)}, u32[]{:S(2)}) collective-permute-start(bf16[2,4,208,256]{3,2,1,0:T(8,128)(2,1)} %get-tuple-element.54), channel_id=1, source_target_pairs={{0,2},{2,0},{4,6},{6,4},{8,10},{10,8},{12,14},{14,12},{16,18},{18,... | collective-permute-start | bytes 2555912 | tf_op jit(solution)/shard_map/ppermute | solution.py:315
  95.5 8.2 %collective-permute-start.14 = (bf16[4,208,128]{2,1,0:T(8,128)(2,1)S(1)}, bf16[4,208,128]{2,1,0:T(8,128)(2,1)S(1)}, u32[]{:S(2)}, u32[]{:S(2)}) collective-permute-start(bf16[4,208,128]{2,1,0:T(8,128)(2,1)S(1)} %get-tuple-element.56), channel_id=1, source_target_pairs={{0,1},{1,0},{2,3},{3,2},{4,5},{5,4},{6,7},{7,6},{8,9},{9,8},{10,11... | collective-permute-start | bytes 638984 | tf_op jit(solution)/shard_map/ppermute | solution.py:360
  97.1 11.6 %collective-permute-start.15 = (bf16[4,208,128]{2,1,0:T(8,128)(2,1)S(1)}, bf16[4,208,128]{2,1,0:T(8,128)(2,1)S(1)}, u32[]{:S(2)}, u32[]{:S(2)}) collective-permute-start(bf16[4,208,128]{2,1,0:T(8,128)(2,1)S(1)} %get-tuple-element.57), channel_id=1, source_target_pairs={{0,4},{1,5},{2,6},{3,7},{4,0},{5,1},{6,2},{7,3},{8,12},{9,13},{10,... | collective-permute-start | bytes 638984 | tf_op jit(solution)/shard_map/ppermute | solution.py:360
  97.5 11.2 %collective-permute-start.16 = (bf16[4,208,128]{2,1,0:T(8,128)(2,1)S(1)}, bf16[4,208,128]{2,1,0:T(8,128)(2,1)S(1)}, u32[]{:S(2)}, u32[]{:S(2)}) collective-permute-start(bf16[4,208,128]{2,1,0:T(8,128)(2,1)S(1)} %get-tuple-element.58), channel_id=1, source_target_pairs={{0,5},{1,4},{2,7},{3,6},{4,1},{5,0},{6,3},{7,2},{8,13},{9,12},{10,... | collective-permute-start | bytes 638984 | tf_op jit(solution)/shard_map/ppermute | solution.py:360
  108.8 5.0 %collective-permute-start.17 = (bf16[2,208,128]{2,1,0:T(8,128)(2,1)S(1)}, bf16[2,208,128]{2,1,0:T(8,128)(2,1)S(1)}, u32[]{:S(2)}, u32[]{:S(2)}) collective-permute-start(bf16[2,208,128]{2,1,0:T(8,128)(2,1)S(1)} %get-tuple-element.60), channel_id=1, source_target_pairs={{0,8},{2,10},{8,16},{10,18},{16,24},{18,26},{1,9},{3,11},{9,17},{1... | collective-permute-start | bytes 319496 | tf_op jit(solution)/shard_map/ppermute | solution.py:315
  (8 other events, 53.0 us)

commit v3 on v2

--- a/solution.py
+++ b/solution.py
@@ -40,59 +40,91 @@
     return sorted({piece for item in items for piece in item})
 
 
-def whiten_kernel(items, pos_ref, valid_ref, spectra_ref, *refs):
-    outs, held = refs[:-1], refs[-1]
-    _, tile, windows, freqs = spectra_ref.shape
+def whiten_kernel(items, tile, valid_ref, spectra_ref, *refs):
+    outs, (raw, held, ready, load_sem, store_sem) = refs[: len(items)], refs[len(items) :]
+    member = lax.rem(lax.axis_index("blk"), GROUP)
+    _, channels, windows, freqs = spectra_ref.shape
     parts = freqs // (GROUP * LANES)
-    place = (tile, valid_ref.shape[1])
-    row = lax.broadcasted_iota(jnp.int32, place, 0) + pl.program_id(0) * tile
-    here = row == lax.broadcasted_iota(jnp.int32, place, 1)
-    valid = jnp.sum(jnp.where(here, valid_ref[...].astype(F32), 0.0), axis=1, keepdims=True)
-    for at, piece in enumerate(pieces_of(items)):
-        lanes = pl.ds(pl.multiple_of(((pos_ref[0] ^ piece[0]) * parts + piece[1]) * LANES, LANES), LANES)
-        for half in range(2):
-            held[at, half] = spectra_ref[half, :, :, lanes].reshape(tile * windows, LANES).astype(F32)
-        values = [[held[at, half, pl.ds(w, tile, stride=windows), :] for half in range(2)] for w in range(windows)]
-        power = values[0][0] * values[0][0] + values[0][1] * values[0][1]
-        for real, imag in values[1:]:
-            power = power + (real * real + imag * imag)
-        scale = valid / jnp.maximum(jnp.sqrt(power * (1.0 / windows)), 0.5)
-        for w in range(windows):
-            both = jnp.concatenate([values[w][half] * scale for half in range(2)], axis=1).astype(BF16)
-            for item, out in zip(items, outs):
-                for index, wanted in enumerate(item):
-                    if wanted == piece:
-                        out[index, w] = both
-
-
-def whiten(spectra, valid, pos, items):
-    _, channels, windows, freqs = spectra.shape
-    tile = min(64, channels)
+    pieces = pieces_of(items)
+    steps = channels // tile
+
+    def load(step):
+        rows = pl.ds(pl.multiple_of(step * tile, tile), tile)
+        return pltpu.make_async_copy(spectra_ref.at[:, rows], raw.at[:, rows], load_sem.at[step])
+
+    def stores(step):
+        rows = pl.ds(pl.multiple_of(step * tile, tile), tile)
+        copies = []
+        for out, item in zip(outs, items):
+            for index, piece in enumerate(item):
+                source = ready.at[pieces.index(piece), :, rows]
+                copies.append(pltpu.make_async_copy(source, out.at[index, :, rows], store_sem.at[step, len(copies)]))
+        return copies
+
+    for step in range(steps):
+        load(step).start()
+
+    def work(step, carry):
+        load(step).wait()
+        rows = pl.ds(pl.multiple_of(step * tile, tile), tile)
+        place = (tile, channels)
+        row = lax.broadcasted_iota(jnp.int32, place, 0) + step * tile
+        here = row == lax.broadcasted_iota(jnp.int32, place, 1)
+        valid = jnp.sum(jnp.where(here, valid_ref[...].astype(F32), 0.0), axis=1, keepdims=True)
+        for at, (flip, part) in enumerate(pieces):
+            lanes = pl.ds(pl.multiple_of(((member ^ flip) * parts + part) * LANES, LANES), LANES)
+            for half in range(2):
+                held[at, half] = raw[half, rows, :, lanes].reshape(tile * windows, LANES).astype(F32)
+            values = [
+                [held[at, half, pl.ds(w, tile, stride=windows), :] for half in range(2)] for w in range(windows)
+            ]
+            power = values[0][0] * values[0][0] + values[0][1] * values[0][1]
+            for real, imag in values[1:]:
+                power = power + (real * real + imag * imag)
+            scale = valid / jnp.maximum(jnp.sqrt(power * (1.0 / windows)), 0.5)
+            for w in range(windows):
+                both = jnp.concatenate([values[w][half] * scale for half in range(2)], axis=1)
+                ready[at, w, rows, :] = both.astype(BF16)
+        for copy in stores(step):
+            copy.start()
+        return carry
+
+    lax.fori_loop(0, steps, work, 0)
+
+    def drain(step, carry):
+        for copy in stores(step):
+            copy.wait()
+        return carry
+
+    lax.fori_loop(0, steps, drain, 0)
+
+
+def whiten(spectra, valid, items):
+    _, channels, windows, _ = spectra.shape
+    tile = min(32, channels)
     count = len(pieces_of(items))
-    in_specs = [
-        pl.BlockSpec((1, channels), lambda i, pos: (0, 0)),
-        pl.BlockSpec((2, tile, windows, freqs), lambda i, pos: (0, i, 0, 0)),
-    ]
-    out_specs = [pl.BlockSpec((len(item), windows, tile, 2 * LANES), lambda i, pos: (0, 0, i, 0)) for item in items]
+    anywhere = pl.BlockSpec(memory_space=pl.ANY)
     return pl.pallas_call(
-        functools.partial(whiten_kernel, items),
-        grid_spec=pltpu.PrefetchScalarGridSpec(
-            num_scalar_prefetch=1,
-            grid=(channels // tile,),
-            in_specs=in_specs,
-            out_specs=out_specs,
-            scratch_shapes=[pltpu.VMEM((count, 2, tile * windows, LANES), F32)],
-        ),
+        functools.partial(whiten_kernel, items, tile),
+        in_specs=[pl.BlockSpec(memory_space=pltpu.VMEM), anywhere],
+        out_specs=[anywhere] * len(items),
+        scratch_shapes=[
+            pltpu.VMEM(spectra.shape, BF16),
+            pltpu.VMEM((count, 2, tile * windows, LANES), F32),
+            pltpu.VMEM((count, windows, channels, 2 * LANES), BF16),
+            pltpu.SemaphoreType.DMA((channels // tile,)),
+            pltpu.SemaphoreType.DMA((channels // tile, sum(len(item) for item in items))),
+        ],
         out_shape=[jax.ShapeDtypeStruct((len(item), windows, channels, 2 * LANES), BF16) for item in items],
         compiler_params=pltpu.CompilerParams(vmem_limit_bytes=56 << 20),
         cost_estimate=pl.CostEstimate(flops=0, bytes_accessed=1000, transcendentals=0),
         name="whiten",
-    )(pos, valid, spectra)
+    )(valid, spectra)
 
 
 def correlate_kernel(pairs, places, part, pos_ref, *refs):
-    count = 2 * GROUP
-    blocks, before = refs[:count], refs[count:-16]
+    count, pieces = 2 * GROUP, sum(len(block) for block in places)
+    blocks, before = iter(refs[:pieces]), refs[pieces:-16]
     fwd_in, lag_in, inv_in, keep_out, send_out = refs[-16:-11]
     held, held_before, fwd_ref, lag_ref, inv_ref, hat, plus, cross, turned, result, sem = refs[-11:]
     member = pos_ref[0]
@@ -104,19 +136,28 @@
         copy.start()
         return copy
 
-    loads = [load(count, fwd_in, fwd_ref)]
-    loads += [load(index, blocks[index].at[places[index]], held.at[index]) for index in range(count)]
+    fwd_load = load(pieces, fwd_in, fwd_ref)
+    loads = []
+    for index, block in enumerate(places):
+        first = 0
+        for place in block:
+            source = next(blocks).at[place]
+            target = held.at[index, pl.ds(first, source.shape[0])]
+            loads.append((index, load(len(loads), source, target)))
+            first += source.shape[0]
     later = [
-        load(count + 1, inv_in, inv_ref),
-        load(count + 2, lag_in.at[(pos_ref[1] * GROUP + member) * PARTS + part], lag_ref),
+        load(pieces + 1, inv_in, inv_ref),
+        load(pieces + 2, lag_in.at[(pos_ref[1] * GROUP + member) * PARTS + part], lag_ref),
     ]
-    later += [load(count + 3 + index, source, held_before.at[index]) for index, source in enumerate(before)]
-    loads[0].wait()
+    later += [load(pieces + 3 + index, source, held_before.at[index]) for index, source in enumerate(before)]
+    fwd_load.wait()
     for index in range(count):
         slot = member ^ (index % GROUP)
         if index >= GROUP:
             slot = jnp.where(slot < 2, slot + 6, slot + 2)
-        loads[1 + index].wait()
+        for target, copy in loads:
+            if target == index:
+                copy.wait()
         for w in range(windows):
             terms = jnp.dot(fwd_ref[...], held[index, w], preferred_element_type=F32)
             cos_r, cos_i = terms[:half, :LANES], terms[:half, LANES:]
@@ -169,7 +210,7 @@
                 total = total + held_before[flip % 2, flip // 2, distance].astype(F32)
             result[flip, distance] = total.astype(BF16)
         out = (keep_out, send_out)[flip % 2].at[flip // 2]
-        stores.append(pltpu.make_async_copy(result.at[flip], out, sem.at[count + 5 + flip]))
+        stores.append(pltpu.make_async_copy(result.at[flip], out, sem.at[pieces + 5 + flip]))
         stores[-1].start()
     for copy in stores:
         copy.wait()
@@ -177,16 +218,18 @@
 
 def correlate(pos, part, blocks, tables, before=()):
     fwd, lag, inv = tables
-    _, windows, channels, lanes = blocks[0][0].shape
+    windows = sum(array.shape[1] for array, _ in blocks[0])
+    channels, lanes = blocks[0][0][0].shape[2:]
     rows = lag.shape[1]
     pairs = pair_list()
     half = fwd.shape[0] // 2
-    places = [place for _, place in blocks]
+    places = [[place for _, place in block] for block in blocks]
+    arrays = [array for block in blocks for array, _ in block]
     shape = (2, ROUNDS, rows, channels)
     anywhere = pl.BlockSpec(memory_space=pl.ANY)
     return pl.pallas_call(
         functools.partial(correlate_kernel, pairs, places, part),
-        in_specs=[pl.BlockSpec(memory_space=pltpu.SMEM)] + [anywhere] * (len(blocks) + len(before) + 3),
+        in_specs=[pl.BlockSpec(memory_space=pltpu.SMEM)] + [anywhere] * (len(arrays) + len(before) + 3),
         out_specs=[anywhere, anywhere],
         scratch_shapes=[
             pltpu.VMEM((2 * GROUP, windows, channels, lanes), BF16),
@@ -199,13 +242,13 @@
             pltpu.VMEM((len(pairs), 2 * half, 2 * LANES), F32),
             pltpu.VMEM((len(pairs), channels, 2 * LANES), BF16),
             pltpu.VMEM((GROUP, *shape[1:]), BF16),
-            pltpu.SemaphoreType.DMA((2 * GROUP + 9,)),
+            pltpu.SemaphoreType.DMA((len(arrays) + 9,)),
         ],
         out_shape=[jax.ShapeDtypeStruct(shape, BF16)] * 2,
-        compiler_params=pltpu.CompilerParams(vmem_limit_bytes=60 << 20),
+        compiler_params=pltpu.CompilerParams(vmem_limit_bytes=62 << 20),
         cost_estimate=pl.CostEstimate(flops=0, bytes_accessed=1000, transcendentals=0),
         name="correlate",
-    )(pos, *[array for array, _ in blocks], *before, fwd, lag, inv)
+    )(pos, *arrays, *before, fwd, lag, inv)
 
 
 def halves_kernel(pos_ref, *refs):
@@ -329,7 +372,6 @@
     y02, y03, y12, y13, core, core0, core1, own0, own1 = whiten(
         spectra,
         valid,
-        pos,
         [[(2, 0)], [(3, 0)], [(2, 1)], [(3, 1)], [(1, 0), (1, 1)], [(1, 0)], [(1, 1)], [(0, 0)], [(0, 1)]],
     )
     y02_came = swap(y02, 2)
@@ -346,8 +388,8 @@
     far12 = forward(after(y12_came, far02))
     far13 = forward(after(y13_came, far03))
 
-    blocks0 = [(own0, 0), (core_came, 0), (y02_came, 0), (y03_came, 0), (near00, 0), (near01, 0), (far02, 0), (far03, 0)]
-    blocks1 = [(own1, 0), (core_came, 1), (y12_came, 0), (y13_came, 0), (near10, 0), (near11, 0), (far12, 0), (far13, 0)]
+    blocks0 = [[(own0, 0)], [(core_came, 0)], [(y02_came, 0)], [(y03_came, 0)], [(near00, 0)], [(near01, 0)], [(far02, 0)], [(far03, 0)]]
+    blocks1 = [[(own1, 0)], [(core_came, 1)], [(y12_came, 0)], [(y13_came, 0)], [(near10, 0)], [(near11, 0)], [(far12, 0)], [(far13, 0)]]
     partial = correlate(after(pos, y13_came), 0, blocks0, tables)
     keep, send = correlate(pos, 1, blocks1, tables, partial)
     came = swap(send, 1)

time: 116 us -> 113 us (0.974)
  local copies, waits for them, and re-layouts: 3.19 us -> 1.19 us
  starting transfers between devices: 35.4 us -> 36.6 us
    unnamed x28 -> x20, local copies, waits for them, and re-layouts: 3.19 us -> 1.19 us
    ppermute x15, starting transfers between devices: 31.8 us -> 33.1 us  [move(): return lax.ppermute(value, 'blk', pairs)]
  transfers between devices with their start and end apart: 18 -> 18, of which waited for: 9 -> 9; matrix products, arithmetic and copies ran while one was open for 0% -> 1% of each run, Pallas kernels for 10% -> 11%
where the time goes in v3:
time: 113 us
  waiting for transfers between devices  41.3 us (37%)
  starting transfers between devices  36.6 us (32%)
  Pallas kernels  33 us (29%)
  local copies, waits for them, and re-layouts  1.19 us (1%)
    ppermute x15, starting transfers between devices, move(): return lax.ppermute(value, 'blk', pairs)  33.1 us
    ppermute x15, waiting for transfers between devices, move(): return lax.ppermute(value, 'blk', pairs)  31.7 us
    pallas_call x2, Pallas kernels, correlate(): pl.pallas_call(functools.partial(correlate_kernel, pairs, places, part),...  23.9 us
    ppermute x3, waiting for transfers between devices, both(): return lax.ppermute(value, ('blk', 'frq'), pairs)  9.61 us
    pallas_call x1, Pallas kernels, whiten(): pl.pallas_call(functools.partial(whiten_kernel, items, tile), in_specs=[p...  6.38 us
    ppermute x3, starting transfers between devices, both(): return lax.ppermute(value, ('blk', 'frq'), pairs)  3.55 us
  transfers between devices with their start and end apart: 18, of which 9 were waited for; matrix products, arithmetic and copies ran while one was open for 1% of the time, Pallas kernels for 11%

profile of v3, /device:TPU:0, one launch (start us, length us, event | category | flops | bytes accessed | tf_op | source)
XLA Modules:
  0.0 112.9 jit_solution(1381562688970312141)
XLA Ops:
  0.0 6.4 %whiten.1 = (bf16[1,4,256,256]{3,2,1,0:T(8,128)(2,1)}, bf16[1,4,256,256]{3,2,1,0:T(8,128)(2,1)}, bf16[1,4,256,256]{3,2,1,0:T(8,128)(2,1)}, bf16[1,4,256,256]{3,2...) custom-call(s32[1,256]{1,0:T(1,128)} %bitcast.6, ...), custom_call_target="tpu_custom_call" | custom-call | bytes 1000 | tf_op jit(solution)/shard_map/whiten/pallas_call | solution.py:107
  6.9 2.6 %collective-permute-start.1 = (bf16[1,4,256,256]{3,2,1,0:T(8,128)(2,1)}, bf16[1,4,256,256]{3,2,1,0:T(8,128)(2,1)S(1)}, u32[]{:S(2)}, u32[]{:S(2)}) collective-permute-start(bf16[1,4,256,256]{3,2,1,0:T(8,128)(2,1)} %get-tuple-element.36), channel_id=1, source_target_pairs={{0,4},{2,6},{4,0},{6,2},{8,12},{10,14},{12,8},{14,10},{16,20},{18,... | collective-permute-start | bytes 1572872 | tf_op jit(solution)/shard_map/ppermute | solution.py:358
  10.8 2.3 %collective-permute-start.3 = (bf16[1,4,256,256]{3,2,1,0:T(8,128)(2,1)}, bf16[1,4,256,256]{3,2,1,0:T(8,128)(2,1)S(1)}, u32[]{:S(2)}, u32[]{:S(2)}) collective-permute-start(bf16[1,4,256,256]{3,2,1,0:T(8,128)(2,1)} %get-tuple-element.39), channel_id=1, source_target_pairs={{0,6},{2,4},{4,2},{6,0},{8,14},{10,12},{12,10},{14,8},{16,22},{18,... | collective-permute-start | bytes 1572872 | tf_op jit(solution)/shard_map/ppermute | solution.py:358
  13.1 9.4 %collective-permute-done.1.refs_2_ = bf16[1,4,256,256]{3,2,1,0:T(8,128)(2,1)S(1)} collective-permute-done((bf16[1,4,256,256]{3,2,1,0:T(8,128)(2,1)}, bf16[1,4,256,256]{3,2,1,0:T(8,128)(2,1)S(1)}, u32[]{:S(2)}, u32[]{:S(2)}) %collective-permute-start.1) | collective-permute-done | bytes 524320 | tf_op jit(solution)/shard_map/ppermute | solution.py:358
  22.5 3.9 %collective-permute-start.9 = (bf16[1,4,256,256]{3,2,1,0:T(8,128)(2,1)S(1)}, bf16[1,4,256,256]{3,2,1,0:T(8,128)(2,1)S(1)}, u32[]{:S(2)}, u32[]{:S(2)}) collective-permute-start(bf16[1,4,256,256]{3,2,1,0:T(8,128)(2,1)S(1)} %collective-permute-done.1.refs_2_), channel_id=1, source_target_pairs={{0,8},{2,10},{8,16},{10,18},{12,4},{14,6},{16,24},{18,26},{20,12},... | collective-permute-start | bytes 1572872 | tf_op jit(solution)/shard_map/ppermute | solution.py:358
  26.4 1.3 %collective-permute-start.7 = (bf16[1,4,256,256]{3,2,1,0:T(8,128)(2,1)}, bf16[1,4,256,256]{3,2,1,0:T(8,128)(2,1)S(1)}, u32[]{:S(2)}, u32[]{:S(2)}) collective-permute-start(bf16[1,4,256,256]{3,2,1,0:T(8,128)(2,1)} %get-tuple-element.44), channel_id=1, source_target_pairs={{4,14},{6,12},{8,2},{10,0},{12,22},{14,20},{16,10},{18,8},{20,30},... | collective-permute-start | bytes 1572872 | tf_op jit(solution)/shard_map/ppermute | solution.py:358
  27.8 5.4 %collective-permute-done.3.refs_3_ = bf16[1,4,256,256]{3,2,1,0:T(8,128)(2,1)S(1)} collective-permute-done((bf16[1,4,256,256]{3,2,1,0:T(8,128)(2,1)}, bf16[1,4,256,256]{3,2,1,0:T(8,128)(2,1)S(1)}, u32[]{:S(2)}, u32[]{:S(2)}) %collective-permute-start.3) | collective-permute-done | bytes 524320 | tf_op jit(solution)/shard_map/ppermute | solution.py:358
  33.2 1.6 %collective-permute-start.2 = (bf16[1,4,256,256]{3,2,1,0:T(8,128)(2,1)}, bf16[1,4,256,256]{3,2,1,0:T(8,128)(2,1)S(1)}, u32[]{:S(2)}, u32[]{:S(2)}) collective-permute-start(bf16[1,4,256,256]{3,2,1,0:T(8,128)(2,1)} %get-tuple-element.37), channel_id=1, source_target_pairs={{0,4},{2,6},{4,0},{6,2},{8,12},{10,14},{12,8},{14,10},{16,20},{18,... | collective-permute-start | bytes 1572872 | tf_op jit(solution)/shard_map/ppermute | solution.py:358
  35.0 2.0 %collective-permute-done.9.refs_6_ = bf16[1,4,256,256]{3,2,1,0:T(8,128)(2,1)S(1)} collective-permute-done((bf16[1,4,256,256]{3,2,1,0:T(8,128)(2,1)S(1)}, bf16[1,4,256,256]{3,2,1,0:T(8,128)(2,1)S(1)}, u32[]{:S(2)}, u32[]{:S(2)}) %collective-permute-start.9) | collective-permute-done | bytes 524320 | tf_op jit(solution)/shard_map/ppermute | solution.py:358
  36.9 4.4 %collective-permute-start.11 = (bf16[1,4,256,256]{3,2,1,0:T(8,128)(2,1)S(1)}, bf16[1,4,256,256]{3,2,1,0:T(8,128)(2,1)S(1)}, u32[]{:S(2)}, u32[]{:S(2)}) collective-permute-start(bf16[1,4,256,256]{3,2,1,0:T(8,128)(2,1)S(1)} %collective-permute-done.3.refs_3_), channel_id=1, source_target_pairs={{0,8},{2,10},{8,16},{10,18},{12,4},{14,6},{16,24},{18,26},{20,12},... | collective-permute-start | bytes 1572872 | tf_op jit(solution)/shard_map/ppermute | solution.py:358
  42.7 1.3 %collective-permute-start.8 = (bf16[1,4,256,256]{3,2,1,0:T(8,128)(2,1)}, bf16[1,4,256,256]{3,2,1,0:T(8,128)(2,1)}, u32[]{:S(2)}, u32[]{:S(2)}) collective-permute-start(bf16[1,4,256,256]{3,2,1,0:T(8,128)(2,1)} %get-tuple-element.45), channel_id=1, source_target_pairs={{4,14},{6,12},{8,2},{10,0},{12,22},{14,20},{16,10},{18,8},{20,30},... | collective-permute-start | bytes 1572872 | tf_op jit(solution)/shard_map/ppermute | solution.py:358
  44.0 4.2 %collective-permute-done.2.refs_2_ = bf16[1,4,256,256]{3,2,1,0:T(8,128)(2,1)S(1)} collective-permute-done((bf16[1,4,256,256]{3,2,1,0:T(8,128)(2,1)}, bf16[1,4,256,256]{3,2,1,0:T(8,128)(2,1)S(1)}, u32[]{:S(2)}, u32[]{:S(2)}) %collective-permute-start.2) | collective-permute-done | bytes 524320 | tf_op jit(solution)/shard_map/ppermute | solution.py:358
  48.2 4.3 %collective-permute-start.10 = (bf16[1,4,256,256]{3,2,1,0:T(8,128)(2,1)S(1)}, bf16[1,4,256,256]{3,2,1,0:T(8,128)(2,1)}, u32[]{:S(2)}, u32[]{:S(2)}) collective-permute-start(bf16[1,4,256,256]{3,2,1,0:T(8,128)(2,1)S(1)} %collective-permute-done.2.refs_2_), channel_id=1, source_target_pairs={{0,8},{2,10},{8,16},{10,18},{12,4},{14,6},{16,24},{18,26},{20,12},... | collective-permute-start | bytes 1572872 | tf_op jit(solution)/shard_map/ppermute | solution.py:358
  52.5 6.0 %collective-permute-done.5.refs_3_ = bf16[1,4,256,256]{3,2,1,0:T(8,128)(2,1)} collective-permute-done((bf16[1,4,256,256]{3,2,1,0:T(8,128)(2,1)}, bf16[1,4,256,256]{3,2,1,0:T(8,128)(2,1)}, u32[]{:S(2)}, u32[]{:S(2)}) %collective-permute-start.5) | collective-permute-done | bytes 524320 | tf_op jit(solution)/shard_map/ppermute | solution.py:358
  58.5 4.7 %collective-permute-start.12 = (bf16[1,4,256,256]{3,2,1,0:T(8,128)(2,1)}, bf16[1,4,256,256]{3,2,1,0:T(8,128)(2,1)}, u32[]{:S(2)}, u32[]{:S(2)}) collective-permute-start(bf16[1,4,256,256]{3,2,1,0:T(8,128)(2,1)} %collective-permute-done.5.refs_3_), channel_id=1, source_target_pairs={{0,8},{2,10},{8,16},{10,18},{12,4},{14,6},{16,24},{18,26},{20,12},... | collective-permute-start | bytes 1572872 | tf_op jit(solution)/shard_map/ppermute | solution.py:358
  63.8 11.9 %correlate.2 = (bf16[2,4,208,256]{3,2,1,0:T(8,128)(2,1)}, bf16[2,4,208,256]{3,2,1,0:T(8,128)(2,1)}) custom-call(s32[2]{0:T(128)} %pad_add_fusion.pos_ref, bf16[1,4,256,256]{3,2,1,0:T(8,128)(2,1)} %get-tuple-element.40.refs_0_, bf16[2,4,256,256]{3,2,1,0:T(8,128)(2,1)} %copy-done.2, bf16[1,4,256,256]{3,2,1,0:T(8,128)(2,1)} %copy-done.4, ...), custom_call_target="tpu_custom_call" | custom-call | bytes 1000 | tf_op jit(solution)/shard_map/correlate/pallas_call | solution.py:230
  75.8 12.0 %correlate.3 = (bf16[2,4,208,256]{3,2,1,0:T(8,128)(2,1)}, bf16[2,4,208,256]{3,2,1,0:T(8,128)(2,1)}) custom-call(s32[2]{0:T(128)} %pad_add_fusion.pos_ref, bf16[1,4,256,256]{3,2,1,0:T(8,128)(2,1)} %get-tuple-element.42.refs_0_, bf16[2,4,256,256]{3,2,1,0:T(8,128)(2,1)} %copy-done.2, bf16[1,4,256,256]{3,2,1,0:T(8,128)(2,1)} %copy-done.3, ...), custom_call_target="tpu_custom_call" | custom-call | bytes 1000 | tf_op jit(solution)/shard_map/correlate/pallas_call | solution.py:230
  87.9 2.4 %collective-permute-done.13.refs_4_.refs_5_.refs_6_.refs_7_ = bf16[2,4,208,256]{3,2,1,0:T(8,128)(2,1)S(1)} collective-permute-done((bf16[2,4,208,256]{3,2,1,0:T(8,128)(2,1)}, bf16[2,4,208,256]{3,2,1,0:T(8,128)(2,1)S(1)}, u32[]{:S(2)}, u32[]{:S(2)}) %collective-permute-start.13) | collective-permute-done | bytes 852000 | tf_op jit(solution)/shard_map/ppermute | solution.py:358
  92.7 1.6 %collective-permute-start.14 = (bf16[4,208,128]{2,1,0:T(8,128)(2,1)S(1)}, bf16[4,208,128]{2,1,0:T(8,128)(2,1)S(1)}, u32[]{:S(2)}, u32[]{:S(2)}) collective-permute-start(bf16[4,208,128]{2,1,0:T(8,128)(2,1)S(1)} %get-tuple-element.56), channel_id=1, source_target_pairs={{0,1},{1,0},{2,3},{3,2},{4,5},{5,4},{6,7},{7,6},{8,9},{9,8},{10,11... | collective-permute-start | bytes 638984 | tf_op jit(solution)/shard_map/ppermute | solution.py:402
  96.2 4.6 %collective-permute-done.14.refs_1_ = bf16[4,208,128]{2,1,0:T(8,128)(2,1)S(1)} collective-permute-done((bf16[4,208,128]{2,1,0:T(8,128)(2,1)S(1)}, bf16[4,208,128]{2,1,0:T(8,128)(2,1)S(1)}, u32[]{:S(2)}, u32[]{:S(2)}) %collective-permute-start.14) | collective-permute-done | bytes 213024 | tf_op jit(solution)/shard_map/ppermute | solution.py:402
  100.9 5.0 %collective-permute-done.15.refs_2_ = bf16[4,208,128]{2,1,0:T(8,128)(2,1)S(1)} collective-permute-done((bf16[4,208,128]{2,1,0:T(8,128)(2,1)S(1)}, bf16[4,208,128]{2,1,0:T(8,128)(2,1)S(1)}, u32[]{:S(2)}, u32[]{:S(2)}) %collective-permute-start.15) | collective-permute-done | bytes 213024 | tf_op jit(solution)/shard_map/ppermute | solution.py:402
  106.0 3.1 %collective-permute-start.17 = (bf16[2,208,128]{2,1,0:T(8,128)(2,1)S(1)}, bf16[2,208,128]{2,1,0:T(8,128)(2,1)S(1)}, u32[]{:S(2)}, u32[]{:S(2)}) collective-permute-start(bf16[2,208,128]{2,1,0:T(8,128)(2,1)S(1)} %get-tuple-element.60), channel_id=1, source_target_pairs={{0,8},{2,10},{8,16},{10,18},{16,24},{18,26},{1,9},{3,11},{9,17},{1... | collective-permute-start | bytes 319496 | tf_op jit(solution)/shard_map/ppermute | solution.py:358
  109.1 2.3 %collective-permute-done.17.behind_ref = bf16[2,208,128]{2,1,0:T(8,128)(2,1)S(1)} collective-permute-done((bf16[2,208,128]{2,1,0:T(8,128)(2,1)S(1)}, bf16[2,208,128]{2,1,0:T(8,128)(2,1)S(1)}, u32[]{:S(2)}, u32[]{:S(2)}) %collective-permute-start.17) | collective-permute-done | bytes 106528 | tf_op jit(solution)/shard_map/ppermute | solution.py:358
  111.4 1.5 %finish.1 = f32[201,4,128]{2,1,0:T(4,128)} custom-call(s32[2]{0:T(128)S(1)} %copy-done.1, f32[4,208,128]{2,1,0:T(8,128)S(1)} %get-tuple-element.59.own_ref, bf16[2,208,128]{2,1,0:T(8,128)(2,1)S(1)} %collective-permute-done.17.behind_ref), custom_call_target="tpu_custom_call" | custom-call | tf_op jit(solution)/shard_map/finish/pallas_call | solution.py:311
  (39 shorter events, 8.6 us)
Async XLA Ops:
  6.4 16.1 %collective-permute-start = (bf16[2,4,256,256]{3,2,1,0:T(8,128)(2,1)}, bf16[2,4,256,256]{3,2,1,0:T(8,128)(2,1)S(1)}, u32[]{:S(2)}, u32[]{:S(2)}) collective-permute-start(bf16[2,4,256,256]{3,2,1,0:T(8,128)(2,1)} %get-tuple-element.34), channel_id=1, source_target_pairs={{0,2},{2,0},{4,6},{6,4},{8,10},{10,8},{12,14},{14,12},{16,18},{18,... | collective-permute-start | bytes 3145736 | tf_op jit(solution)/shard_map/ppermute | solution.py:358
  6.9 15.6 %collective-permute-start.1 = (bf16[1,4,256,256]{3,2,1,0:T(8,128)(2,1)}, bf16[1,4,256,256]{3,2,1,0:T(8,128)(2,1)S(1)}, u32[]{:S(2)}, u32[]{:S(2)}) collective-permute-start(bf16[1,4,256,256]{3,2,1,0:T(8,128)(2,1)} %get-tuple-element.36), channel_id=1, source_target_pairs={{0,4},{2,6},{4,0},{6,2},{8,12},{10,14},{12,8},{14,10},{16,20},{18,... | collective-permute-start | bytes 1572872 | tf_op jit(solution)/shard_map/ppermute | solution.py:358
  9.5 18.2 %collective-permute-start.4 = (bf16[1,4,256,256]{3,2,1,0:T(8,128)(2,1)}, bf16[1,4,256,256]{3,2,1,0:T(8,128)(2,1)S(1)}, u32[]{:S(2)}, u32[]{:S(2)}) collective-permute-start(bf16[1,4,256,256]{3,2,1,0:T(8,128)(2,1)} %get-tuple-element.40.refs_0_), channel_id=1, source_target_pairs={{4,12},{6,14},{8,0},{10,2},{12,20},{14,22},{16,8},{18,10},{20,28},... | collective-permute-start | bytes 1572872 | tf_op jit(solution)/shard_map/ppermute | solution.py:358
  10.8 22.4 %collective-permute-start.3 = (bf16[1,4,256,256]{3,2,1,0:T(8,128)(2,1)}, bf16[1,4,256,256]{3,2,1,0:T(8,128)(2,1)S(1)}, u32[]{:S(2)}, u32[]{:S(2)}) collective-permute-start(bf16[1,4,256,256]{3,2,1,0:T(8,128)(2,1)} %get-tuple-element.39), channel_id=1, source_target_pairs={{0,6},{2,4},{4,2},{6,0},{8,14},{10,12},{12,10},{14,8},{16,22},{18,... | collective-permute-start | bytes 1572872 | tf_op jit(solution)/shard_map/ppermute | solution.py:358
  22.5 25.7 %copy-start.4 = (bf16[1,4,256,256]{3,2,1,0:T(8,128)(2,1)}, bf16[1,4,256,256]{3,2,1,0:T(8,128)(2,1)S(1)}, u32[]{:S(2)}) copy-start(bf16[1,4,256,256]{3,2,1,0:T(8,128)(2,1)S(1)} %collective-permute-done.1.refs_2_) | copy-start | bytes 1572868
  22.5 41.3 %copy-start.2 = (bf16[2,4,256,256]{3,2,1,0:T(8,128)(2,1)}, bf16[2,4,256,256]{3,2,1,0:T(8,128)(2,1)S(1)}, u32[]{:S(2)}) copy-start(bf16[2,4,256,256]{3,2,1,0:T(8,128)(2,1)S(1)} %collective-permute-done.refs_1_) | copy-start | bytes 3145732
  22.5 14.5 %collective-permute-start.9 = (bf16[1,4,256,256]{3,2,1,0:T(8,128)(2,1)S(1)}, bf16[1,4,256,256]{3,2,1,0:T(8,128)(2,1)S(1)}, u32[]{:S(2)}, u32[]{:S(2)}) collective-permute-start(bf16[1,4,256,256]{3,2,1,0:T(8,128)(2,1)S(1)} %collective-permute-done.1.refs_2_), channel_id=1, source_target_pairs={{0,8},{2,10},{8,16},{10,18},{12,4},{14,6},{16,24},{18,26},{20,12},... | collective-permute-start | bytes 1572872 | tf_op jit(solution)/shard_map/ppermute | solution.py:358
  26.4 16.2 %collective-permute-start.7 = (bf16[1,4,256,256]{3,2,1,0:T(8,128)(2,1)}, bf16[1,4,256,256]{3,2,1,0:T(8,128)(2,1)S(1)}, u32[]{:S(2)}, u32[]{:S(2)}) collective-permute-start(bf16[1,4,256,256]{3,2,1,0:T(8,128)(2,1)} %get-tuple-element.44), channel_id=1, source_target_pairs={{4,14},{6,12},{8,2},{10,0},{12,22},{14,20},{16,10},{18,8},{20,30},... | collective-permute-start | bytes 1572872 | tf_op jit(solution)/shard_map/ppermute | solution.py:358
  27.7 24.7 %copy-start.5 = (bf16[1,4,256,256]{3,2,1,0:T(8,128)(2,1)}, bf16[1,4,256,256]{3,2,1,0:T(8,128)(2,1)S(1)}, u32[]{:S(2)}) copy-start(bf16[1,4,256,256]{3,2,1,0:T(8,128)(2,1)S(1)} %collective-permute-done.4.refs_4_) | copy-start | bytes 1572868
  33.2 25.2 %copy-start.6 = (bf16[1,4,256,256]{3,2,1,0:T(8,128)(2,1)}, bf16[1,4,256,256]{3,2,1,0:T(8,128)(2,1)S(1)}, u32[]{:S(2)}) copy-start(bf16[1,4,256,256]{3,2,1,0:T(8,128)(2,1)S(1)} %collective-permute-done.3.refs_3_) | copy-start | bytes 1572868
  33.2 15.0 %collective-permute-start.2 = (bf16[1,4,256,256]{3,2,1,0:T(8,128)(2,1)}, bf16[1,4,256,256]{3,2,1,0:T(8,128)(2,1)S(1)}, u32[]{:S(2)}, u32[]{:S(2)}) collective-permute-start(bf16[1,4,256,256]{3,2,1,0:T(8,128)(2,1)} %get-tuple-element.37), channel_id=1, source_target_pairs={{0,4},{2,6},{4,0},{6,2},{8,12},{10,14},{12,8},{14,10},{16,20},{18,... | collective-permute-start | bytes 1572872 | tf_op jit(solution)/shard_map/ppermute | solution.py:358
  34.8 23.7 %collective-permute-start.5 = (bf16[1,4,256,256]{3,2,1,0:T(8,128)(2,1)}, bf16[1,4,256,256]{3,2,1,0:T(8,128)(2,1)}, u32[]{:S(2)}, u32[]{:S(2)}) collective-permute-start(bf16[1,4,256,256]{3,2,1,0:T(8,128)(2,1)} %get-tuple-element.41), channel_id=1, source_target_pairs={{0,6},{2,4},{4,2},{6,0},{8,14},{10,12},{12,10},{14,8},{16,22},{18,... | collective-permute-start | bytes 1572872 | tf_op jit(solution)/shard_map/ppermute | solution.py:358
  36.9 21.5 %copy-start.7 = (bf16[1,4,256,256]{3,2,1,0:T(8,128)(2,1)}, bf16[1,4,256,256]{3,2,1,0:T(8,128)(2,1)S(1)}, u32[]{:S(2)}) copy-start(bf16[1,4,256,256]{3,2,1,0:T(8,128)(2,1)S(1)} %collective-permute-done.9.refs_6_) | copy-start | bytes 1572868
  36.9 21.5 %collective-permute-start.11 = (bf16[1,4,256,256]{3,2,1,0:T(8,128)(2,1)S(1)}, bf16[1,4,256,256]{3,2,1,0:T(8,128)(2,1)S(1)}, u32[]{:S(2)}, u32[]{:S(2)}) collective-permute-start(bf16[1,4,256,256]{3,2,1,0:T(8,128)(2,1)S(1)} %collective-permute-done.3.refs_3_), channel_id=1, source_target_pairs={{0,8},{2,10},{8,16},{10,18},{12,4},{14,6},{16,24},{18,26},{20,12},... | collective-permute-start | bytes 1572872 | tf_op jit(solution)/shard_map/ppermute | solution.py:358
  41.4 34.3 %collective-permute-start.6 = (bf16[1,4,256,256]{3,2,1,0:T(8,128)(2,1)}, bf16[1,4,256,256]{3,2,1,0:T(8,128)(2,1)}, u32[]{:S(2)}, u32[]{:S(2)}) collective-permute-start(bf16[1,4,256,256]{3,2,1,0:T(8,128)(2,1)} %get-tuple-element.42.refs_0_), channel_id=1, source_target_pairs={{4,12},{6,14},{8,0},{10,2},{12,20},{14,22},{16,8},{18,10},{20,28},... | collective-permute-start | bytes 1572872 | tf_op jit(solution)/shard_map/ppermute | solution.py:358
  42.7 33.0 %collective-permute-start.8 = (bf16[1,4,256,256]{3,2,1,0:T(8,128)(2,1)}, bf16[1,4,256,256]{3,2,1,0:T(8,128)(2,1)}, u32[]{:S(2)}, u32[]{:S(2)}) collective-permute-start(bf16[1,4,256,256]{3,2,1,0:T(8,128)(2,1)} %get-tuple-element.45), channel_id=1, source_target_pairs={{4,14},{6,12},{8,2},{10,0},{12,22},{14,20},{16,10},{18,8},{20,30},... | collective-permute-start | bytes 1572872 | tf_op jit(solution)/shard_map/ppermute | solution.py:358
  48.2 27.6 %copy-start.3 = (bf16[1,4,256,256]{3,2,1,0:T(8,128)(2,1)}, bf16[1,4,256,256]{3,2,1,0:T(8,128)(2,1)S(1)}, u32[]{:S(2)}) copy-start(bf16[1,4,256,256]{3,2,1,0:T(8,128)(2,1)S(1)} %collective-permute-done.2.refs_2_) | copy-start | bytes 1572868
  48.2 27.6 %collective-permute-start.10 = (bf16[1,4,256,256]{3,2,1,0:T(8,128)(2,1)S(1)}, bf16[1,4,256,256]{3,2,1,0:T(8,128)(2,1)}, u32[]{:S(2)}, u32[]{:S(2)}) collective-permute-start(bf16[1,4,256,256]{3,2,1,0:T(8,128)(2,1)S(1)} %collective-permute-done.2.refs_2_), channel_id=1, source_target_pairs={{0,8},{2,10},{8,16},{10,18},{12,4},{14,6},{16,24},{18,26},{20,12},... | collective-permute-start | bytes 1572872 | tf_op jit(solution)/shard_map/ppermute | solution.py:358
  58.5 17.3 %collective-permute-start.12 = (bf16[1,4,256,256]{3,2,1,0:T(8,128)(2,1)}, bf16[1,4,256,256]{3,2,1,0:T(8,128)(2,1)}, u32[]{:S(2)}, u32[]{:S(2)}) collective-permute-start(bf16[1,4,256,256]{3,2,1,0:T(8,128)(2,1)} %collective-permute-done.5.refs_3_), channel_id=1, source_target_pairs={{0,8},{2,10},{8,16},{10,18},{12,4},{14,6},{16,24},{18,26},{20,12},... | collective-permute-start | bytes 1572872 | tf_op jit(solution)/shard_map/ppermute | solution.py:358
  87.7 2.7 %collective-permute-start.13 = (bf16[2,4,208,256]{3,2,1,0:T(8,128)(2,1)}, bf16[2,4,208,256]{3,2,1,0:T(8,128)(2,1)S(1)}, u32[]{:S(2)}, u32[]{:S(2)}) collective-permute-start(bf16[2,4,208,256]{3,2,1,0:T(8,128)(2,1)} %get-tuple-element.54), channel_id=1, source_target_pairs={{0,2},{2,0},{4,6},{6,4},{8,10},{10,8},{12,14},{14,12},{16,18},{18,... | collective-permute-start | bytes 2555912 | tf_op jit(solution)/shard_map/ppermute | solution.py:358
  92.7 8.2 %collective-permute-start.14 = (bf16[4,208,128]{2,1,0:T(8,128)(2,1)S(1)}, bf16[4,208,128]{2,1,0:T(8,128)(2,1)S(1)}, u32[]{:S(2)}, u32[]{:S(2)}) collective-permute-start(bf16[4,208,128]{2,1,0:T(8,128)(2,1)S(1)} %get-tuple-element.56), channel_id=1, source_target_pairs={{0,1},{1,0},{2,3},{3,2},{4,5},{5,4},{6,7},{7,6},{8,9},{9,8},{10,11... | collective-permute-start | bytes 638984 | tf_op jit(solution)/shard_map/ppermute | solution.py:402
  94.3 11.6 %collective-permute-start.15 = (bf16[4,208,128]{2,1,0:T(8,128)(2,1)S(1)}, bf16[4,208,128]{2,1,0:T(8,128)(2,1)S(1)}, u32[]{:S(2)}, u32[]{:S(2)}) collective-permute-start(bf16[4,208,128]{2,1,0:T(8,128)(2,1)S(1)} %get-tuple-element.57), channel_id=1, source_target_pairs={{0,4},{1,5},{2,6},{3,7},{4,0},{5,1},{6,2},{7,3},{8,12},{9,13},{10,... | collective-permute-start | bytes 638984 | tf_op jit(solution)/shard_map/ppermute | solution.py:402
  95.5 10.4 %collective-permute-start.16 = (bf16[4,208,128]{2,1,0:T(8,128)(2,1)S(1)}, bf16[4,208,128]{2,1,0:T(8,128)(2,1)S(1)}, u32[]{:S(2)}, u32[]{:S(2)}) collective-permute-start(bf16[4,208,128]{2,1,0:T(8,128)(2,1)S(1)} %get-tuple-element.58), channel_id=1, source_target_pairs={{0,5},{1,4},{2,7},{3,6},{4,1},{5,0},{6,3},{7,2},{8,13},{9,12},{10,... | collective-permute-start | bytes 638984 | tf_op jit(solution)/shard_map/ppermute | solution.py:402
  106.0 5.4 %collective-permute-start.17 = (bf16[2,208,128]{2,1,0:T(8,128)(2,1)S(1)}, bf16[2,208,128]{2,1,0:T(8,128)(2,1)S(1)}, u32[]{:S(2)}, u32[]{:S(2)}) collective-permute-start(bf16[2,208,128]{2,1,0:T(8,128)(2,1)S(1)} %get-tuple-element.60), channel_id=1, source_target_pairs={{0,8},{2,10},{8,16},{10,18},{16,24},{18,26},{1,9},{3,11},{9,17},{1... | collective-permute-start | bytes 319496 | tf_op jit(solution)/shard_map/ppermute | solution.py:358
  (4 other events, 41.1 us)

commit v4 on v3

--- a/solution.py
+++ b/solution.py
@@ -379,10 +379,10 @@
     core_came = swap(core, 1)
     near00 = near(own0, 0)
     near01 = near(core0, 1)
-    y12_came = swap(after(y12, y02_came, core_came), 2)
+    y12_came = swap(y12, 2)
     far02 = forward(after(y02_came, core_came))
     near10 = near(after(own1, near00), 0)
-    y13_came = swap(after(y13, y03_came, near00), 3)
+    y13_came = swap(after(y13, y02_came), 3)
     far03 = forward(after(y03_came, near00, far02))
     near11 = near(after(core1, near01), 1)
     far12 = forward(after(y12_came, far02))

time: 113 us -> 112 us (level)
  waiting for transfers between devices: 41.3 us -> 38.7 us
  starting transfers between devices: 36.6 us -> 38.3 us
    ppermute x15, waiting for transfers between devices: 31.7 us -> 28.7 us  [move(): return lax.ppermute(value, 'blk', pairs)]
    ppermute x15, starting transfers between devices: 33.1 us -> 34.7 us  [move(): return lax.ppermute(value, 'blk', pairs)]
  transfers between devices with their start and end apart: 18 -> 18, of which waited for: 9 -> 11; matrix products, arithmetic and copies ran while one was open for 1% -> 1% of each run, Pallas kernels for 11% -> 11%
where the time goes in v4:
time: 112 us
  waiting for transfers between devices  38.7 us (35%)
  starting transfers between devices  38.3 us (34%)
  Pallas kernels  33.1 us (30%)
  local copies, waits for them, and re-layouts  1.19 us (1%)
    ppermute x15, starting transfers between devices, move(): return lax.ppermute(value, 'blk', pairs)  34.7 us
    ppermute x15, waiting for transfers between devices, move(): return lax.ppermute(value, 'blk', pairs)  28.7 us
    pallas_call x2, Pallas kernels, correlate(): pl.pallas_call(functools.partial(correlate_kernel, pairs, places, part),...  23.9 us
    ppermute x3, waiting for transfers between devices, both(): return lax.ppermute(value, ('blk', 'frq'), pairs)  10 us
    pallas_call x1, Pallas kernels, whiten(): pl.pallas_call(functools.partial(whiten_kernel, items, tile), in_specs=[p...  6.36 us
    ppermute x3, starting transfers between devices, both(): return lax.ppermute(value, ('blk', 'frq'), pairs)  3.63 us
  transfers between devices with their start and end apart: 18, of which 11 were waited for; matrix products, arithmetic and copies ran while one was open for 1% of the time, Pallas kernels for 11%

profile of v4, /device:TPU:0, one launch (start us, length us, event | category | flops | bytes accessed | tf_op | source)
XLA Modules:
  0.0 112.0 jit_solution(1173549044914147450)
XLA Ops:
  0.0 6.4 %whiten.1 = (bf16[1,4,256,256]{3,2,1,0:T(8,128)(2,1)}, bf16[1,4,256,256]{3,2,1,0:T(8,128)(2,1)}, bf16[1,4,256,256]{3,2,1,0:T(8,128)(2,1)}, bf16[1,4,256,256]{3,2...) custom-call(s32[1,256]{1,0:T(1,128)} %bitcast.6, ...), custom_call_target="tpu_custom_call" | custom-call | bytes 1000 | tf_op jit(solution)/shard_map/whiten/pallas_call | solution.py:107
  6.9 2.6 %collective-permute-start.2 = (bf16[1,4,256,256]{3,2,1,0:T(8,128)(2,1)}, bf16[1,4,256,256]{3,2,1,0:T(8,128)(2,1)S(1)}, u32[]{:S(2)}, u32[]{:S(2)}) collective-permute-start(bf16[1,4,256,256]{3,2,1,0:T(8,128)(2,1)} %get-tuple-element.36), channel_id=1, source_target_pairs={{0,4},{2,6},{4,0},{6,2},{8,12},{10,14},{12,8},{14,10},{16,20},{18,... | collective-permute-start | bytes 1572872 | tf_op jit(solution)/shard_map/ppermute | solution.py:358
  10.8 2.3 %collective-permute-start.10 = (bf16[1,4,256,256]{3,2,1,0:T(8,128)(2,1)}, bf16[1,4,256,256]{3,2,1,0:T(8,128)(2,1)S(1)}, u32[]{:S(2)}, u32[]{:S(2)}) collective-permute-start(bf16[1,4,256,256]{3,2,1,0:T(8,128)(2,1)} %get-tuple-element.45), channel_id=1, source_target_pairs={{0,6},{2,4},{4,2},{6,0},{8,14},{10,12},{12,10},{14,8},{16,22},{18,... | collective-permute-start | bytes 1572872 | tf_op jit(solution)/shard_map/ppermute | solution.py:358
  13.1 9.4 %collective-permute-done.2.refs_2_ = bf16[1,4,256,256]{3,2,1,0:T(8,128)(2,1)S(1)} collective-permute-done((bf16[1,4,256,256]{3,2,1,0:T(8,128)(2,1)}, bf16[1,4,256,256]{3,2,1,0:T(8,128)(2,1)S(1)}, u32[]{:S(2)}, u32[]{:S(2)}) %collective-permute-start.2) | collective-permute-done | bytes 524320 | tf_op jit(solution)/shard_map/ppermute | solution.py:358
  22.5 3.9 %collective-permute-start.8 = (bf16[1,4,256,256]{3,2,1,0:T(8,128)(2,1)S(1)}, bf16[1,4,256,256]{3,2,1,0:T(8,128)(2,1)S(1)}, u32[]{:S(2)}, u32[]{:S(2)}) collective-permute-start(bf16[1,4,256,256]{3,2,1,0:T(8,128)(2,1)S(1)} %collective-permute-done.2.refs_2_), channel_id=1, source_target_pairs={{0,8},{2,10},{8,16},{10,18},{12,4},{14,6},{16,24},{18,26},{20,12},... | collective-permute-start | bytes 1572872 | tf_op jit(solution)/shard_map/ppermute | solution.py:358
  26.4 1.3 %collective-permute-start.6 = (bf16[1,4,256,256]{3,2,1,0:T(8,128)(2,1)}, bf16[1,4,256,256]{3,2,1,0:T(8,128)(2,1)S(1)}, u32[]{:S(2)}, u32[]{:S(2)}) collective-permute-start(bf16[1,4,256,256]{3,2,1,0:T(8,128)(2,1)} %get-tuple-element.41), channel_id=1, source_target_pairs={{4,14},{6,12},{8,2},{10,0},{12,22},{14,20},{16,10},{18,8},{20,30},... | collective-permute-start | bytes 1572872 | tf_op jit(solution)/shard_map/ppermute | solution.py:358
  30.2 3.1 %collective-permute-done.10.refs_3_ = bf16[1,4,256,256]{3,2,1,0:T(8,128)(2,1)S(1)} collective-permute-done((bf16[1,4,256,256]{3,2,1,0:T(8,128)(2,1)}, bf16[1,4,256,256]{3,2,1,0:T(8,128)(2,1)S(1)}, u32[]{:S(2)}, u32[]{:S(2)}) %collective-permute-start.10) | collective-permute-done | bytes 524320 | tf_op jit(solution)/shard_map/ppermute | solution.py:358
  33.3 3.6 %collective-permute-done.8.refs_6_ = bf16[1,4,256,256]{3,2,1,0:T(8,128)(2,1)S(1)} collective-permute-done((bf16[1,4,256,256]{3,2,1,0:T(8,128)(2,1)S(1)}, bf16[1,4,256,256]{3,2,1,0:T(8,128)(2,1)S(1)}, u32[]{:S(2)}, u32[]{:S(2)}) %collective-permute-start.8) | collective-permute-done | bytes 524320 | tf_op jit(solution)/shard_map/ppermute | solution.py:358
  36.9 4.4 %collective-permute-start.11 = (bf16[1,4,256,256]{3,2,1,0:T(8,128)(2,1)S(1)}, bf16[1,4,256,256]{3,2,1,0:T(8,128)(2,1)S(1)}, u32[]{:S(2)}, u32[]{:S(2)}) collective-permute-start(bf16[1,4,256,256]{3,2,1,0:T(8,128)(2,1)S(1)} %collective-permute-done.10.refs_3_), channel_id=1, source_target_pairs={{0,8},{2,10},{8,16},{10,18},{12,4},{14,6},{16,24},{18,26},{20,12},... | collective-permute-start | bytes 1572872 | tf_op jit(solution)/shard_map/ppermute | solution.py:358
  41.3 1.3 %collective-permute-start.5 = (bf16[1,4,256,256]{3,2,1,0:T(8,128)(2,1)}, bf16[1,4,256,256]{3,2,1,0:T(8,128)(2,1)}, u32[]{:S(2)}, u32[]{:S(2)}) collective-permute-start(bf16[1,4,256,256]{3,2,1,0:T(8,128)(2,1)} %get-tuple-element.39.refs_0_), channel_id=1, source_target_pairs={{4,12},{6,14},{8,0},{10,2},{12,20},{14,22},{16,8},{18,10},{20,28},... | collective-permute-start | bytes 1572872 | tf_op jit(solution)/shard_map/ppermute | solution.py:358
  42.7 1.3 %collective-permute-start.7 = (bf16[1,4,256,256]{3,2,1,0:T(8,128)(2,1)}, bf16[1,4,256,256]{3,2,1,0:T(8,128)(2,1)}, u32[]{:S(2)}, u32[]{:S(2)}) collective-permute-start(bf16[1,4,256,256]{3,2,1,0:T(8,128)(2,1)} %get-tuple-element.42), channel_id=1, source_target_pairs={{4,14},{6,12},{8,2},{10,0},{12,22},{14,20},{16,10},{18,8},{20,30},... | collective-permute-start | bytes 1572872 | tf_op jit(solution)/shard_map/ppermute | solution.py:358
  44.9 5.0 %collective-permute-start.9 = (bf16[1,4,256,256]{3,2,1,0:T(8,128)(2,1)S(1)}, bf16[1,4,256,256]{3,2,1,0:T(8,128)(2,1)}, u32[]{:S(2)}, u32[]{:S(2)}) collective-permute-start(bf16[1,4,256,256]{3,2,1,0:T(8,128)(2,1)S(1)} %collective-permute-done.1.refs_2_), channel_id=1, source_target_pairs={{0,8},{2,10},{8,16},{10,18},{12,4},{14,6},{16,24},{18,26},{20,12},... | collective-permute-start | bytes 1572872 | tf_op jit(solution)/shard_map/ppermute | solution.py:358
  50.0 5.8 %collective-permute-done.3.refs_3_ = bf16[1,4,256,256]{3,2,1,0:T(8,128)(2,1)} collective-permute-done((bf16[1,4,256,256]{3,2,1,0:T(8,128)(2,1)}, bf16[1,4,256,256]{3,2,1,0:T(8,128)(2,1)}, u32[]{:S(2)}, u32[]{:S(2)}) %collective-permute-start.3) | collective-permute-done | bytes 524320 | tf_op jit(solution)/shard_map/ppermute | solution.py:358
  55.8 4.3 %collective-permute-start.12 = (bf16[1,4,256,256]{3,2,1,0:T(8,128)(2,1)}, bf16[1,4,256,256]{3,2,1,0:T(8,128)(2,1)}, u32[]{:S(2)}, u32[]{:S(2)}) collective-permute-start(bf16[1,4,256,256]{3,2,1,0:T(8,128)(2,1)} %collective-permute-done.3.refs_3_), channel_id=1, source_target_pairs={{0,8},{2,10},{8,16},{10,18},{12,4},{14,6},{16,24},{18,26},{20,12},... | collective-permute-start | bytes 1572872 | tf_op jit(solution)/shard_map/ppermute | solution.py:358
  60.7 11.9 %correlate.2 = (bf16[2,4,208,256]{3,2,1,0:T(8,128)(2,1)}, bf16[2,4,208,256]{3,2,1,0:T(8,128)(2,1)}) custom-call(s32[2]{0:T(128)} %pad_add_fusion.pos_ref, bf16[1,4,256,256]{3,2,1,0:T(8,128)(2,1)} %get-tuple-element.38.refs_0_, bf16[2,4,256,256]{3,2,1,0:T(8,128)(2,1)} %copy-done.2, bf16[1,4,256,256]{3,2,1,0:T(8,128)(2,1)} %copy-done.4, ...), custom_call_target="tpu_custom_call" | custom-call | bytes 1000 | tf_op jit(solution)/shard_map/correlate/pallas_call | solution.py:230
  73.5 12.0 %correlate.3 = (bf16[2,4,208,256]{3,2,1,0:T(8,128)(2,1)}, bf16[2,4,208,256]{3,2,1,0:T(8,128)(2,1)}) custom-call(s32[2]{0:T(128)} %pad_add_fusion.pos_ref, bf16[1,4,256,256]{3,2,1,0:T(8,128)(2,1)} %get-tuple-element.39.refs_0_, bf16[2,4,256,256]{3,2,1,0:T(8,128)(2,1)} %copy-done.2, bf16[1,4,256,256]{3,2,1,0:T(8,128)(2,1)} %copy-done.3, ...), custom_call_target="tpu_custom_call" | custom-call | bytes 1000 | tf_op jit(solution)/shard_map/correlate/pallas_call | solution.py:230
  85.6 2.6 %collective-permute-done.13.refs_4_.refs_5_.refs_6_.refs_7_ = bf16[2,4,208,256]{3,2,1,0:T(8,128)(2,1)S(1)} collective-permute-done((bf16[2,4,208,256]{3,2,1,0:T(8,128)(2,1)}, bf16[2,4,208,256]{3,2,1,0:T(8,128)(2,1)S(1)}, u32[]{:S(2)}, u32[]{:S(2)}) %collective-permute-start.13) | collective-permute-done | bytes 852000 | tf_op jit(solution)/shard_map/ppermute | solution.py:358
  90.5 1.6 %collective-permute-start.14 = (bf16[4,208,128]{2,1,0:T(8,128)(2,1)S(1)}, bf16[4,208,128]{2,1,0:T(8,128)(2,1)S(1)}, u32[]{:S(2)}, u32[]{:S(2)}) collective-permute-start(bf16[4,208,128]{2,1,0:T(8,128)(2,1)S(1)} %get-tuple-element.54), channel_id=1, source_target_pairs={{0,1},{1,0},{2,3},{3,2},{4,5},{5,4},{6,7},{7,6},{8,9},{9,8},{10,11... | collective-permute-start | bytes 638984 | tf_op jit(solution)/shard_map/ppermute | solution.py:402
  92.1 2.1 %collective-permute-start.15 = (bf16[4,208,128]{2,1,0:T(8,128)(2,1)S(1)}, bf16[4,208,128]{2,1,0:T(8,128)(2,1)S(1)}, u32[]{:S(2)}, u32[]{:S(2)}) collective-permute-start(bf16[4,208,128]{2,1,0:T(8,128)(2,1)S(1)} %get-tuple-element.55), channel_id=1, source_target_pairs={{0,4},{1,5},{2,6},{3,7},{4,0},{5,1},{6,2},{7,3},{8,12},{9,13},{10,... | collective-permute-start | bytes 638984 | tf_op jit(solution)/shard_map/ppermute | solution.py:402
  94.2 4.5 %collective-permute-done.14.refs_1_ = bf16[4,208,128]{2,1,0:T(8,128)(2,1)S(1)} collective-permute-done((bf16[4,208,128]{2,1,0:T(8,128)(2,1)S(1)}, bf16[4,208,128]{2,1,0:T(8,128)(2,1)S(1)}, u32[]{:S(2)}, u32[]{:S(2)}) %collective-permute-start.14) | collective-permute-done | bytes 213024 | tf_op jit(solution)/shard_map/ppermute | solution.py:402
  98.7 4.8 %collective-permute-done.15.refs_2_ = bf16[4,208,128]{2,1,0:T(8,128)(2,1)S(1)} collective-permute-done((bf16[4,208,128]{2,1,0:T(8,128)(2,1)S(1)}, bf16[4,208,128]{2,1,0:T(8,128)(2,1)S(1)}, u32[]{:S(2)}, u32[]{:S(2)}) %collective-permute-start.15) | collective-permute-done | bytes 213024 | tf_op jit(solution)/shard_map/ppermute | solution.py:402
  104.3 3.9 %collective-permute-start.17 = (bf16[2,208,128]{2,1,0:T(8,128)(2,1)S(1)}, bf16[2,208,128]{2,1,0:T(8,128)(2,1)S(1)}, u32[]{:S(2)}, u32[]{:S(2)}) collective-permute-start(bf16[2,208,128]{2,1,0:T(8,128)(2,1)S(1)} %get-tuple-element.58), channel_id=1, source_target_pairs={{0,8},{2,10},{8,16},{10,18},{16,24},{18,26},{1,9},{3,11},{9,17},{1... | collective-permute-start | bytes 319496 | tf_op jit(solution)/shard_map/ppermute | solution.py:358
  108.2 2.3 %collective-permute-done.17.behind_ref = bf16[2,208,128]{2,1,0:T(8,128)(2,1)S(1)} collective-permute-done((bf16[2,208,128]{2,1,0:T(8,128)(2,1)S(1)}, bf16[2,208,128]{2,1,0:T(8,128)(2,1)S(1)}, u32[]{:S(2)}, u32[]{:S(2)}) %collective-permute-start.17) | collective-permute-done | bytes 106528 | tf_op jit(solution)/shard_map/ppermute | solution.py:358
  110.4 1.5 %finish.1 = f32[201,4,128]{2,1,0:T(4,128)} custom-call(s32[2]{0:T(128)S(1)} %copy-done.1, f32[4,208,128]{2,1,0:T(8,128)S(1)} %get-tuple-element.57.own_ref, bf16[2,208,128]{2,1,0:T(8,128)(2,1)S(1)} %collective-permute-done.17.behind_ref), custom_call_target="tpu_custom_call" | custom-call | tf_op jit(solution)/shard_map/finish/pallas_call | solution.py:311
  (39 shorter events, 10.0 us)
Async XLA Ops:
  6.4 16.1 %collective-permute-start = (bf16[2,4,256,256]{3,2,1,0:T(8,128)(2,1)}, bf16[2,4,256,256]{3,2,1,0:T(8,128)(2,1)S(1)}, u32[]{:S(2)}, u32[]{:S(2)}) collective-permute-start(bf16[2,4,256,256]{3,2,1,0:T(8,128)(2,1)} %get-tuple-element.33), channel_id=1, source_target_pairs={{0,2},{2,0},{4,6},{6,4},{8,10},{10,8},{12,14},{14,12},{16,18},{18,... | collective-permute-start | bytes 3145736 | tf_op jit(solution)/shard_map/ppermute | solution.py:358
  6.9 15.6 %collective-permute-start.2 = (bf16[1,4,256,256]{3,2,1,0:T(8,128)(2,1)}, bf16[1,4,256,256]{3,2,1,0:T(8,128)(2,1)S(1)}, u32[]{:S(2)}, u32[]{:S(2)}) collective-permute-start(bf16[1,4,256,256]{3,2,1,0:T(8,128)(2,1)} %get-tuple-element.36), channel_id=1, source_target_pairs={{0,4},{2,6},{4,0},{6,2},{8,12},{10,14},{12,8},{14,10},{16,20},{18,... | collective-permute-start | bytes 1572872 | tf_op jit(solution)/shard_map/ppermute | solution.py:358
  9.5 19.4 %collective-permute-start.4 = (bf16[1,4,256,256]{3,2,1,0:T(8,128)(2,1)}, bf16[1,4,256,256]{3,2,1,0:T(8,128)(2,1)S(1)}, u32[]{:S(2)}, u32[]{:S(2)}) collective-permute-start(bf16[1,4,256,256]{3,2,1,0:T(8,128)(2,1)} %get-tuple-element.38.refs_0_), channel_id=1, source_target_pairs={{4,12},{6,14},{8,0},{10,2},{12,20},{14,22},{16,8},{18,10},{20,28},... | collective-permute-start | bytes 1572872 | tf_op jit(solution)/shard_map/ppermute | solution.py:358
  10.8 22.5 %collective-permute-start.10 = (bf16[1,4,256,256]{3,2,1,0:T(8,128)(2,1)}, bf16[1,4,256,256]{3,2,1,0:T(8,128)(2,1)S(1)}, u32[]{:S(2)}, u32[]{:S(2)}) collective-permute-start(bf16[1,4,256,256]{3,2,1,0:T(8,128)(2,1)} %get-tuple-element.45), channel_id=1, source_target_pairs={{0,6},{2,4},{4,2},{6,0},{8,14},{10,12},{12,10},{14,8},{16,22},{18,... | collective-permute-start | bytes 1572872 | tf_op jit(solution)/shard_map/ppermute | solution.py:358
  22.5 22.5 %copy-start.4 = (bf16[1,4,256,256]{3,2,1,0:T(8,128)(2,1)}, bf16[1,4,256,256]{3,2,1,0:T(8,128)(2,1)S(1)}, u32[]{:S(2)}) copy-start(bf16[1,4,256,256]{3,2,1,0:T(8,128)(2,1)S(1)} %collective-permute-done.2.refs_2_) | copy-start | bytes 1572868
  22.5 38.2 %copy-start.2 = (bf16[2,4,256,256]{3,2,1,0:T(8,128)(2,1)}, bf16[2,4,256,256]{3,2,1,0:T(8,128)(2,1)S(1)}, u32[]{:S(2)}) copy-start(bf16[2,4,256,256]{3,2,1,0:T(8,128)(2,1)S(1)} %collective-permute-done.refs_1_) | copy-start | bytes 3145732
  22.5 14.5 %collective-permute-start.8 = (bf16[1,4,256,256]{3,2,1,0:T(8,128)(2,1)S(1)}, bf16[1,4,256,256]{3,2,1,0:T(8,128)(2,1)S(1)}, u32[]{:S(2)}, u32[]{:S(2)}) collective-permute-start(bf16[1,4,256,256]{3,2,1,0:T(8,128)(2,1)S(1)} %collective-permute-done.2.refs_2_), channel_id=1, source_target_pairs={{0,8},{2,10},{8,16},{10,18},{12,4},{14,6},{16,24},{18,26},{20,12},... | collective-permute-start | bytes 1572872 | tf_op jit(solution)/shard_map/ppermute | solution.py:358
  26.4 16.2 %collective-permute-start.6 = (bf16[1,4,256,256]{3,2,1,0:T(8,128)(2,1)}, bf16[1,4,256,256]{3,2,1,0:T(8,128)(2,1)S(1)}, u32[]{:S(2)}, u32[]{:S(2)}) collective-permute-start(bf16[1,4,256,256]{3,2,1,0:T(8,128)(2,1)} %get-tuple-element.41), channel_id=1, source_target_pairs={{4,14},{6,12},{8,2},{10,0},{12,22},{14,20},{16,10},{18,8},{20,30},... | collective-permute-start | bytes 1572872 | tf_op jit(solution)/shard_map/ppermute | solution.py:358
  27.7 17.2 %collective-permute-start.1 = (bf16[1,4,256,256]{3,2,1,0:T(8,128)(2,1)}, bf16[1,4,256,256]{3,2,1,0:T(8,128)(2,1)S(1)}, u32[]{:S(2)}, u32[]{:S(2)}) collective-permute-start(bf16[1,4,256,256]{3,2,1,0:T(8,128)(2,1)} %get-tuple-element.34), channel_id=1, source_target_pairs={{0,4},{2,6},{4,0},{6,2},{8,12},{10,14},{12,8},{14,10},{16,20},{18,... | collective-permute-start | bytes 1572872 | tf_op jit(solution)/shard_map/ppermute | solution.py:358
  28.9 21.1 %copy-start.5 = (bf16[1,4,256,256]{3,2,1,0:T(8,128)(2,1)}, bf16[1,4,256,256]{3,2,1,0:T(8,128)(2,1)S(1)}, u32[]{:S(2)}) copy-start(bf16[1,4,256,256]{3,2,1,0:T(8,128)(2,1)S(1)} %collective-permute-done.4.refs_4_) | copy-start | bytes 1572868
  28.9 26.8 %collective-permute-start.3 = (bf16[1,4,256,256]{3,2,1,0:T(8,128)(2,1)}, bf16[1,4,256,256]{3,2,1,0:T(8,128)(2,1)}, u32[]{:S(2)}, u32[]{:S(2)}) collective-permute-start(bf16[1,4,256,256]{3,2,1,0:T(8,128)(2,1)} %get-tuple-element.37), channel_id=1, source_target_pairs={{0,6},{2,4},{4,2},{6,0},{8,14},{10,12},{12,10},{14,8},{16,22},{18,... | collective-permute-start | bytes 1572872 | tf_op jit(solution)/shard_map/ppermute | solution.py:358
  33.3 22.5 %copy-start.6 = (bf16[1,4,256,256]{3,2,1,0:T(8,128)(2,1)}, bf16[1,4,256,256]{3,2,1,0:T(8,128)(2,1)S(1)}, u32[]{:S(2)}) copy-start(bf16[1,4,256,256]{3,2,1,0:T(8,128)(2,1)S(1)} %collective-permute-done.10.refs_3_) | copy-start | bytes 1572868
  36.9 18.8 %copy-start.7 = (bf16[1,4,256,256]{3,2,1,0:T(8,128)(2,1)}, bf16[1,4,256,256]{3,2,1,0:T(8,128)(2,1)S(1)}, u32[]{:S(2)}) copy-start(bf16[1,4,256,256]{3,2,1,0:T(8,128)(2,1)S(1)} %collective-permute-done.8.refs_6_) | copy-start | bytes 1572868
  36.9 18.8 %collective-permute-start.11 = (bf16[1,4,256,256]{3,2,1,0:T(8,128)(2,1)S(1)}, bf16[1,4,256,256]{3,2,1,0:T(8,128)(2,1)S(1)}, u32[]{:S(2)}, u32[]{:S(2)}) collective-permute-start(bf16[1,4,256,256]{3,2,1,0:T(8,128)(2,1)S(1)} %collective-permute-done.10.refs_3_), channel_id=1, source_target_pairs={{0,8},{2,10},{8,16},{10,18},{12,4},{14,6},{16,24},{18,26},{20,12},... | collective-permute-start | bytes 1572872 | tf_op jit(solution)/shard_map/ppermute | solution.py:358
  41.3 31.2 %collective-permute-start.5 = (bf16[1,4,256,256]{3,2,1,0:T(8,128)(2,1)}, bf16[1,4,256,256]{3,2,1,0:T(8,128)(2,1)}, u32[]{:S(2)}, u32[]{:S(2)}) collective-permute-start(bf16[1,4,256,256]{3,2,1,0:T(8,128)(2,1)} %get-tuple-element.39.refs_0_), channel_id=1, source_target_pairs={{4,12},{6,14},{8,0},{10,2},{12,20},{14,22},{16,8},{18,10},{20,28},... | collective-permute-start | bytes 1572872 | tf_op jit(solution)/shard_map/ppermute | solution.py:358
  42.7 29.9 %collective-permute-start.7 = (bf16[1,4,256,256]{3,2,1,0:T(8,128)(2,1)}, bf16[1,4,256,256]{3,2,1,0:T(8,128)(2,1)}, u32[]{:S(2)}, u32[]{:S(2)}) collective-permute-start(bf16[1,4,256,256]{3,2,1,0:T(8,128)(2,1)} %get-tuple-element.42), channel_id=1, source_target_pairs={{4,14},{6,12},{8,2},{10,0},{12,22},{14,20},{16,10},{18,8},{20,30},... | collective-permute-start | bytes 1572872 | tf_op jit(solution)/shard_map/ppermute | solution.py:358
  44.9 28.6 %copy-start.3 = (bf16[1,4,256,256]{3,2,1,0:T(8,128)(2,1)}, bf16[1,4,256,256]{3,2,1,0:T(8,128)(2,1)S(1)}, u32[]{:S(2)}) copy-start(bf16[1,4,256,256]{3,2,1,0:T(8,128)(2,1)S(1)} %collective-permute-done.1.refs_2_) | copy-start | bytes 1572868
  44.9 27.7 %collective-permute-start.9 = (bf16[1,4,256,256]{3,2,1,0:T(8,128)(2,1)S(1)}, bf16[1,4,256,256]{3,2,1,0:T(8,128)(2,1)}, u32[]{:S(2)}, u32[]{:S(2)}) collective-permute-start(bf16[1,4,256,256]{3,2,1,0:T(8,128)(2,1)S(1)} %collective-permute-done.1.refs_2_), channel_id=1, source_target_pairs={{0,8},{2,10},{8,16},{10,18},{12,4},{14,6},{16,24},{18,26},{20,12},... | collective-permute-start | bytes 1572872 | tf_op jit(solution)/shard_map/ppermute | solution.py:358
  55.8 17.7 %collective-permute-start.12 = (bf16[1,4,256,256]{3,2,1,0:T(8,128)(2,1)}, bf16[1,4,256,256]{3,2,1,0:T(8,128)(2,1)}, u32[]{:S(2)}, u32[]{:S(2)}) collective-permute-start(bf16[1,4,256,256]{3,2,1,0:T(8,128)(2,1)} %collective-permute-done.3.refs_3_), channel_id=1, source_target_pairs={{0,8},{2,10},{8,16},{10,18},{12,4},{14,6},{16,24},{18,26},{20,12},... | collective-permute-start | bytes 1572872 | tf_op jit(solution)/shard_map/ppermute | solution.py:358
  85.6 2.7 %collective-permute-start.13 = (bf16[2,4,208,256]{3,2,1,0:T(8,128)(2,1)}, bf16[2,4,208,256]{3,2,1,0:T(8,128)(2,1)S(1)}, u32[]{:S(2)}, u32[]{:S(2)}) collective-permute-start(bf16[2,4,208,256]{3,2,1,0:T(8,128)(2,1)} %get-tuple-element.52), channel_id=1, source_target_pairs={{0,2},{2,0},{4,6},{6,4},{8,10},{10,8},{12,14},{14,12},{16,18},{18,... | collective-permute-start | bytes 2555912 | tf_op jit(solution)/shard_map/ppermute | solution.py:358
  90.5 8.2 %collective-permute-start.14 = (bf16[4,208,128]{2,1,0:T(8,128)(2,1)S(1)}, bf16[4,208,128]{2,1,0:T(8,128)(2,1)S(1)}, u32[]{:S(2)}, u32[]{:S(2)}) collective-permute-start(bf16[4,208,128]{2,1,0:T(8,128)(2,1)S(1)} %get-tuple-element.54), channel_id=1, source_target_pairs={{0,1},{1,0},{2,3},{3,2},{4,5},{5,4},{6,7},{7,6},{8,9},{9,8},{10,11... | collective-permute-start | bytes 638984 | tf_op jit(solution)/shard_map/ppermute | solution.py:402
  92.1 11.4 %collective-permute-start.15 = (bf16[4,208,128]{2,1,0:T(8,128)(2,1)S(1)}, bf16[4,208,128]{2,1,0:T(8,128)(2,1)S(1)}, u32[]{:S(2)}, u32[]{:S(2)}) collective-permute-start(bf16[4,208,128]{2,1,0:T(8,128)(2,1)S(1)} %get-tuple-element.55), channel_id=1, source_target_pairs={{0,4},{1,5},{2,6},{3,7},{4,0},{5,1},{6,2},{7,3},{8,12},{9,13},{10,... | collective-permute-start | bytes 638984 | tf_op jit(solution)/shard_map/ppermute | solution.py:402
  94.2 10.0 %collective-permute-start.16 = (bf16[4,208,128]{2,1,0:T(8,128)(2,1)S(1)}, bf16[4,208,128]{2,1,0:T(8,128)(2,1)S(1)}, u32[]{:S(2)}, u32[]{:S(2)}) collective-permute-start(bf16[4,208,128]{2,1,0:T(8,128)(2,1)S(1)} %get-tuple-element.56), channel_id=1, source_target_pairs={{0,5},{1,4},{2,7},{3,6},{4,1},{5,0},{6,3},{7,2},{8,13},{9,12},{10,... | collective-permute-start | bytes 638984 | tf_op jit(solution)/shard_map/ppermute | solution.py:402
  104.3 6.1 %collective-permute-start.17 = (bf16[2,208,128]{2,1,0:T(8,128)(2,1)S(1)}, bf16[2,208,128]{2,1,0:T(8,128)(2,1)S(1)}, u32[]{:S(2)}, u32[]{:S(2)}) collective-permute-start(bf16[2,208,128]{2,1,0:T(8,128)(2,1)S(1)} %get-tuple-element.58), channel_id=1, source_target_pairs={{0,8},{2,10},{8,16},{10,18},{16,24},{18,26},{1,9},{3,11},{9,17},{1... | collective-permute-start | bytes 319496 | tf_op jit(solution)/shard_map/ppermute | solution.py:358
  (4 other events, 37.7 us)

commit v5 on v4

--- a/solution.py
+++ b/solution.py
@@ -81,7 +81,7 @@
             power = values[0][0] * values[0][0] + values[0][1] * values[0][1]
             for real, imag in values[1:]:
                 power = power + (real * real + imag * imag)
-            scale = valid / jnp.maximum(jnp.sqrt(power * (1.0 / windows)), 0.5)
+            scale = valid * jnp.minimum(lax.rsqrt(power * (1.0 / windows)), 2.0)
             for w in range(windows):
                 both = jnp.concatenate([values[w][half] * scale for half in range(2)], axis=1)
                 ready[at, w, rows, :] = both.astype(BF16)

time: 112 us -> 112 us (level)
  no operation moved by 1% of the time
where the time goes in v5:
time: 112 us
  waiting for transfers between devices  38.6 us (34%)
  starting transfers between devices  38.4 us (34%)
  Pallas kernels  32.8 us (29%)
  local copies, waits for them, and re-layouts  1.19 us (1%)
    ppermute x15, starting transfers between devices, move(): return lax.ppermute(value, 'blk', pairs)  34.8 us
    ppermute x15, waiting for transfers between devices, move(): return lax.ppermute(value, 'blk', pairs)  28.6 us
    pallas_call x2, Pallas kernels, correlate(): pl.pallas_call(functools.partial(correlate_kernel, pairs, places, part),...  23.9 us
    ppermute x3, waiting for transfers between devices, both(): return lax.ppermute(value, ('blk', 'frq'), pairs)  10 us
    pallas_call x1, Pallas kernels, whiten(): pl.pallas_call(functools.partial(whiten_kernel, items, tile), in_specs=[p...  6.11 us
    ppermute x3, starting transfers between devices, both(): return lax.ppermute(value, ('blk', 'frq'), pairs)  3.58 us
  transfers between devices with their start and end apart: 18, of which 11 were waited for; matrix products, arithmetic and copies ran while one was open for 1% of the time, Pallas kernels for 11%

profile of v5, /device:TPU:0, one launch (start us, length us, event | category | flops | bytes accessed | tf_op | source)
XLA Modules:
  0.0 111.7 jit_solution(1892248915648896666)
XLA Ops:
  0.0 6.1 %whiten.1 = (bf16[1,4,256,256]{3,2,1,0:T(8,128)(2,1)}, bf16[1,4,256,256]{3,2,1,0:T(8,128)(2,1)}, bf16[1,4,256,256]{3,2,1,0:T(8,128)(2,1)}, bf16[1,4,256,256]{3,2...) custom-call(s32[1,256]{1,0:T(1,128)} %bitcast.6, ...), custom_call_target="tpu_custom_call" | custom-call | bytes 1000 | tf_op jit(solution)/shard_map/whiten/pallas_call | solution.py:107
  6.6 2.6 %collective-permute-start.2 = (bf16[1,4,256,256]{3,2,1,0:T(8,128)(2,1)}, bf16[1,4,256,256]{3,2,1,0:T(8,128)(2,1)S(1)}, u32[]{:S(2)}, u32[]{:S(2)}) collective-permute-start(bf16[1,4,256,256]{3,2,1,0:T(8,128)(2,1)} %get-tuple-element.36), channel_id=1, source_target_pairs={{0,4},{2,6},{4,0},{6,2},{8,12},{10,14},{12,8},{14,10},{16,20},{18,... | collective-permute-start | bytes 1572872 | tf_op jit(solution)/shard_map/ppermute | solution.py:358
  10.5 2.3 %collective-permute-start.10 = (bf16[1,4,256,256]{3,2,1,0:T(8,128)(2,1)}, bf16[1,4,256,256]{3,2,1,0:T(8,128)(2,1)S(1)}, u32[]{:S(2)}, u32[]{:S(2)}) collective-permute-start(bf16[1,4,256,256]{3,2,1,0:T(8,128)(2,1)} %get-tuple-element.45), channel_id=1, source_target_pairs={{0,6},{2,4},{4,2},{6,0},{8,14},{10,12},{12,10},{14,8},{16,22},{18,... | collective-permute-start | bytes 1572872 | tf_op jit(solution)/shard_map/ppermute | solution.py:358
  12.8 9.4 %collective-permute-done.2.refs_2_ = bf16[1,4,256,256]{3,2,1,0:T(8,128)(2,1)S(1)} collective-permute-done((bf16[1,4,256,256]{3,2,1,0:T(8,128)(2,1)}, bf16[1,4,256,256]{3,2,1,0:T(8,128)(2,1)S(1)}, u32[]{:S(2)}, u32[]{:S(2)}) %collective-permute-start.2) | collective-permute-done | bytes 524320 | tf_op jit(solution)/shard_map/ppermute | solution.py:358
  22.2 4.0 %collective-permute-start.8 = (bf16[1,4,256,256]{3,2,1,0:T(8,128)(2,1)S(1)}, bf16[1,4,256,256]{3,2,1,0:T(8,128)(2,1)S(1)}, u32[]{:S(2)}, u32[]{:S(2)}) collective-permute-start(bf16[1,4,256,256]{3,2,1,0:T(8,128)(2,1)S(1)} %collective-permute-done.2.refs_2_), channel_id=1, source_target_pairs={{0,8},{2,10},{8,16},{10,18},{12,4},{14,6},{16,24},{18,26},{20,12},... | collective-permute-start | bytes 1572872 | tf_op jit(solution)/shard_map/ppermute | solution.py:358
  26.2 1.3 %collective-permute-start.6 = (bf16[1,4,256,256]{3,2,1,0:T(8,128)(2,1)}, bf16[1,4,256,256]{3,2,1,0:T(8,128)(2,1)S(1)}, u32[]{:S(2)}, u32[]{:S(2)}) collective-permute-start(bf16[1,4,256,256]{3,2,1,0:T(8,128)(2,1)} %get-tuple-element.41), channel_id=1, source_target_pairs={{4,14},{6,12},{8,2},{10,0},{12,22},{14,20},{16,10},{18,8},{20,30},... | collective-permute-start | bytes 1572872 | tf_op jit(solution)/shard_map/ppermute | solution.py:358
  29.9 3.1 %collective-permute-done.10.refs_3_ = bf16[1,4,256,256]{3,2,1,0:T(8,128)(2,1)S(1)} collective-permute-done((bf16[1,4,256,256]{3,2,1,0:T(8,128)(2,1)}, bf16[1,4,256,256]{3,2,1,0:T(8,128)(2,1)S(1)}, u32[]{:S(2)}, u32[]{:S(2)}) %collective-permute-start.10) | collective-permute-done | bytes 524320 | tf_op jit(solution)/shard_map/ppermute | solution.py:358
  33.0 3.7 %collective-permute-done.8.refs_6_ = bf16[1,4,256,256]{3,2,1,0:T(8,128)(2,1)S(1)} collective-permute-done((bf16[1,4,256,256]{3,2,1,0:T(8,128)(2,1)S(1)}, bf16[1,4,256,256]{3,2,1,0:T(8,128)(2,1)S(1)}, u32[]{:S(2)}, u32[]{:S(2)}) %collective-permute-start.8) | collective-permute-done | bytes 524320 | tf_op jit(solution)/shard_map/ppermute | solution.py:358
  36.7 4.4 %collective-permute-start.11 = (bf16[1,4,256,256]{3,2,1,0:T(8,128)(2,1)S(1)}, bf16[1,4,256,256]{3,2,1,0:T(8,128)(2,1)S(1)}, u32[]{:S(2)}, u32[]{:S(2)}) collective-permute-start(bf16[1,4,256,256]{3,2,1,0:T(8,128)(2,1)S(1)} %collective-permute-done.10.refs_3_), channel_id=1, source_target_pairs={{0,8},{2,10},{8,16},{10,18},{12,4},{14,6},{16,24},{18,26},{20,12},... | collective-permute-start | bytes 1572872 | tf_op jit(solution)/shard_map/ppermute | solution.py:358
  41.1 1.3 %collective-permute-start.5 = (bf16[1,4,256,256]{3,2,1,0:T(8,128)(2,1)}, bf16[1,4,256,256]{3,2,1,0:T(8,128)(2,1)}, u32[]{:S(2)}, u32[]{:S(2)}) collective-permute-start(bf16[1,4,256,256]{3,2,1,0:T(8,128)(2,1)} %get-tuple-element.39.refs_0_), channel_id=1, source_target_pairs={{4,12},{6,14},{8,0},{10,2},{12,20},{14,22},{16,8},{18,10},{20,28},... | collective-permute-start | bytes 1572872 | tf_op jit(solution)/shard_map/ppermute | solution.py:358
  42.4 1.3 %collective-permute-start.7 = (bf16[1,4,256,256]{3,2,1,0:T(8,128)(2,1)}, bf16[1,4,256,256]{3,2,1,0:T(8,128)(2,1)}, u32[]{:S(2)}, u32[]{:S(2)}) collective-permute-start(bf16[1,4,256,256]{3,2,1,0:T(8,128)(2,1)} %get-tuple-element.42), channel_id=1, source_target_pairs={{4,14},{6,12},{8,2},{10,0},{12,22},{14,20},{16,10},{18,8},{20,30},... | collective-permute-start | bytes 1572872 | tf_op jit(solution)/shard_map/ppermute | solution.py:358
  44.6 5.1 %collective-permute-start.9 = (bf16[1,4,256,256]{3,2,1,0:T(8,128)(2,1)S(1)}, bf16[1,4,256,256]{3,2,1,0:T(8,128)(2,1)}, u32[]{:S(2)}, u32[]{:S(2)}) collective-permute-start(bf16[1,4,256,256]{3,2,1,0:T(8,128)(2,1)S(1)} %collective-permute-done.1.refs_2_), channel_id=1, source_target_pairs={{0,8},{2,10},{8,16},{10,18},{12,4},{14,6},{16,24},{18,26},{20,12},... | collective-permute-start | bytes 1572872 | tf_op jit(solution)/shard_map/ppermute | solution.py:358
  49.7 5.7 %collective-permute-done.3.refs_3_ = bf16[1,4,256,256]{3,2,1,0:T(8,128)(2,1)} collective-permute-done((bf16[1,4,256,256]{3,2,1,0:T(8,128)(2,1)}, bf16[1,4,256,256]{3,2,1,0:T(8,128)(2,1)}, u32[]{:S(2)}, u32[]{:S(2)}) %collective-permute-start.3) | collective-permute-done | bytes 524320 | tf_op jit(solution)/shard_map/ppermute | solution.py:358
  55.5 4.4 %collective-permute-start.12 = (bf16[1,4,256,256]{3,2,1,0:T(8,128)(2,1)}, bf16[1,4,256,256]{3,2,1,0:T(8,128)(2,1)}, u32[]{:S(2)}, u32[]{:S(2)}) collective-permute-start(bf16[1,4,256,256]{3,2,1,0:T(8,128)(2,1)} %collective-permute-done.3.refs_3_), channel_id=1, source_target_pairs={{0,8},{2,10},{8,16},{10,18},{12,4},{14,6},{16,24},{18,26},{20,12},... | collective-permute-start | bytes 1572872 | tf_op jit(solution)/shard_map/ppermute | solution.py:358
  60.5 11.9 %correlate.2 = (bf16[2,4,208,256]{3,2,1,0:T(8,128)(2,1)}, bf16[2,4,208,256]{3,2,1,0:T(8,128)(2,1)}) custom-call(s32[2]{0:T(128)} %pad_add_fusion.pos_ref, bf16[1,4,256,256]{3,2,1,0:T(8,128)(2,1)} %get-tuple-element.38.refs_0_, bf16[2,4,256,256]{3,2,1,0:T(8,128)(2,1)} %copy-done.2, bf16[1,4,256,256]{3,2,1,0:T(8,128)(2,1)} %copy-done.4, ...), custom_call_target="tpu_custom_call" | custom-call | bytes 1000 | tf_op jit(solution)/shard_map/correlate/pallas_call | solution.py:230
  73.3 12.0 %correlate.3 = (bf16[2,4,208,256]{3,2,1,0:T(8,128)(2,1)}, bf16[2,4,208,256]{3,2,1,0:T(8,128)(2,1)}) custom-call(s32[2]{0:T(128)} %pad_add_fusion.pos_ref, bf16[1,4,256,256]{3,2,1,0:T(8,128)(2,1)} %get-tuple-element.39.refs_0_, bf16[2,4,256,256]{3,2,1,0:T(8,128)(2,1)} %copy-done.2, bf16[1,4,256,256]{3,2,1,0:T(8,128)(2,1)} %copy-done.3, ...), custom_call_target="tpu_custom_call" | custom-call | bytes 1000 | tf_op jit(solution)/shard_map/correlate/pallas_call | solution.py:230
  85.4 2.6 %collective-permute-done.13.refs_4_.refs_5_.refs_6_.refs_7_ = bf16[2,4,208,256]{3,2,1,0:T(8,128)(2,1)S(1)} collective-permute-done((bf16[2,4,208,256]{3,2,1,0:T(8,128)(2,1)}, bf16[2,4,208,256]{3,2,1,0:T(8,128)(2,1)S(1)}, u32[]{:S(2)}, u32[]{:S(2)}) %collective-permute-start.13) | collective-permute-done | bytes 852000 | tf_op jit(solution)/shard_map/ppermute | solution.py:358
  90.3 1.6 %collective-permute-start.14 = (bf16[4,208,128]{2,1,0:T(8,128)(2,1)S(1)}, bf16[4,208,128]{2,1,0:T(8,128)(2,1)S(1)}, u32[]{:S(2)}, u32[]{:S(2)}) collective-permute-start(bf16[4,208,128]{2,1,0:T(8,128)(2,1)S(1)} %get-tuple-element.54), channel_id=1, source_target_pairs={{0,1},{1,0},{2,3},{3,2},{4,5},{5,4},{6,7},{7,6},{8,9},{9,8},{10,11... | collective-permute-start | bytes 638984 | tf_op jit(solution)/shard_map/ppermute | solution.py:402
  91.8 2.0 %collective-permute-start.15 = (bf16[4,208,128]{2,1,0:T(8,128)(2,1)S(1)}, bf16[4,208,128]{2,1,0:T(8,128)(2,1)S(1)}, u32[]{:S(2)}, u32[]{:S(2)}) collective-permute-start(bf16[4,208,128]{2,1,0:T(8,128)(2,1)S(1)} %get-tuple-element.55), channel_id=1, source_target_pairs={{0,4},{1,5},{2,6},{3,7},{4,0},{5,1},{6,2},{7,3},{8,12},{9,13},{10,... | collective-permute-start | bytes 638984 | tf_op jit(solution)/shard_map/ppermute | solution.py:402
  93.9 4.6 %collective-permute-done.14.refs_1_ = bf16[4,208,128]{2,1,0:T(8,128)(2,1)S(1)} collective-permute-done((bf16[4,208,128]{2,1,0:T(8,128)(2,1)S(1)}, bf16[4,208,128]{2,1,0:T(8,128)(2,1)S(1)}, u32[]{:S(2)}, u32[]{:S(2)}) %collective-permute-start.14) | collective-permute-done | bytes 213024 | tf_op jit(solution)/shard_map/ppermute | solution.py:402
  98.4 4.7 %collective-permute-done.15.refs_2_ = bf16[4,208,128]{2,1,0:T(8,128)(2,1)S(1)} collective-permute-done((bf16[4,208,128]{2,1,0:T(8,128)(2,1)S(1)}, bf16[4,208,128]{2,1,0:T(8,128)(2,1)S(1)}, u32[]{:S(2)}, u32[]{:S(2)}) %collective-permute-start.15) | collective-permute-done | bytes 213024 | tf_op jit(solution)/shard_map/ppermute | solution.py:402
  104.0 3.9 %collective-permute-start.17 = (bf16[2,208,128]{2,1,0:T(8,128)(2,1)S(1)}, bf16[2,208,128]{2,1,0:T(8,128)(2,1)S(1)}, u32[]{:S(2)}, u32[]{:S(2)}) collective-permute-start(bf16[2,208,128]{2,1,0:T(8,128)(2,1)S(1)} %get-tuple-element.58), channel_id=1, source_target_pairs={{0,8},{2,10},{8,16},{10,18},{16,24},{18,26},{1,9},{3,11},{9,17},{1... | collective-permute-start | bytes 319496 | tf_op jit(solution)/shard_map/ppermute | solution.py:358
  107.9 2.3 %collective-permute-done.17.behind_ref = bf16[2,208,128]{2,1,0:T(8,128)(2,1)S(1)} collective-permute-done((bf16[2,208,128]{2,1,0:T(8,128)(2,1)S(1)}, bf16[2,208,128]{2,1,0:T(8,128)(2,1)S(1)}, u32[]{:S(2)}, u32[]{:S(2)}) %collective-permute-start.17) | collective-permute-done | bytes 106528 | tf_op jit(solution)/shard_map/ppermute | solution.py:358
  110.2 1.5 %finish.1 = f32[201,4,128]{2,1,0:T(4,128)} custom-call(s32[2]{0:T(128)S(1)} %copy-done.1, f32[4,208,128]{2,1,0:T(8,128)S(1)} %get-tuple-element.57.own_ref, bf16[2,208,128]{2,1,0:T(8,128)(2,1)S(1)} %collective-permute-done.17.behind_ref), custom_call_target="tpu_custom_call" | custom-call | tf_op jit(solution)/shard_map/finish/pallas_call | solution.py:311
  (39 shorter events, 9.9 us)
Async XLA Ops:
  6.1 16.1 %collective-permute-start = (bf16[2,4,256,256]{3,2,1,0:T(8,128)(2,1)}, bf16[2,4,256,256]{3,2,1,0:T(8,128)(2,1)S(1)}, u32[]{:S(2)}, u32[]{:S(2)}) collective-permute-start(bf16[2,4,256,256]{3,2,1,0:T(8,128)(2,1)} %get-tuple-element.33), channel_id=1, source_target_pairs={{0,2},{2,0},{4,6},{6,4},{8,10},{10,8},{12,14},{14,12},{16,18},{18,... | collective-permute-start | bytes 3145736 | tf_op jit(solution)/shard_map/ppermute | solution.py:358
  6.6 15.5 %collective-permute-start.2 = (bf16[1,4,256,256]{3,2,1,0:T(8,128)(2,1)}, bf16[1,4,256,256]{3,2,1,0:T(8,128)(2,1)S(1)}, u32[]{:S(2)}, u32[]{:S(2)}) collective-permute-start(bf16[1,4,256,256]{3,2,1,0:T(8,128)(2,1)} %get-tuple-element.36), channel_id=1, source_target_pairs={{0,4},{2,6},{4,0},{6,2},{8,12},{10,14},{12,8},{14,10},{16,20},{18,... | collective-permute-start | bytes 1572872 | tf_op jit(solution)/shard_map/ppermute | solution.py:358
  9.2 19.4 %collective-permute-start.4 = (bf16[1,4,256,256]{3,2,1,0:T(8,128)(2,1)}, bf16[1,4,256,256]{3,2,1,0:T(8,128)(2,1)S(1)}, u32[]{:S(2)}, u32[]{:S(2)}) collective-permute-start(bf16[1,4,256,256]{3,2,1,0:T(8,128)(2,1)} %get-tuple-element.38.refs_0_), channel_id=1, source_target_pairs={{4,12},{6,14},{8,0},{10,2},{12,20},{14,22},{16,8},{18,10},{20,28},... | collective-permute-start | bytes 1572872 | tf_op jit(solution)/shard_map/ppermute | solution.py:358
  10.5 22.5 %collective-permute-start.10 = (bf16[1,4,256,256]{3,2,1,0:T(8,128)(2,1)}, bf16[1,4,256,256]{3,2,1,0:T(8,128)(2,1)S(1)}, u32[]{:S(2)}, u32[]{:S(2)}) collective-permute-start(bf16[1,4,256,256]{3,2,1,0:T(8,128)(2,1)} %get-tuple-element.45), channel_id=1, source_target_pairs={{0,6},{2,4},{4,2},{6,0},{8,14},{10,12},{12,10},{14,8},{16,22},{18,... | collective-permute-start | bytes 1572872 | tf_op jit(solution)/shard_map/ppermute | solution.py:358
  22.2 22.5 %copy-start.4 = (bf16[1,4,256,256]{3,2,1,0:T(8,128)(2,1)}, bf16[1,4,256,256]{3,2,1,0:T(8,128)(2,1)S(1)}, u32[]{:S(2)}) copy-start(bf16[1,4,256,256]{3,2,1,0:T(8,128)(2,1)S(1)} %collective-permute-done.2.refs_2_) | copy-start | bytes 1572868
  22.2 38.3 %copy-start.2 = (bf16[2,4,256,256]{3,2,1,0:T(8,128)(2,1)}, bf16[2,4,256,256]{3,2,1,0:T(8,128)(2,1)S(1)}, u32[]{:S(2)}) copy-start(bf16[2,4,256,256]{3,2,1,0:T(8,128)(2,1)S(1)} %collective-permute-done.refs_1_) | copy-start | bytes 3145732
  22.2 14.5 %collective-permute-start.8 = (bf16[1,4,256,256]{3,2,1,0:T(8,128)(2,1)S(1)}, bf16[1,4,256,256]{3,2,1,0:T(8,128)(2,1)S(1)}, u32[]{:S(2)}, u32[]{:S(2)}) collective-permute-start(bf16[1,4,256,256]{3,2,1,0:T(8,128)(2,1)S(1)} %collective-permute-done.2.refs_2_), channel_id=1, source_target_pairs={{0,8},{2,10},{8,16},{10,18},{12,4},{14,6},{16,24},{18,26},{20,12},... | collective-permute-start | bytes 1572872 | tf_op jit(solution)/shard_map/ppermute | solution.py:358
  26.2 16.2 %collective-permute-start.6 = (bf16[1,4,256,256]{3,2,1,0:T(8,128)(2,1)}, bf16[1,4,256,256]{3,2,1,0:T(8,128)(2,1)S(1)}, u32[]{:S(2)}, u32[]{:S(2)}) collective-permute-start(bf16[1,4,256,256]{3,2,1,0:T(8,128)(2,1)} %get-tuple-element.41), channel_id=1, source_target_pairs={{4,14},{6,12},{8,2},{10,0},{12,22},{14,20},{16,10},{18,8},{20,30},... | collective-permute-start | bytes 1572872 | tf_op jit(solution)/shard_map/ppermute | solution.py:358
  27.5 17.2 %collective-permute-start.1 = (bf16[1,4,256,256]{3,2,1,0:T(8,128)(2,1)}, bf16[1,4,256,256]{3,2,1,0:T(8,128)(2,1)S(1)}, u32[]{:S(2)}, u32[]{:S(2)}) collective-permute-start(bf16[1,4,256,256]{3,2,1,0:T(8,128)(2,1)} %get-tuple-element.34), channel_id=1, source_target_pairs={{0,4},{2,6},{4,0},{6,2},{8,12},{10,14},{12,8},{14,10},{16,20},{18,... | collective-permute-start | bytes 1572872 | tf_op jit(solution)/shard_map/ppermute | solution.py:358
  28.6 21.1 %copy-start.5 = (bf16[1,4,256,256]{3,2,1,0:T(8,128)(2,1)}, bf16[1,4,256,256]{3,2,1,0:T(8,128)(2,1)S(1)}, u32[]{:S(2)}) copy-start(bf16[1,4,256,256]{3,2,1,0:T(8,128)(2,1)S(1)} %collective-permute-done.4.refs_4_) | copy-start | bytes 1572868
  28.6 26.8 %collective-permute-start.3 = (bf16[1,4,256,256]{3,2,1,0:T(8,128)(2,1)}, bf16[1,4,256,256]{3,2,1,0:T(8,128)(2,1)}, u32[]{:S(2)}, u32[]{:S(2)}) collective-permute-start(bf16[1,4,256,256]{3,2,1,0:T(8,128)(2,1)} %get-tuple-element.37), channel_id=1, source_target_pairs={{0,6},{2,4},{4,2},{6,0},{8,14},{10,12},{12,10},{14,8},{16,22},{18,... | collective-permute-start | bytes 1572872 | tf_op jit(solution)/shard_map/ppermute | solution.py:358
  33.0 22.5 %copy-start.6 = (bf16[1,4,256,256]{3,2,1,0:T(8,128)(2,1)}, bf16[1,4,256,256]{3,2,1,0:T(8,128)(2,1)S(1)}, u32[]{:S(2)}) copy-start(bf16[1,4,256,256]{3,2,1,0:T(8,128)(2,1)S(1)} %collective-permute-done.10.refs_3_) | copy-start | bytes 1572868
  36.7 18.8 %copy-start.7 = (bf16[1,4,256,256]{3,2,1,0:T(8,128)(2,1)}, bf16[1,4,256,256]{3,2,1,0:T(8,128)(2,1)S(1)}, u32[]{:S(2)}) copy-start(bf16[1,4,256,256]{3,2,1,0:T(8,128)(2,1)S(1)} %collective-permute-done.8.refs_6_) | copy-start | bytes 1572868
  36.7 18.8 %collective-permute-start.11 = (bf16[1,4,256,256]{3,2,1,0:T(8,128)(2,1)S(1)}, bf16[1,4,256,256]{3,2,1,0:T(8,128)(2,1)S(1)}, u32[]{:S(2)}, u32[]{:S(2)}) collective-permute-start(bf16[1,4,256,256]{3,2,1,0:T(8,128)(2,1)S(1)} %collective-permute-done.10.refs_3_), channel_id=1, source_target_pairs={{0,8},{2,10},{8,16},{10,18},{12,4},{14,6},{16,24},{18,26},{20,12},... | collective-permute-start | bytes 1572872 | tf_op jit(solution)/shard_map/ppermute | solution.py:358
  41.1 31.2 %collective-permute-start.5 = (bf16[1,4,256,256]{3,2,1,0:T(8,128)(2,1)}, bf16[1,4,256,256]{3,2,1,0:T(8,128)(2,1)}, u32[]{:S(2)}, u32[]{:S(2)}) collective-permute-start(bf16[1,4,256,256]{3,2,1,0:T(8,128)(2,1)} %get-tuple-element.39.refs_0_), channel_id=1, source_target_pairs={{4,12},{6,14},{8,0},{10,2},{12,20},{14,22},{16,8},{18,10},{20,28},... | collective-permute-start | bytes 1572872 | tf_op jit(solution)/shard_map/ppermute | solution.py:358
  42.4 29.9 %collective-permute-start.7 = (bf16[1,4,256,256]{3,2,1,0:T(8,128)(2,1)}, bf16[1,4,256,256]{3,2,1,0:T(8,128)(2,1)}, u32[]{:S(2)}, u32[]{:S(2)}) collective-permute-start(bf16[1,4,256,256]{3,2,1,0:T(8,128)(2,1)} %get-tuple-element.42), channel_id=1, source_target_pairs={{4,14},{6,12},{8,2},{10,0},{12,22},{14,20},{16,10},{18,8},{20,30},... | collective-permute-start | bytes 1572872 | tf_op jit(solution)/shard_map/ppermute | solution.py:358
  44.6 28.6 %copy-start.3 = (bf16[1,4,256,256]{3,2,1,0:T(8,128)(2,1)}, bf16[1,4,256,256]{3,2,1,0:T(8,128)(2,1)S(1)}, u32[]{:S(2)}) copy-start(bf16[1,4,256,256]{3,2,1,0:T(8,128)(2,1)S(1)} %collective-permute-done.1.refs_2_) | copy-start | bytes 1572868
  44.6 27.7 %collective-permute-start.9 = (bf16[1,4,256,256]{3,2,1,0:T(8,128)(2,1)S(1)}, bf16[1,4,256,256]{3,2,1,0:T(8,128)(2,1)}, u32[]{:S(2)}, u32[]{:S(2)}) collective-permute-start(bf16[1,4,256,256]{3,2,1,0:T(8,128)(2,1)S(1)} %collective-permute-done.1.refs_2_), channel_id=1, source_target_pairs={{0,8},{2,10},{8,16},{10,18},{12,4},{14,6},{16,24},{18,26},{20,12},... | collective-permute-start | bytes 1572872 | tf_op jit(solution)/shard_map/ppermute | solution.py:358
  55.5 17.8 %collective-permute-start.12 = (bf16[1,4,256,256]{3,2,1,0:T(8,128)(2,1)}, bf16[1,4,256,256]{3,2,1,0:T(8,128)(2,1)}, u32[]{:S(2)}, u32[]{:S(2)}) collective-permute-start(bf16[1,4,256,256]{3,2,1,0:T(8,128)(2,1)} %collective-permute-done.3.refs_3_), channel_id=1, source_target_pairs={{0,8},{2,10},{8,16},{10,18},{12,4},{14,6},{16,24},{18,26},{20,12},... | collective-permute-start | bytes 1572872 | tf_op jit(solution)/shard_map/ppermute | solution.py:358
  85.3 2.7 %collective-permute-start.13 = (bf16[2,4,208,256]{3,2,1,0:T(8,128)(2,1)}, bf16[2,4,208,256]{3,2,1,0:T(8,128)(2,1)S(1)}, u32[]{:S(2)}, u32[]{:S(2)}) collective-permute-start(bf16[2,4,208,256]{3,2,1,0:T(8,128)(2,1)} %get-tuple-element.52), channel_id=1, source_target_pairs={{0,2},{2,0},{4,6},{6,4},{8,10},{10,8},{12,14},{14,12},{16,18},{18,... | collective-permute-start | bytes 2555912 | tf_op jit(solution)/shard_map/ppermute | solution.py:358
  90.3 8.2 %collective-permute-start.14 = (bf16[4,208,128]{2,1,0:T(8,128)(2,1)S(1)}, bf16[4,208,128]{2,1,0:T(8,128)(2,1)S(1)}, u32[]{:S(2)}, u32[]{:S(2)}) collective-permute-start(bf16[4,208,128]{2,1,0:T(8,128)(2,1)S(1)} %get-tuple-element.54), channel_id=1, source_target_pairs={{0,1},{1,0},{2,3},{3,2},{4,5},{5,4},{6,7},{7,6},{8,9},{9,8},{10,11... | collective-permute-start | bytes 638984 | tf_op jit(solution)/shard_map/ppermute | solution.py:402
  91.8 11.3 %collective-permute-start.15 = (bf16[4,208,128]{2,1,0:T(8,128)(2,1)S(1)}, bf16[4,208,128]{2,1,0:T(8,128)(2,1)S(1)}, u32[]{:S(2)}, u32[]{:S(2)}) collective-permute-start(bf16[4,208,128]{2,1,0:T(8,128)(2,1)S(1)} %get-tuple-element.55), channel_id=1, source_target_pairs={{0,4},{1,5},{2,6},{3,7},{4,0},{5,1},{6,2},{7,3},{8,12},{9,13},{10,... | collective-permute-start | bytes 638984 | tf_op jit(solution)/shard_map/ppermute | solution.py:402
  93.9 10.0 %collective-permute-start.16 = (bf16[4,208,128]{2,1,0:T(8,128)(2,1)S(1)}, bf16[4,208,128]{2,1,0:T(8,128)(2,1)S(1)}, u32[]{:S(2)}, u32[]{:S(2)}) collective-permute-start(bf16[4,208,128]{2,1,0:T(8,128)(2,1)S(1)} %get-tuple-element.56), channel_id=1, source_target_pairs={{0,5},{1,4},{2,7},{3,6},{4,1},{5,0},{6,3},{7,2},{8,13},{9,12},{10,... | collective-permute-start | bytes 638984 | tf_op jit(solution)/shard_map/ppermute | solution.py:402
  104.0 6.2 %collective-permute-start.17 = (bf16[2,208,128]{2,1,0:T(8,128)(2,1)S(1)}, bf16[2,208,128]{2,1,0:T(8,128)(2,1)S(1)}, u32[]{:S(2)}, u32[]{:S(2)}) collective-permute-start(bf16[2,208,128]{2,1,0:T(8,128)(2,1)S(1)} %get-tuple-element.58), channel_id=1, source_target_pairs={{0,8},{2,10},{8,16},{10,18},{16,24},{18,26},{1,9},{3,11},{9,17},{1... | collective-permute-start | bytes 319496 | tf_op jit(solution)/shard_map/ppermute | solution.py:358
  (4 other events, 37.7 us)

commit v6 on v5

--- a/solution.py
+++ b/solution.py
@@ -101,7 +101,7 @@
 
 def whiten(spectra, valid, items):
     _, channels, windows, _ = spectra.shape
-    tile = min(32, channels)
+    tile = min(64, channels)
     count = len(pieces_of(items))
     anywhere = pl.BlockSpec(memory_space=pl.ANY)
     return pl.pallas_call(

time: 112 us -> 112 us (level)
  no operation moved by 1% of the time
where the time goes in v6:
time: 112 us
  waiting for transfers between devices  38.7 us (35%)
  starting transfers between devices  38.3 us (34%)
  Pallas kernels  32.9 us (29%)
  local copies, waits for them, and re-layouts  1.19 us (1%)
    ppermute x15, starting transfers between devices, move(): return lax.ppermute(value, 'blk', pairs)  34.7 us
    ppermute x15, waiting for transfers between devices, move(): return lax.ppermute(value, 'blk', pairs)  28.6 us
    pallas_call x2, Pallas kernels, correlate(): pl.pallas_call(functools.partial(correlate_kernel, pairs, places, part),...  23.9 us
    ppermute x3, waiting for transfers between devices, both(): return lax.ppermute(value, ('blk', 'frq'), pairs)  10 us
    pallas_call x1, Pallas kernels, whiten(): pl.pallas_call(functools.partial(whiten_kernel, items, tile), in_specs=[p...  6.19 us
    ppermute x3, starting transfers between devices, both(): return lax.ppermute(value, ('blk', 'frq'), pairs)  3.63 us
  transfers between devices with their start and end apart: 18, of which 11 were waited for; matrix products, arithmetic and copies ran while one was open for 1% of the time, Pallas kernels for 11%

profile of v6, /device:TPU:0, one launch (start us, length us, event | category | flops | bytes accessed | tf_op | source)
XLA Modules:
  0.0 111.8 jit_solution(14444304362590839728)
XLA Ops:
  0.0 6.2 %whiten.1 = (bf16[1,4,256,256]{3,2,1,0:T(8,128)(2,1)}, bf16[1,4,256,256]{3,2,1,0:T(8,128)(2,1)}, bf16[1,4,256,256]{3,2,1,0:T(8,128)(2,1)}, bf16[1,4,256,256]{3,2...) custom-call(s32[1,256]{1,0:T(1,128)} %bitcast.6, ...), custom_call_target="tpu_custom_call" | custom-call | bytes 1000 | tf_op jit(solution)/shard_map/whiten/pallas_call | solution.py:107
  6.7 2.6 %collective-permute-start.2 = (bf16[1,4,256,256]{3,2,1,0:T(8,128)(2,1)}, bf16[1,4,256,256]{3,2,1,0:T(8,128)(2,1)S(1)}, u32[]{:S(2)}, u32[]{:S(2)}) collective-permute-start(bf16[1,4,256,256]{3,2,1,0:T(8,128)(2,1)} %get-tuple-element.36), channel_id=1, source_target_pairs={{0,4},{2,6},{4,0},{6,2},{8,12},{10,14},{12,8},{14,10},{16,20},{18,... | collective-permute-start | bytes 1572872 | tf_op jit(solution)/shard_map/ppermute | solution.py:358
  10.6 2.3 %collective-permute-start.10 = (bf16[1,4,256,256]{3,2,1,0:T(8,128)(2,1)}, bf16[1,4,256,256]{3,2,1,0:T(8,128)(2,1)S(1)}, u32[]{:S(2)}, u32[]{:S(2)}) collective-permute-start(bf16[1,4,256,256]{3,2,1,0:T(8,128)(2,1)} %get-tuple-element.45), channel_id=1, source_target_pairs={{0,6},{2,4},{4,2},{6,0},{8,14},{10,12},{12,10},{14,8},{16,22},{18,... | collective-permute-start | bytes 1572872 | tf_op jit(solution)/shard_map/ppermute | solution.py:358
  12.9 9.4 %collective-permute-done.2.refs_2_ = bf16[1,4,256,256]{3,2,1,0:T(8,128)(2,1)S(1)} collective-permute-done((bf16[1,4,256,256]{3,2,1,0:T(8,128)(2,1)}, bf16[1,4,256,256]{3,2,1,0:T(8,128)(2,1)S(1)}, u32[]{:S(2)}, u32[]{:S(2)}) %collective-permute-start.2) | collective-permute-done | bytes 524320 | tf_op jit(solution)/shard_map/ppermute | solution.py:358
  22.3 4.0 %collective-permute-start.8 = (bf16[1,4,256,256]{3,2,1,0:T(8,128)(2,1)S(1)}, bf16[1,4,256,256]{3,2,1,0:T(8,128)(2,1)S(1)}, u32[]{:S(2)}, u32[]{:S(2)}) collective-permute-start(bf16[1,4,256,256]{3,2,1,0:T(8,128)(2,1)S(1)} %collective-permute-done.2.refs_2_), channel_id=1, source_target_pairs={{0,8},{2,10},{8,16},{10,18},{12,4},{14,6},{16,24},{18,26},{20,12},... | collective-permute-start | bytes 1572872 | tf_op jit(solution)/shard_map/ppermute | solution.py:358
  26.2 1.3 %collective-permute-start.6 = (bf16[1,4,256,256]{3,2,1,0:T(8,128)(2,1)}, bf16[1,4,256,256]{3,2,1,0:T(8,128)(2,1)S(1)}, u32[]{:S(2)}, u32[]{:S(2)}) collective-permute-start(bf16[1,4,256,256]{3,2,1,0:T(8,128)(2,1)} %get-tuple-element.41), channel_id=1, source_target_pairs={{4,14},{6,12},{8,2},{10,0},{12,22},{14,20},{16,10},{18,8},{20,30},... | collective-permute-start | bytes 1572872 | tf_op jit(solution)/shard_map/ppermute | solution.py:358
  30.0 3.1 %collective-permute-done.10.refs_3_ = bf16[1,4,256,256]{3,2,1,0:T(8,128)(2,1)S(1)} collective-permute-done((bf16[1,4,256,256]{3,2,1,0:T(8,128)(2,1)}, bf16[1,4,256,256]{3,2,1,0:T(8,128)(2,1)S(1)}, u32[]{:S(2)}, u32[]{:S(2)}) %collective-permute-start.10) | collective-permute-done | bytes 524320 | tf_op jit(solution)/shard_map/ppermute | solution.py:358
  33.1 3.7 %collective-permute-done.8.refs_6_ = bf16[1,4,256,256]{3,2,1,0:T(8,128)(2,1)S(1)} collective-permute-done((bf16[1,4,256,256]{3,2,1,0:T(8,128)(2,1)S(1)}, bf16[1,4,256,256]{3,2,1,0:T(8,128)(2,1)S(1)}, u32[]{:S(2)}, u32[]{:S(2)}) %collective-permute-start.8) | collective-permute-done | bytes 524320 | tf_op jit(solution)/shard_map/ppermute | solution.py:358
  36.8 4.4 %collective-permute-start.11 = (bf16[1,4,256,256]{3,2,1,0:T(8,128)(2,1)S(1)}, bf16[1,4,256,256]{3,2,1,0:T(8,128)(2,1)S(1)}, u32[]{:S(2)}, u32[]{:S(2)}) collective-permute-start(bf16[1,4,256,256]{3,2,1,0:T(8,128)(2,1)S(1)} %collective-permute-done.10.refs_3_), channel_id=1, source_target_pairs={{0,8},{2,10},{8,16},{10,18},{12,4},{14,6},{16,24},{18,26},{20,12},... | collective-permute-start | bytes 1572872 | tf_op jit(solution)/shard_map/ppermute | solution.py:358
  41.2 1.3 %collective-permute-start.5 = (bf16[1,4,256,256]{3,2,1,0:T(8,128)(2,1)}, bf16[1,4,256,256]{3,2,1,0:T(8,128)(2,1)}, u32[]{:S(2)}, u32[]{:S(2)}) collective-permute-start(bf16[1,4,256,256]{3,2,1,0:T(8,128)(2,1)} %get-tuple-element.39.refs_0_), channel_id=1, source_target_pairs={{4,12},{6,14},{8,0},{10,2},{12,20},{14,22},{16,8},{18,10},{20,28},... | collective-permute-start | bytes 1572872 | tf_op jit(solution)/shard_map/ppermute | solution.py:358
  42.5 1.3 %collective-permute-start.7 = (bf16[1,4,256,256]{3,2,1,0:T(8,128)(2,1)}, bf16[1,4,256,256]{3,2,1,0:T(8,128)(2,1)}, u32[]{:S(2)}, u32[]{:S(2)}) collective-permute-start(bf16[1,4,256,256]{3,2,1,0:T(8,128)(2,1)} %get-tuple-element.42), channel_id=1, source_target_pairs={{4,14},{6,12},{8,2},{10,0},{12,22},{14,20},{16,10},{18,8},{20,30},... | collective-permute-start | bytes 1572872 | tf_op jit(solution)/shard_map/ppermute | solution.py:358
  44.8 5.1 %collective-permute-start.9 = (bf16[1,4,256,256]{3,2,1,0:T(8,128)(2,1)S(1)}, bf16[1,4,256,256]{3,2,1,0:T(8,128)(2,1)}, u32[]{:S(2)}, u32[]{:S(2)}) collective-permute-start(bf16[1,4,256,256]{3,2,1,0:T(8,128)(2,1)S(1)} %collective-permute-done.1.refs_2_), channel_id=1, source_target_pairs={{0,8},{2,10},{8,16},{10,18},{12,4},{14,6},{16,24},{18,26},{20,12},... | collective-permute-start | bytes 1572872 | tf_op jit(solution)/shard_map/ppermute | solution.py:358
  49.8 5.8 %collective-permute-done.3.refs_3_ = bf16[1,4,256,256]{3,2,1,0:T(8,128)(2,1)} collective-permute-done((bf16[1,4,256,256]{3,2,1,0:T(8,128)(2,1)}, bf16[1,4,256,256]{3,2,1,0:T(8,128)(2,1)}, u32[]{:S(2)}, u32[]{:S(2)}) %collective-permute-start.3) | collective-permute-done | bytes 524320 | tf_op jit(solution)/shard_map/ppermute | solution.py:358
  55.6 4.4 %collective-permute-start.12 = (bf16[1,4,256,256]{3,2,1,0:T(8,128)(2,1)}, bf16[1,4,256,256]{3,2,1,0:T(8,128)(2,1)}, u32[]{:S(2)}, u32[]{:S(2)}) collective-permute-start(bf16[1,4,256,256]{3,2,1,0:T(8,128)(2,1)} %collective-permute-done.3.refs_3_), channel_id=1, source_target_pairs={{0,8},{2,10},{8,16},{10,18},{12,4},{14,6},{16,24},{18,26},{20,12},... | collective-permute-start | bytes 1572872 | tf_op jit(solution)/shard_map/ppermute | solution.py:358
  60.5 11.9 %correlate.2 = (bf16[2,4,208,256]{3,2,1,0:T(8,128)(2,1)}, bf16[2,4,208,256]{3,2,1,0:T(8,128)(2,1)}) custom-call(s32[2]{0:T(128)} %pad_add_fusion.pos_ref, bf16[1,4,256,256]{3,2,1,0:T(8,128)(2,1)} %get-tuple-element.38.refs_0_, bf16[2,4,256,256]{3,2,1,0:T(8,128)(2,1)} %copy-done.2, bf16[1,4,256,256]{3,2,1,0:T(8,128)(2,1)} %copy-done.4, ...), custom_call_target="tpu_custom_call" | custom-call | bytes 1000 | tf_op jit(solution)/shard_map/correlate/pallas_call | solution.py:230
  73.3 12.0 %correlate.3 = (bf16[2,4,208,256]{3,2,1,0:T(8,128)(2,1)}, bf16[2,4,208,256]{3,2,1,0:T(8,128)(2,1)}) custom-call(s32[2]{0:T(128)} %pad_add_fusion.pos_ref, bf16[1,4,256,256]{3,2,1,0:T(8,128)(2,1)} %get-tuple-element.39.refs_0_, bf16[2,4,256,256]{3,2,1,0:T(8,128)(2,1)} %copy-done.2, bf16[1,4,256,256]{3,2,1,0:T(8,128)(2,1)} %copy-done.3, ...), custom_call_target="tpu_custom_call" | custom-call | bytes 1000 | tf_op jit(solution)/shard_map/correlate/pallas_call | solution.py:230
  85.5 2.6 %collective-permute-done.13.refs_4_.refs_5_.refs_6_.refs_7_ = bf16[2,4,208,256]{3,2,1,0:T(8,128)(2,1)S(1)} collective-permute-done((bf16[2,4,208,256]{3,2,1,0:T(8,128)(2,1)}, bf16[2,4,208,256]{3,2,1,0:T(8,128)(2,1)S(1)}, u32[]{:S(2)}, u32[]{:S(2)}) %collective-permute-start.13) | collective-permute-done | bytes 852000 | tf_op jit(solution)/shard_map/ppermute | solution.py:358
  90.4 1.6 %collective-permute-start.14 = (bf16[4,208,128]{2,1,0:T(8,128)(2,1)S(1)}, bf16[4,208,128]{2,1,0:T(8,128)(2,1)S(1)}, u32[]{:S(2)}, u32[]{:S(2)}) collective-permute-start(bf16[4,208,128]{2,1,0:T(8,128)(2,1)S(1)} %get-tuple-element.54), channel_id=1, source_target_pairs={{0,1},{1,0},{2,3},{3,2},{4,5},{5,4},{6,7},{7,6},{8,9},{9,8},{10,11... | collective-permute-start | bytes 638984 | tf_op jit(solution)/shard_map/ppermute | solution.py:402
  91.9 2.1 %collective-permute-start.15 = (bf16[4,208,128]{2,1,0:T(8,128)(2,1)S(1)}, bf16[4,208,128]{2,1,0:T(8,128)(2,1)S(1)}, u32[]{:S(2)}, u32[]{:S(2)}) collective-permute-start(bf16[4,208,128]{2,1,0:T(8,128)(2,1)S(1)} %get-tuple-element.55), channel_id=1, source_target_pairs={{0,4},{1,5},{2,6},{3,7},{4,0},{5,1},{6,2},{7,3},{8,12},{9,13},{10,... | collective-permute-start | bytes 638984 | tf_op jit(solution)/shard_map/ppermute | solution.py:402
  94.0 4.5 %collective-permute-done.14.refs_1_ = bf16[4,208,128]{2,1,0:T(8,128)(2,1)S(1)} collective-permute-done((bf16[4,208,128]{2,1,0:T(8,128)(2,1)S(1)}, bf16[4,208,128]{2,1,0:T(8,128)(2,1)S(1)}, u32[]{:S(2)}, u32[]{:S(2)}) %collective-permute-start.14) | collective-permute-done | bytes 213024 | tf_op jit(solution)/shard_map/ppermute | solution.py:402
  98.5 4.8 %collective-permute-done.15.refs_2_ = bf16[4,208,128]{2,1,0:T(8,128)(2,1)S(1)} collective-permute-done((bf16[4,208,128]{2,1,0:T(8,128)(2,1)S(1)}, bf16[4,208,128]{2,1,0:T(8,128)(2,1)S(1)}, u32[]{:S(2)}, u32[]{:S(2)}) %collective-permute-start.15) | collective-permute-done | bytes 213024 | tf_op jit(solution)/shard_map/ppermute | solution.py:402
  104.1 3.9 %collective-permute-start.17 = (bf16[2,208,128]{2,1,0:T(8,128)(2,1)S(1)}, bf16[2,208,128]{2,1,0:T(8,128)(2,1)S(1)}, u32[]{:S(2)}, u32[]{:S(2)}) collective-permute-start(bf16[2,208,128]{2,1,0:T(8,128)(2,1)S(1)} %get-tuple-element.58), channel_id=1, source_target_pairs={{0,8},{2,10},{8,16},{10,18},{16,24},{18,26},{1,9},{3,11},{9,17},{1... | collective-permute-start | bytes 319496 | tf_op jit(solution)/shard_map/ppermute | solution.py:358
  108.0 2.3 %collective-permute-done.17.behind_ref = bf16[2,208,128]{2,1,0:T(8,128)(2,1)S(1)} collective-permute-done((bf16[2,208,128]{2,1,0:T(8,128)(2,1)S(1)}, bf16[2,208,128]{2,1,0:T(8,128)(2,1)S(1)}, u32[]{:S(2)}, u32[]{:S(2)}) %collective-permute-start.17) | collective-permute-done | bytes 106528 | tf_op jit(solution)/shard_map/ppermute | solution.py:358
  110.3 1.5 %finish.1 = f32[201,4,128]{2,1,0:T(4,128)} custom-call(s32[2]{0:T(128)S(1)} %copy-done.1, f32[4,208,128]{2,1,0:T(8,128)S(1)} %get-tuple-element.57.own_ref, bf16[2,208,128]{2,1,0:T(8,128)(2,1)S(1)} %collective-permute-done.17.behind_ref), custom_call_target="tpu_custom_call" | custom-call | tf_op jit(solution)/shard_map/finish/pallas_call | solution.py:311
  (39 shorter events, 10.0 us)
Async XLA Ops:
  6.2 16.1 %collective-permute-start = (bf16[2,4,256,256]{3,2,1,0:T(8,128)(2,1)}, bf16[2,4,256,256]{3,2,1,0:T(8,128)(2,1)S(1)}, u32[]{:S(2)}, u32[]{:S(2)}) collective-permute-start(bf16[2,4,256,256]{3,2,1,0:T(8,128)(2,1)} %get-tuple-element.33), channel_id=1, source_target_pairs={{0,2},{2,0},{4,6},{6,4},{8,10},{10,8},{12,14},{14,12},{16,18},{18,... | collective-permute-start | bytes 3145736 | tf_op jit(solution)/shard_map/ppermute | solution.py:358
  6.7 15.6 %collective-permute-start.2 = (bf16[1,4,256,256]{3,2,1,0:T(8,128)(2,1)}, bf16[1,4,256,256]{3,2,1,0:T(8,128)(2,1)S(1)}, u32[]{:S(2)}, u32[]{:S(2)}) collective-permute-start(bf16[1,4,256,256]{3,2,1,0:T(8,128)(2,1)} %get-tuple-element.36), channel_id=1, source_target_pairs={{0,4},{2,6},{4,0},{6,2},{8,12},{10,14},{12,8},{14,10},{16,20},{18,... | collective-permute-start | bytes 1572872 | tf_op jit(solution)/shard_map/ppermute | solution.py:358
  9.3 19.4 %collective-permute-start.4 = (bf16[1,4,256,256]{3,2,1,0:T(8,128)(2,1)}, bf16[1,4,256,256]{3,2,1,0:T(8,128)(2,1)S(1)}, u32[]{:S(2)}, u32[]{:S(2)}) collective-permute-start(bf16[1,4,256,256]{3,2,1,0:T(8,128)(2,1)} %get-tuple-element.38.refs_0_), channel_id=1, source_target_pairs={{4,12},{6,14},{8,0},{10,2},{12,20},{14,22},{16,8},{18,10},{20,28},... | collective-permute-start | bytes 1572872 | tf_op jit(solution)/shard_map/ppermute | solution.py:358
  10.6 22.5 %collective-permute-start.10 = (bf16[1,4,256,256]{3,2,1,0:T(8,128)(2,1)}, bf16[1,4,256,256]{3,2,1,0:T(8,128)(2,1)S(1)}, u32[]{:S(2)}, u32[]{:S(2)}) collective-permute-start(bf16[1,4,256,256]{3,2,1,0:T(8,128)(2,1)} %get-tuple-element.45), channel_id=1, source_target_pairs={{0,6},{2,4},{4,2},{6,0},{8,14},{10,12},{12,10},{14,8},{16,22},{18,... | collective-permute-start | bytes 1572872 | tf_op jit(solution)/shard_map/ppermute | solution.py:358
  22.3 22.5 %copy-start.4 = (bf16[1,4,256,256]{3,2,1,0:T(8,128)(2,1)}, bf16[1,4,256,256]{3,2,1,0:T(8,128)(2,1)S(1)}, u32[]{:S(2)}) copy-start(bf16[1,4,256,256]{3,2,1,0:T(8,128)(2,1)S(1)} %collective-permute-done.2.refs_2_) | copy-start | bytes 1572868
  22.3 38.3 %copy-start.2 = (bf16[2,4,256,256]{3,2,1,0:T(8,128)(2,1)}, bf16[2,4,256,256]{3,2,1,0:T(8,128)(2,1)S(1)}, u32[]{:S(2)}) copy-start(bf16[2,4,256,256]{3,2,1,0:T(8,128)(2,1)S(1)} %collective-permute-done.refs_1_) | copy-start | bytes 3145732
  22.3 14.5 %collective-permute-start.8 = (bf16[1,4,256,256]{3,2,1,0:T(8,128)(2,1)S(1)}, bf16[1,4,256,256]{3,2,1,0:T(8,128)(2,1)S(1)}, u32[]{:S(2)}, u32[]{:S(2)}) collective-permute-start(bf16[1,4,256,256]{3,2,1,0:T(8,128)(2,1)S(1)} %collective-permute-done.2.refs_2_), channel_id=1, source_target_pairs={{0,8},{2,10},{8,16},{10,18},{12,4},{14,6},{16,24},{18,26},{20,12},... | collective-permute-start | bytes 1572872 | tf_op jit(solution)/shard_map/ppermute | solution.py:358
  26.2 16.2 %collective-permute-start.6 = (bf16[1,4,256,256]{3,2,1,0:T(8,128)(2,1)}, bf16[1,4,256,256]{3,2,1,0:T(8,128)(2,1)S(1)}, u32[]{:S(2)}, u32[]{:S(2)}) collective-permute-start(bf16[1,4,256,256]{3,2,1,0:T(8,128)(2,1)} %get-tuple-element.41), channel_id=1, source_target_pairs={{4,14},{6,12},{8,2},{10,0},{12,22},{14,20},{16,10},{18,8},{20,30},... | collective-permute-start | bytes 1572872 | tf_op jit(solution)/shard_map/ppermute | solution.py:358
  27.5 17.2 %collective-permute-start.1 = (bf16[1,4,256,256]{3,2,1,0:T(8,128)(2,1)}, bf16[1,4,256,256]{3,2,1,0:T(8,128)(2,1)S(1)}, u32[]{:S(2)}, u32[]{:S(2)}) collective-permute-start(bf16[1,4,256,256]{3,2,1,0:T(8,128)(2,1)} %get-tuple-element.34), channel_id=1, source_target_pairs={{0,4},{2,6},{4,0},{6,2},{8,12},{10,14},{12,8},{14,10},{16,20},{18,... | collective-permute-start | bytes 1572872 | tf_op jit(solution)/shard_map/ppermute | solution.py:358
  28.7 21.1 %copy-start.5 = (bf16[1,4,256,256]{3,2,1,0:T(8,128)(2,1)}, bf16[1,4,256,256]{3,2,1,0:T(8,128)(2,1)S(1)}, u32[]{:S(2)}) copy-start(bf16[1,4,256,256]{3,2,1,0:T(8,128)(2,1)S(1)} %collective-permute-done.4.refs_4_) | copy-start | bytes 1572868
  28.7 26.8 %collective-permute-start.3 = (bf16[1,4,256,256]{3,2,1,0:T(8,128)(2,1)}, bf16[1,4,256,256]{3,2,1,0:T(8,128)(2,1)}, u32[]{:S(2)}, u32[]{:S(2)}) collective-permute-start(bf16[1,4,256,256]{3,2,1,0:T(8,128)(2,1)} %get-tuple-element.37), channel_id=1, source_target_pairs={{0,6},{2,4},{4,2},{6,0},{8,14},{10,12},{12,10},{14,8},{16,22},{18,... | collective-permute-start | bytes 1572872 | tf_op jit(solution)/shard_map/ppermute | solution.py:358
  33.1 22.5 %copy-start.6 = (bf16[1,4,256,256]{3,2,1,0:T(8,128)(2,1)}, bf16[1,4,256,256]{3,2,1,0:T(8,128)(2,1)S(1)}, u32[]{:S(2)}) copy-start(bf16[1,4,256,256]{3,2,1,0:T(8,128)(2,1)S(1)} %collective-permute-done.10.refs_3_) | copy-start | bytes 1572868
  36.8 18.8 %copy-start.7 = (bf16[1,4,256,256]{3,2,1,0:T(8,128)(2,1)}, bf16[1,4,256,256]{3,2,1,0:T(8,128)(2,1)S(1)}, u32[]{:S(2)}) copy-start(bf16[1,4,256,256]{3,2,1,0:T(8,128)(2,1)S(1)} %collective-permute-done.8.refs_6_) | copy-start | bytes 1572868
  36.8 18.8 %collective-permute-start.11 = (bf16[1,4,256,256]{3,2,1,0:T(8,128)(2,1)S(1)}, bf16[1,4,256,256]{3,2,1,0:T(8,128)(2,1)S(1)}, u32[]{:S(2)}, u32[]{:S(2)}) collective-permute-start(bf16[1,4,256,256]{3,2,1,0:T(8,128)(2,1)S(1)} %collective-permute-done.10.refs_3_), channel_id=1, source_target_pairs={{0,8},{2,10},{8,16},{10,18},{12,4},{14,6},{16,24},{18,26},{20,12},... | collective-permute-start | bytes 1572872 | tf_op jit(solution)/shard_map/ppermute | solution.py:358
  41.2 31.2 %collective-permute-start.5 = (bf16[1,4,256,256]{3,2,1,0:T(8,128)(2,1)}, bf16[1,4,256,256]{3,2,1,0:T(8,128)(2,1)}, u32[]{:S(2)}, u32[]{:S(2)}) collective-permute-start(bf16[1,4,256,256]{3,2,1,0:T(8,128)(2,1)} %get-tuple-element.39.refs_0_), channel_id=1, source_target_pairs={{4,12},{6,14},{8,0},{10,2},{12,20},{14,22},{16,8},{18,10},{20,28},... | collective-permute-start | bytes 1572872 | tf_op jit(solution)/shard_map/ppermute | solution.py:358
  42.5 29.9 %collective-permute-start.7 = (bf16[1,4,256,256]{3,2,1,0:T(8,128)(2,1)}, bf16[1,4,256,256]{3,2,1,0:T(8,128)(2,1)}, u32[]{:S(2)}, u32[]{:S(2)}) collective-permute-start(bf16[1,4,256,256]{3,2,1,0:T(8,128)(2,1)} %get-tuple-element.42), channel_id=1, source_target_pairs={{4,14},{6,12},{8,2},{10,0},{12,22},{14,20},{16,10},{18,8},{20,30},... | collective-permute-start | bytes 1572872 | tf_op jit(solution)/shard_map/ppermute | solution.py:358
  44.8 28.6 %copy-start.3 = (bf16[1,4,256,256]{3,2,1,0:T(8,128)(2,1)}, bf16[1,4,256,256]{3,2,1,0:T(8,128)(2,1)S(1)}, u32[]{:S(2)}) copy-start(bf16[1,4,256,256]{3,2,1,0:T(8,128)(2,1)S(1)} %collective-permute-done.1.refs_2_) | copy-start | bytes 1572868
  44.8 27.7 %collective-permute-start.9 = (bf16[1,4,256,256]{3,2,1,0:T(8,128)(2,1)S(1)}, bf16[1,4,256,256]{3,2,1,0:T(8,128)(2,1)}, u32[]{:S(2)}, u32[]{:S(2)}) collective-permute-start(bf16[1,4,256,256]{3,2,1,0:T(8,128)(2,1)S(1)} %collective-permute-done.1.refs_2_), channel_id=1, source_target_pairs={{0,8},{2,10},{8,16},{10,18},{12,4},{14,6},{16,24},{18,26},{20,12},... | collective-permute-start | bytes 1572872 | tf_op jit(solution)/shard_map/ppermute | solution.py:358
  55.6 17.7 %collective-permute-start.12 = (bf16[1,4,256,256]{3,2,1,0:T(8,128)(2,1)}, bf16[1,4,256,256]{3,2,1,0:T(8,128)(2,1)}, u32[]{:S(2)}, u32[]{:S(2)}) collective-permute-start(bf16[1,4,256,256]{3,2,1,0:T(8,128)(2,1)} %collective-permute-done.3.refs_3_), channel_id=1, source_target_pairs={{0,8},{2,10},{8,16},{10,18},{12,4},{14,6},{16,24},{18,26},{20,12},... | collective-permute-start | bytes 1572872 | tf_op jit(solution)/shard_map/ppermute | solution.py:358
  85.4 2.7 %collective-permute-start.13 = (bf16[2,4,208,256]{3,2,1,0:T(8,128)(2,1)}, bf16[2,4,208,256]{3,2,1,0:T(8,128)(2,1)S(1)}, u32[]{:S(2)}, u32[]{:S(2)}) collective-permute-start(bf16[2,4,208,256]{3,2,1,0:T(8,128)(2,1)} %get-tuple-element.52), channel_id=1, source_target_pairs={{0,2},{2,0},{4,6},{6,4},{8,10},{10,8},{12,14},{14,12},{16,18},{18,... | collective-permute-start | bytes 2555912 | tf_op jit(solution)/shard_map/ppermute | solution.py:358
  90.4 8.2 %collective-permute-start.14 = (bf16[4,208,128]{2,1,0:T(8,128)(2,1)S(1)}, bf16[4,208,128]{2,1,0:T(8,128)(2,1)S(1)}, u32[]{:S(2)}, u32[]{:S(2)}) collective-permute-start(bf16[4,208,128]{2,1,0:T(8,128)(2,1)S(1)} %get-tuple-element.54), channel_id=1, source_target_pairs={{0,1},{1,0},{2,3},{3,2},{4,5},{5,4},{6,7},{7,6},{8,9},{9,8},{10,11... | collective-permute-start | bytes 638984 | tf_op jit(solution)/shard_map/ppermute | solution.py:402
  91.9 11.4 %collective-permute-start.15 = (bf16[4,208,128]{2,1,0:T(8,128)(2,1)S(1)}, bf16[4,208,128]{2,1,0:T(8,128)(2,1)S(1)}, u32[]{:S(2)}, u32[]{:S(2)}) collective-permute-start(bf16[4,208,128]{2,1,0:T(8,128)(2,1)S(1)} %get-tuple-element.55), channel_id=1, source_target_pairs={{0,4},{1,5},{2,6},{3,7},{4,0},{5,1},{6,2},{7,3},{8,12},{9,13},{10,... | collective-permute-start | bytes 638984 | tf_op jit(solution)/shard_map/ppermute | solution.py:402
  94.0 10.0 %collective-permute-start.16 = (bf16[4,208,128]{2,1,0:T(8,128)(2,1)S(1)}, bf16[4,208,128]{2,1,0:T(8,128)(2,1)S(1)}, u32[]{:S(2)}, u32[]{:S(2)}) collective-permute-start(bf16[4,208,128]{2,1,0:T(8,128)(2,1)S(1)} %get-tuple-element.56), channel_id=1, source_target_pairs={{0,5},{1,4},{2,7},{3,6},{4,1},{5,0},{6,3},{7,2},{8,13},{9,12},{10,... | collective-permute-start | bytes 638984 | tf_op jit(solution)/shard_map/ppermute | solution.py:402
  104.1 6.1 %collective-permute-start.17 = (bf16[2,208,128]{2,1,0:T(8,128)(2,1)S(1)}, bf16[2,208,128]{2,1,0:T(8,128)(2,1)S(1)}, u32[]{:S(2)}, u32[]{:S(2)}) collective-permute-start(bf16[2,208,128]{2,1,0:T(8,128)(2,1)S(1)} %get-tuple-element.58), channel_id=1, source_target_pairs={{0,8},{2,10},{8,16},{10,18},{16,24},{18,26},{1,9},{3,11},{9,17},{1... | collective-permute-start | bytes 319496 | tf_op jit(solution)/shard_map/ppermute | solution.py:358
  (4 other events, 37.7 us)
